TPU v7x, 32 devices: a whole 2x2x4 slice. The times are simulated.
32 devices in a mesh: dp: 4 (over z), ctx: 4 (over x, core), tp: 2 (over y).
Axes of the slice: x: 2, y: 2, z: 4, core: 2. Of those that a mesh axis runs over, the one named last changes fastest.
Arguments:
- hidden_in: bfloat16 [8192, 1024], P(('dp', 'ctx')), may hold values from -6 to 6
- out_grad: bfloat16 [8192, 1024], P(('dp', 'ctx')), may hold values from -6 to 6
- segments: int32 [4, 2048], P('dp', 'ctx'), may hold values from 0 to 3, never falling along the last dimension, each value on 1 to 1024 neighbouring positions
- routes: int32 [8192, 2], P(('dp', 'ctx')), may hold values from 0 to 3, all different within a row
- bucket_table: int32 [4095], replicated, may hold values from 0 to 31
- qkv_weight: bfloat16 [1024, 3, 1024], P(('dp', 'ctx'), None, 'tp'), may hold values from -0.1875 to 0.1875
- out_weight: bfloat16 [1024, 1024], P('tp', ('dp', 'ctx')), may hold values from -4 to 4
- router: bfloat16 [1024, 4], P(('dp', 'ctx')), may hold values from -0.1875 to 0.1875
- norm_gains: bfloat16 [2, 1024], P(None, ('dp', 'ctx')), may hold values from 0.5 to 1.5
- position_bias: float32 [16, 32], P('tp'), may hold values from -6 to 6
- expert_in: bfloat16 [4, 2, 1024, 2816], P('dp', None, 'ctx', 'tp'), may hold values from -0.1875 to 0.1875
- expert_down: bfloat16 [4, 2816, 1024], P('dp', 'tp', 'ctx'), may hold values from -0.875 to 0.875
- qkv_first: float32 [1024, 3, 1024], P(('dp', 'ctx'), None, 'tp'), may hold values from -192 to 192
- qkv_second: float32 [1024, 3, 1024], P(('dp', 'ctx'), None, 'tp'), may hold values from 3907.584 to 15482.88
- out_first: float32 [1024, 1024], P('tp', ('dp', 'ctx')), may hold values from -8 to 8
- out_second: float32 [1024, 1024], P('tp', ('dp', 'ctx')), may hold values from 7.632 to 30.24
- router_first: float32 [1024, 4], P(('dp', 'ctx')), may hold values from -2048 to 2048
- router_second: float32 [1024, 4], P(('dp', 'ctx')), may hold values from 640218.56 to 2536715
- gains_first: float32 [2, 1024], P(None, ('dp', 'ctx')), may hold values from -192 to 192
- gains_second: float32 [2, 1024], P(None, ('dp', 'ctx')), may hold values from 4220.191 to 16721.51
- bias_first: float32 [16, 32], P('tp'), may hold values from -128 to 128
- bias_second: float32 [16, 32], P('tp'), may hold values from 1953.792 to 7741.44
- in_first: float32 [4, 2, 1024, 2816], P('dp', None, 'ctx', 'tp'), may hold values from -32 to 32
- in_second: float32 [4, 2, 1024, 2816], P('dp', None, 'ctx', 'tp'), may hold values from 113.67517 to 450.41104
- down_first: float32 [4, 2816, 1024], P('dp', 'tp', 'ctx'), may hold values from -6 to 6
- down_second: float32 [4, 2816, 1024], P('dp', 'tp', 'ctx'), may hold values from 4.88448 to 19.3536
Outputs:
- output: float32 [8192, 1024], P(('dp', 'ctx'))
- input_grad: float32 [8192, 1024], P(('dp', 'ctx'))
- qkv_grad: float32 [1024, 3, 1024], P(('dp', 'ctx'), None, 'tp')
- qkv_first_new: float32 [1024, 3, 1024], P(('dp', 'ctx'), None, 'tp')
- qkv_second_new: float32 [1024, 3, 1024], P(('dp', 'ctx'), None, 'tp')
- qkv_update: float32 [1024, 3, 1024], P(('dp', 'ctx'), None, 'tp')
- out_grad_weight: float32 [1024, 1024], P('tp', ('dp', 'ctx'))
- out_first_new: float32 [1024, 1024], P('tp', ('dp', 'ctx'))
- out_second_new: float32 [1024, 1024], P('tp', ('dp', 'ctx'))
- out_update: float32 [1024, 1024], P('tp', ('dp', 'ctx'))
- router_grad: float32 [1024, 4], P(('dp', 'ctx'))
- router_first_new: float32 [1024, 4], P(('dp', 'ctx'))
- router_second_new: float32 [1024, 4], P(('dp', 'ctx'))
- router_update: float32 [1024, 4], P(('dp', 'ctx'))
- gains_grad: float32 [2, 1024], P(None, ('dp', 'ctx'))
- gains_first_new: float32 [2, 1024], P(None, ('dp', 'ctx'))
- gains_second_new: float32 [2, 1024], P(None, ('dp', 'ctx'))
- gains_update: float32 [2, 1024], P(None, ('dp', 'ctx'))
- bias_grad: float32 [16, 32], P('tp')
- bias_first_new: float32 [16, 32], P('tp')
- bias_second_new: float32 [16, 32], P('tp')
- bias_update: float32 [16, 32], P('tp')
- in_grad: float32 [4, 2, 1024, 2816], P('dp', None, 'ctx', 'tp')
- in_first_new: float32 [4, 2, 1024, 2816], P('dp', None, 'ctx', 'tp')
- in_second_new: float32 [4, 2, 1024, 2816], P('dp', None, 'ctx', 'tp')
- in_update: float32 [4, 2, 1024, 2816], P('dp', None, 'ctx', 'tp')
- down_grad: float32 [4, 2816, 1024], P('dp', 'tp', 'ctx')
- down_first_new: float32 [4, 2816, 1024], P('dp', 'tp', 'ctx')
- down_second_new: float32 [4, 2816, 1024], P('dp', 'tp', 'ctx')
- down_update: float32 [4, 2816, 1024], P('dp', 'tp', 'ctx')
Inputs may be any that keep to these rules, and one draw needn't show every extreme that they name: `segments`: along each sequence the document number never falls; each document has 1 to 1024 positions, one exactly 1024. `routes`: A token's 2 experts differ; every expert is named by some token.
All inputs are finite; a program needn't handle non-finite values.
Results may differ from a plain program's by a relative error of at most 0.017.
Values may be sent and summed in bfloat16 or wider, within the bound.
A program may use at most 384 MiB of HBM per device.

v0:
```python
import functools

import jax
import jax.numpy as jnp
from jax import lax
from jax.experimental import pallas as pl
from jax.experimental.pallas import tpu as pltpu
from jax.sharding import PartitionSpec as P

D = 1024
HEAD_DIM = 64
BUCKETS = 32

NORM_EPS = 1e-06
NEG_FILL = -1e30
BETA_ONE = 0.9
BETA_TWO = 0.95
FIX_ONE = 1.0 - 0.9**10
FIX_TWO = 1.0 - 0.95**10
ADAM_EPS = 1e-08
WEIGHT_DECAY = 0.1
MAIN_RATE = 0.02
BIAS_RATE = 0.2

F32 = jnp.float32
BF16 = jnp.bfloat16
LANES = 128
BLOCK = 256
VMEM_CAP = 60 * 1024 * 1024
GELU_K = 0.7978845608028654
GELU_C = 0.044715


def rms_scale(values):
    return lax.rsqrt(jnp.mean(values * values, axis=-1, keepdims=True) + NORM_EPS)


def norm_back(values, scale_here, gain_here, gradient):
    weighted = gain_here * gradient
    row_inner = jnp.mean(values * weighted, axis=-1, keepdims=True)
    input_part = scale_here * weighted - values * scale_here**3 * row_inner
    return (input_part, jnp.sum(gradient * values * scale_here, axis=0))


def adamw_step(weight, gradient, first_moment, second_moment, step_rate):
    first_new = BETA_ONE * first_moment + (1.0 - BETA_ONE) * gradient
    second_new = BETA_TWO * second_moment + (1.0 - BETA_TWO) * gradient * gradient
    update = -step_rate * (
        first_new / FIX_ONE / (jnp.sqrt(second_new / FIX_TWO) + ADAM_EPS) + WEIGHT_DECAY * weight
    )
    return (first_new, second_new, update)


def swap(values, axis, bits):
    count = lax.axis_size(axis)
    return lax.ppermute(values, axis, [(i, i ^ bits) for i in range(count)])


def gather_xor(values, axis):
    pieces = {0: values}
    bit = lax.axis_size(axis) >> 1
    while bit:
        for key in list(pieces):
            pieces[key | bit] = swap(pieces[key], axis, bit)
        bit >>= 1
    return [pieces[m] for m in range(len(pieces))]


def scatter_sum(parts, axis):
    live = dict(enumerate(parts))
    bit = 1
    while bit < lax.axis_size(axis):
        left = {}
        for key in live:
            if key & bit == 0:
                moved = swap(live[key | bit].astype(BF16), axis, bit)
                left[key] = live[key].astype(F32) + moved.astype(F32)
        live = left
        bit <<= 1
    return live[0]


def all_sum(values, axis):
    bit = 1
    while bit < lax.axis_size(axis):
        values = values + swap(values, axis, bit)
        bit <<= 1
    return values


def in_order(pieces, place, dim):
    bit = 1
    while bit < len(pieces):
        odd = (place & bit) > 0
        pieces = [jnp.where(odd, pieces[m ^ bit], pieces[m]) for m in range(len(pieces))]
        bit <<= 1
    return jnp.concatenate(pieces, axis=dim)


def assemble_kernel(place_ref, *refs):
    pieces, whole, sems = refs[:-2], refs[-2], refs[-1]
    rows = pieces[0].shape[0]
    copies = []
    for m, piece in enumerate(pieces):
        start = pl.multiple_of((place_ref[0] ^ m) * rows, rows)
        copies.append(pltpu.make_async_copy(piece, whole.at[pl.ds(start, rows)], sems.at[m]))
    for copy in copies:
        copy.start()
    for copy in copies:
        copy.wait()


def assemble(pieces, place):
    count, rows = len(pieces), pieces[0].shape[0]
    return pl.pallas_call(
        assemble_kernel,
        out_shape=jax.ShapeDtypeStruct((count * rows,) + pieces[0].shape[1:], pieces[0].dtype),
        in_specs=[pl.BlockSpec(memory_space=pltpu.SMEM)]
        + [pl.BlockSpec(memory_space=pl.ANY)] * count,
        out_specs=pl.BlockSpec(memory_space=pl.ANY),
        scratch_shapes=[pltpu.SemaphoreType.DMA((count,))],
    )(place.reshape(1), *pieces)


NT = (((1,), (1,)), ((), ()))
NN = (((1,), (0,)), ((), ()))


def mm(left, right, dims=NN):
    return lax.dot_general(left, right, dims, preferred_element_type=F32)


def fold_max(values):
    return jnp.max(values.reshape(values.shape[0] // 8, 8, values.shape[1]), axis=0)


def fold_sum(values):
    return jnp.sum(values.reshape(values.shape[0] // 8, 8, values.shape[1]), axis=0)


def skewed(row):
    width = row.shape[1]
    tall = jnp.broadcast_to(row, (LANES, width))
    return pltpu.roll(tall, width - (LANES - 1), 1, stride=1, stride_axis=0)


def unskew_sum(field):
    half = field.shape[0] // 2
    while half >= 1:
        field = pltpu.roll(field[:half], half, 1) + field[half:]
        half //= 2
    return field


def head_masks(rows):
    lane = lax.broadcasted_iota(jnp.int32, (rows, LANES), 1)
    return [(lane < HEAD_DIM).astype(BF16), (lane >= HEAD_DIM).astype(BF16)]


def score_tile(key_block, query_head, skew_ref, head, first, same):
    scores = mm(key_block, query_head, NT)
    tiles = []
    for s in range(BLOCK // LANES):
        column = pl.multiple_of(first - s * LANES, LANES)
        tiles.append(skew_ref[head, :, pl.ds(column, BLOCK)])
    return jnp.where(same, scores + jnp.concatenate(tiles, axis=0), NEG_FILL)


def attention_kernel(
    active_ref, base_ref, query_ref, key_ref, value_ref, window_ref, doc_row_ref, doc_col_ref,
    out_ref, total_ref, skew_ref, flip_ref, score_ref, most_ref, sum_ref, mix_ref,
):
    tokens, length = query_ref.shape[0], key_ref.shape[0]
    key_blocks = length // BLOCK
    masks = head_masks(BLOCK)
    for h in range(2):
        skew_ref[h] = skewed(window_ref[0, h : h + 1, :])

    @pl.loop(0, key_blocks)
    def _(kb):
        rows = pl.ds(pl.multiple_of(kb * BLOCK, BLOCK), BLOCK)
        flip_ref[:, rows] = value_ref[rows, :].T

    for qb in range(tokens // BLOCK):
        here = slice(qb * BLOCK, (qb + 1) * BLOCK)
        pair = query_ref[here, :] * jnp.asarray(HEAD_DIM**-0.5, BF16)
        query_heads = [pair * mask for mask in masks]
        doc_row = doc_row_ref[0:1, here]
        most_ref[...] = jnp.full_like(most_ref, NEG_FILL)
        sum_ref[...] = jnp.zeros_like(sum_ref)
        mix_ref[...] = jnp.zeros_like(mix_ref)

        @pl.loop(0, key_blocks)
        def _(kb):
            @pl.when(active_ref[qb, kb] > 0)
            def _():
                rows = pl.ds(pl.multiple_of(kb * BLOCK, BLOCK), BLOCK)
                column = doc_col_ref[rows, :]
                same = jnp.concatenate([column] * (BLOCK // LANES), axis=1) == doc_row
                for h in range(2):
                    tile = score_tile(
                        key_ref[rows, :], query_heads[h], skew_ref, h,
                        base_ref[kb] + qb * BLOCK, same,
                    )
                    score_ref[h, rows, :] = tile
                    most_ref[h] = jnp.maximum(most_ref[h], fold_max(tile))

        most = [jnp.max(most_ref[h], axis=0, keepdims=True) for h in range(2)]

        @pl.loop(0, key_blocks)
        def _(kb):
            @pl.when(active_ref[qb, kb] > 0)
            def _():
                rows = pl.ds(pl.multiple_of(kb * BLOCK, BLOCK), BLOCK)
                for h in range(2):
                    weights = jnp.exp(score_ref[h, rows, :] - most[h])
                    sum_ref[h] += fold_sum(weights)
                    mix_ref[h] += mm(
                        flip_ref[h * HEAD_DIM : (h + 1) * HEAD_DIM, rows], weights.astype(BF16)
                    )

        columns = []
        for h in range(2):
            total = jnp.sum(sum_ref[h], axis=0, keepdims=True)
            columns.append(mix_ref[h] / total)
            total_ref[0, h : h + 1, here] = most[h] + jnp.log(total)
        out_ref[here, :] = jnp.concatenate(columns, axis=0).T.astype(BF16)


def attention_back_kernel(
    active_ref, base_ref, query_ref, key_ref, value_ref, grad_ref, total_ref, window_ref,
    doc_row_ref, doc_col_ref,
    query_grad_ref, key_grad_ref, value_grad_ref, offset_ref,
    skew_ref, field_ref, flip_ref, weight_ref, change_ref, inner_ref, mix_ref, key_sum, value_sum,
):
    tokens, length = query_ref.shape[0], key_ref.shape[0]
    key_blocks = length // BLOCK
    masks = head_masks(BLOCK)
    for h in range(2):
        skew_ref[h] = skewed(window_ref[0, h : h + 1, :])
    field_ref[...] = jnp.zeros_like(field_ref)
    key_sum[...] = jnp.zeros_like(key_sum)
    value_sum[...] = jnp.zeros_like(value_sum)

    @pl.loop(0, key_blocks)
    def _(kb):
        rows = pl.ds(pl.multiple_of(kb * BLOCK, BLOCK), BLOCK)
        flip_ref[:, rows] = key_ref[rows, :].T

    for qb in range(tokens // BLOCK):
        here = slice(qb * BLOCK, (qb + 1) * BLOCK)
        pair = query_ref[here, :] * jnp.asarray(HEAD_DIM**-0.5, BF16)
        query_heads = [pair * mask for mask in masks]
        grad_pair = grad_ref[here, :]
        grad_heads = [grad_pair * mask for mask in masks]
        doc_row = doc_row_ref[0:1, here]
        inner_ref[...] = jnp.zeros_like(inner_ref)
        mix_ref[...] = jnp.zeros_like(mix_ref)
        totals = [total_ref[0, h : h + 1, here] for h in range(2)]

        @pl.loop(0, key_blocks)
        def _(kb):
            @pl.when(active_ref[qb, kb] > 0)
            def _():
                rows = pl.ds(pl.multiple_of(kb * BLOCK, BLOCK), BLOCK)
                column = doc_col_ref[rows, :]
                same = jnp.concatenate([column] * (BLOCK // LANES), axis=1) == doc_row
                for h in range(2):
                    tile = score_tile(
                        key_ref[rows, :], query_heads[h], skew_ref, h,
                        base_ref[kb] + qb * BLOCK, same,
                    )
                    weights = jnp.exp(tile - totals[h])
                    change = mm(value_ref[rows, :], grad_heads[h], NT)
                    weight_ref[h, rows, :] = weights
                    change_ref[h, rows, :] = change
                    inner_ref[h] += fold_sum(weights * change)

        inner = [jnp.sum(inner_ref[h], axis=0, keepdims=True) for h in range(2)]

        @pl.loop(0, key_blocks)
        def _(kb):
            @pl.when(active_ref[qb, kb] > 0)
            def _():
                rows = pl.ds(pl.multiple_of(kb * BLOCK, BLOCK), BLOCK)
                key_part = value_part = None
                for h in range(2):
                    weights = weight_ref[h, rows, :]
                    score_grad = weights * (change_ref[h, rows, :] - inner[h])
                    for s in range(BLOCK // LANES):
                        first = pl.multiple_of(base_ref[kb] + qb * BLOCK - s * LANES, LANES)
                        field_ref[h, :, pl.ds(first, BLOCK)] += score_grad[
                            s * LANES : (s + 1) * LANES
                        ]
                    low = score_grad.astype(BF16)
                    key_here = mm(low, query_heads[h])
                    value_here = mm(weights.astype(BF16), grad_heads[h])
                    key_part = key_here if h == 0 else key_part + key_here
                    value_part = value_here if h == 0 else value_part + value_here
                    mix_ref[h] += mm(flip_ref[h * HEAD_DIM : (h + 1) * HEAD_DIM, rows], low)
                key_sum[rows, :] += key_part
                value_sum[rows, :] += value_part

        both = jnp.concatenate([mix_ref[0], mix_ref[1]], axis=0) * HEAD_DIM**-0.5
        query_grad_ref[here, :] = both.T.astype(BF16)

    key_grad_ref[...] = key_sum[...].astype(BF16)
    value_grad_ref[...] = value_sum[...].astype(BF16)
    for h in range(2):
        offset_ref[0, h : h + 1, :] = unskew_sum(field_ref[h])


def attention_specs(tokens, length, pairs, width):
    smem = pl.BlockSpec(memory_space=pltpu.SMEM)
    return dict(
        smem=smem,
        query=pl.BlockSpec((tokens, LANES), lambda i: (0, i)),
        key=pl.BlockSpec((length, LANES), lambda i: (0, i)),
        value=pl.BlockSpec((length, LANES), lambda i: (0, i + pairs)),
        window=pl.BlockSpec((1, 8, width), lambda i: (i, 0, 0)),
        total=pl.BlockSpec((1, 8, tokens), lambda i: (i, 0, 0)),
        doc_row=pl.BlockSpec((8, tokens), lambda i: (0, 0)),
        doc_col=pl.BlockSpec((length, LANES), lambda i: (0, 0)),
    )


def attention(active, base, queries, key_values, window, doc_row, doc_col):
    tokens, length = queries.shape[0], key_values.shape[0]
    pairs, width = window.shape[0], window.shape[2]
    specs = attention_specs(tokens, length, pairs, width)
    return pl.pallas_call(
        attention_kernel,
        grid=(pairs,),
        in_specs=[
            specs["smem"], specs["smem"], specs["query"], specs["key"], specs["value"],
            specs["window"], specs["doc_row"], specs["doc_col"],
        ],
        out_specs=[specs["query"], specs["total"]],
        out_shape=[
            jax.ShapeDtypeStruct(queries.shape, BF16),
            jax.ShapeDtypeStruct((pairs, 8, tokens), F32),
        ],
        scratch_shapes=[
            pltpu.VMEM((2, LANES, width), F32),
            pltpu.VMEM((LANES, length), BF16),
            pltpu.VMEM((2, length, BLOCK), F32),
            pltpu.VMEM((2, 8, BLOCK), F32),
            pltpu.VMEM((2, 8, BLOCK), F32),
            pltpu.VMEM((2, HEAD_DIM, BLOCK), F32),
        ],
        compiler_params=pltpu.CompilerParams(vmem_limit_bytes=VMEM_CAP),
        name="attention_forward",
    )(active, base, queries, key_values, key_values, window, doc_row, doc_col)


def attention_back(active, base, queries, key_values, grads, totals, window, doc_row, doc_col):
    tokens, length = queries.shape[0], key_values.shape[0]
    pairs, width = window.shape[0], window.shape[2]
    specs = attention_specs(tokens, length, pairs, width)
    return pl.pallas_call(
        attention_back_kernel,
        grid=(pairs,),
        in_specs=[
            specs["smem"], specs["smem"], specs["query"], specs["key"], specs["value"],
            specs["query"], specs["total"], specs["window"], specs["doc_row"], specs["doc_col"],
        ],
        out_specs=[specs["query"], specs["key"], specs["key"], specs["window"]],
        out_shape=[
            jax.ShapeDtypeStruct(queries.shape, BF16),
            jax.ShapeDtypeStruct((length, queries.shape[1]), BF16),
            jax.ShapeDtypeStruct((length, queries.shape[1]), BF16),
            jax.ShapeDtypeStruct((pairs, 8, width), F32),
        ],
        scratch_shapes=[
            pltpu.VMEM((2, LANES, width), F32),
            pltpu.VMEM((2, LANES, width), F32),
            pltpu.VMEM((LANES, length), BF16),
            pltpu.VMEM((2, length, BLOCK), F32),
            pltpu.VMEM((2, length, BLOCK), F32),
            pltpu.VMEM((2, 8, BLOCK), F32),
            pltpu.VMEM((2, HEAD_DIM, BLOCK), F32),
            pltpu.VMEM((length, LANES), F32),
            pltpu.VMEM((length, LANES), F32),
        ],
        compiler_params=pltpu.CompilerParams(vmem_limit_bytes=VMEM_CAP),
        name="attention_backward",
    )(active, base, queries, key_values, key_values, grads, totals, window, doc_row, doc_col)


def expert_kernel(experts, count, shares, place_ref, rows_ref, grads_ref, router_ref, *refs):
    ins, downs = refs[:count], refs[count : 2 * count]
    (rows_all, scaled_all, act_ref, gate_low_ref, up_low_ref, row_part, out_part,
     in_all, down_all, sems) = refs[-10:]
    expert, ctx, share = place_ref[0], place_ref[1], place_ref[2]
    depth = ins[0].shape[1]
    ff = ins[0].shape[2]

    @pl.when(pl.program_id(0) == 0)
    def _():
        copies = []
        for j in range(count):
            part = pl.ds(j * depth, depth)
            copies.append(pltpu.make_async_copy(ins[j], in_all.at[:, part, :], sems.at[0, j]))
            copies.append(pltpu.make_async_copy(downs[j], down_all.at[:, part], sems.at[1, j]))
        for copy in copies:
            copy.start()
        for copy in copies:
            copy.wait()

    slots = rows_ref.shape[0]
    lane = lax.broadcasted_iota(jnp.int32, (slots, LANES), 1)
    logits = jnp.where(lane < experts, mm(rows_ref[...], router_ref[...]), NEG_FILL)
    powers = jnp.exp(logits - jnp.max(logits, axis=1, keepdims=True))
    probs = powers / jnp.sum(powers, axis=1, keepdims=True)
    gate = jnp.sum(jnp.where(lane == expert, probs, 0.0), axis=1, keepdims=True)
    rows_all[...] = rows_ref[...]
    scaled_all[...] = (gate * grads_ref[...].astype(F32)).astype(BF16)
    order = [pl.ds(pl.multiple_of((ctx ^ j) * depth, depth), depth) for j in range(count)]
    rows = jnp.concatenate([rows_ref[:, part] for part in order], axis=1)
    grads = jnp.concatenate([grads_ref[:, part] for part in order], axis=1)
    dots = jnp.zeros((slots, 1), F32)
    for start in range(0, ff, BLOCK):
        part = slice(start, min(ff, start + BLOCK))
        value = mm(rows, in_all[0, :, part])
        up = mm(rows, in_all[1, :, part])
        back = mm(grads, down_all[part, :], NT)
        square = value * value
        wave = jnp.tanh(GELU_K * value * (1.0 + GELU_C * square))
        half = 0.5 * (1.0 + wave)
        bent = value * half
        slope = half + 0.5 * value * (1.0 - wave * wave) * (
            GELU_K * (1.0 + 3.0 * GELU_C * square)
        )
        act = (bent * up).astype(BF16)
        act_ref[:, part] = act
        dots += jnp.sum(act.astype(F32) * back, axis=1, keepdims=True)
        scaled = gate * back
        gate_low_ref[:, part] = (scaled * up * slope).astype(BF16)
        up_low_ref[:, part] = (scaled * bent).astype(BF16)
    share_width = D // shares
    for j in range(count):
        part = slice(j * depth, (j + 1) * depth)
        first = (ctx ^ j) * depth
        owner = (first // share_width) ^ share
        spot = pl.ds(pl.multiple_of(first % share_width, depth), depth)
        row = mm(gate_low_ref[...], in_all[0, part, :], NT)
        row += mm(up_low_ref[...], in_all[1, part, :], NT)
        row_part[owner, :, spot] = row.astype(BF16)
        out_part[owner, :, spot] = (gate * mm(act_ref[...], down_all[:, part])).astype(BF16)
    high = dots.astype(BF16).astype(F32)
    stride = LANES // shares
    tail = jnp.where(lane == share * stride + expert, high, 0.0)
    tail = jnp.where(lane == share * stride + stride // 2 + expert, dots - high, tail)
    for m in range(shares):
        row_part[m, :, share_width:] = tail.astype(BF16)


def expert_block(block, blocks, places, rows, grads, router, ins, downs, held, experts, shares):
    slots, width = rows.shape
    ff = ins[0].shape[2]
    count = len(ins)
    share_width = width // shares
    vmem = pl.BlockSpec(memory_space=pltpu.VMEM)
    hbm = pl.BlockSpec(memory_space=pl.ANY)
    at_block = lambda i: (block, 0)
    sizes = (width, width, ff, ff, ff)
    aliases = {4 + 2 * count + k: k for k in range(5)} if held else {}
    return pl.pallas_call(
        functools.partial(expert_kernel, experts, count, shares),
        grid=(1,),
        in_specs=[pl.BlockSpec(memory_space=pltpu.SMEM)]
        + [vmem] * 3
        + [hbm] * (2 * count + len(held)),
        out_specs=[pl.BlockSpec((slots, size), at_block) for size in sizes] + [vmem] * 2,
        out_shape=[jax.ShapeDtypeStruct((blocks * slots, size), BF16) for size in sizes]
        + [
            jax.ShapeDtypeStruct((shares, slots, share_width + LANES), BF16),
            jax.ShapeDtypeStruct((shares, slots, share_width), BF16),
        ],
        scratch_shapes=[
            pltpu.VMEM((2, width, ff), BF16),
            pltpu.VMEM((ff, width), BF16),
            pltpu.SemaphoreType.DMA((2, count)),
        ],
        input_output_aliases=aliases,
        compiler_params=pltpu.CompilerParams(vmem_limit_bytes=VMEM_CAP),
        name="expert_block",
    )(places, rows, grads, router, *ins, *downs, *held)


def shards(
    hidden_in,
    out_grad,
    segments,
    routes,
    bucket_table,
    qkv_weight,
    out_weight,
    router,
    norm_gains,
    position_bias,
    expert_in,
    expert_down,
    qkv_first,
    qkv_second,
    out_first,
    out_second,
    router_first,
    router_second,
    gains_first,
    gains_second,
    bias_first,
    bias_second,
    in_first,
    in_second,
    down_first,
    down_second,
):
    tokens = hidden_in.shape[0]
    dp_count, ctx_count, tp_count = (lax.axis_size(a) for a in ("dp", "ctx", "tp"))
    dp_place, ctx_place, tp_place = (lax.axis_index(a) for a in ("dp", "ctx", "tp"))
    length = tokens * ctx_count
    heads_here = position_bias.shape[0]
    width_here = heads_here * HEAD_DIM
    pairs = heads_here // 2
    expert_count = router.shape[1]
    top_count = routes.shape[1]
    own_rows = router.shape[0]
    share_width = D // tp_count

    tail_pack = jnp.pad(
        jnp.concatenate([router, norm_gains.T], axis=1), ((0, 0), (0, LANES - expert_count - 2))
    )
    pack = jnp.concatenate(
        [qkv_weight.reshape(own_rows, 3 * width_here), out_weight.T, tail_pack], axis=1
    )
    hidden_pieces = gather_xor(hidden_in, "ctx")
    ctx_pack = assemble(gather_xor(pack, "ctx"), ctx_place)
    full_pack = assemble(gather_xor(ctx_pack, "dp"), dp_place)
    docs_pieces = gather_xor(segments.reshape(1, -1), "ctx")
    qkv_flat = full_pack[:, : 3 * width_here]
    out_flip = full_pack[:, 3 * width_here : 4 * width_here]
    small = full_pack[:, 4 * width_here :]
    router_full = small[:, :expert_count]
    gain_values = small[:, expert_count : expert_count + 2].T.astype(F32)
    out_all = in_order(gather_xor(out_flip, "tp"), tp_place, 1)

    capacity = max(2, min(tokens, 5 * top_count * tokens // (4 * expert_count)))
    flat_routes = routes.reshape(-1)
    route_onehot = (
        flat_routes[:, None] == jnp.arange(expert_count, dtype=jnp.int32)[None, :]
    ).astype(jnp.int32)
    earlier = jnp.cumsum(route_onehot, axis=0) - route_onehot
    position = jnp.sum(earlier * route_onehot, axis=1).reshape(tokens, top_count)
    slot_expert = dp_place ^ jnp.arange(dp_count, dtype=jnp.int32)
    slot_index = jnp.arange(capacity, dtype=jnp.int32)
    chosen = jnp.zeros((dp_count, capacity, tokens), jnp.bool_)
    for k in range(top_count):
        chosen = chosen | (
            (routes[:, k][None, None, :] == slot_expert[:, None, None])
            & (position[:, k][None, None, :] == slot_index[None, :, None])
        )
    picker = chosen.astype(BF16)
    send_grads = jnp.einsum(
        "mct,td->mcd", picker, out_grad, preferred_element_type=F32
    ).astype(BF16)
    arrived_grads = [send_grads[0]] + [swap(send_grads[m], "dp", m) for m in range(1, dp_count)]
    in_pieces = gather_xor(expert_in[0], "ctx")
    down_pieces = gather_xor(expert_down[0], "ctx")

    rev_table = bucket_table[::-1]
    window_width = tokens + length
    rev_table = jnp.pad(rev_table, (0, 1), constant_values=BUCKETS)
    first_row = ctx_place * tokens
    window_table = lax.dynamic_slice(rev_table, (first_row,), (window_width,))
    table_onehot = (
        window_table[None, :] == jnp.arange(BUCKETS, dtype=jnp.int32)[:, None]
    ).astype(F32)
    window = jnp.dot(
        position_bias, table_onehot, precision=lax.Precision.HIGHEST, preferred_element_type=F32
    )
    window = jnp.pad(window.reshape(pairs, 2, window_width), ((0, 0), (0, 6), (0, 0)))
    docs_row = segments.reshape(1, tokens)
    docs_all = jnp.concatenate(docs_pieces, axis=1).reshape(length)
    doc_col = jnp.broadcast_to(docs_all[:, None], (length, LANES))
    doc_row = jnp.broadcast_to(docs_row, (8, tokens))
    query_docs = docs_row.reshape(tokens // BLOCK, BLOCK)
    key_docs = docs_all.reshape(length // BLOCK, BLOCK)
    active = (
        (key_docs[:, -1][None, :] >= query_docs[:, 0][:, None])
        & (key_docs[:, 0][None, :] <= query_docs[:, -1][:, None])
    ).astype(jnp.int32)
    block_rows = (
        (ctx_place ^ jnp.arange(ctx_count, dtype=jnp.int32))[:, None] * tokens
        + jnp.arange(tokens // BLOCK, dtype=jnp.int32)[None, :] * BLOCK
    ).reshape(-1)
    base = (length - LANES - block_rows).astype(jnp.int32)

    hidden_all = jnp.concatenate(hidden_pieces, axis=0)
    inputs = hidden_in.astype(F32)
    scale_one = rms_scale(inputs)
    normed_one = (inputs * scale_one * gain_values[0]).astype(BF16)
    inputs_all = hidden_all.astype(F32)
    normed_all = (inputs_all * rms_scale(inputs_all) * gain_values[0]).astype(BF16)
    queries = jnp.dot(
        normed_one, qkv_flat[:, :width_here], preferred_element_type=F32
    ).astype(BF16)
    key_values = jnp.dot(
        normed_all, qkv_flat[:, width_here:], preferred_element_type=F32
    ).astype(BF16)

    attended, totals = attention(active, base, queries, key_values, window, doc_row, doc_col)
    attended_all = in_order(gather_xor(attended, "tp"), tp_place, 1)
    middle = inputs + mm(attended_all, out_all, NT)
    scale_two = rms_scale(middle)
    normed_two = (middle * scale_two * gain_values[1]).astype(BF16)
    router_probs = jax.nn.softmax(
        jnp.dot(normed_two, router_full, preferred_element_type=F32), axis=-1
    )
    send_rows = jnp.einsum(
        "mct,td->mcd", picker, normed_two, preferred_element_type=F32
    ).astype(BF16)
    arrived_rows = [send_rows[0]] + [swap(send_rows[m], "dp", m) for m in range(1, dp_count)]

    router_lanes = jnp.where(
        jnp.arange(LANES)[None, :] < expert_count, small, jnp.zeros_like(small)
    )
    places = jnp.stack([dp_place, ctx_place, tp_place]).astype(jnp.int32)
    held = ()
    back_rows, back_outs = [], []
    for m in range(dp_count):
        *held, row_part, out_part = expert_block(
            m, dp_count, places, arrived_rows[m], arrived_grads[m], router_lanes,
            in_pieces, down_pieces, held, expert_count, tp_count,
        )
        row_sum = scatter_sum([row_part[k] for k in range(tp_count)], "tp").astype(BF16)
        out_sum = scatter_sum([out_part[k] for k in range(tp_count)], "tp").astype(BF16)
        back_rows.append(swap(row_sum, "dp", m) if m else row_sum)
        back_outs.append(swap(out_sum, "dp", m) if m else out_sum)
    rows_all, scaled_all, act_all, gate_low_all, up_low_all = held

    def rows_by_ctx(values):
        depth = values.shape[0] // ctx_count
        return [
            lax.dynamic_slice_in_dim(values, (ctx_place ^ j) * depth, depth, 0)
            for j in range(ctx_count)
        ]

    def columns_by_ctx(values):
        depth = values.shape[1] // ctx_count
        return [
            lax.dynamic_slice_in_dim(values, (ctx_place ^ j) * depth, depth, 1)
            for j in range(ctx_count)
        ]

    def weight_grad(left, right):
        return lax.dot_general(
            left, right, (((0,), (0,)), ((), ())), preferred_element_type=F32
        ).astype(BF16)

    gate_total = scatter_sum(rows_by_ctx(weight_grad(rows_all, gate_low_all)), "ctx")
    up_total = scatter_sum(rows_by_ctx(weight_grad(rows_all, up_low_all)), "ctx")
    down_total = scatter_sum(columns_by_ctx(weight_grad(act_all, scaled_all)), "ctx")[None]
    in_total = jnp.stack([gate_total, up_total], axis=0)[None]

    def to_tokens(parts):
        whole = jnp.concatenate(parts, axis=0)
        flat = picker.reshape(dp_count * capacity, tokens)
        return lax.dot_general(flat, whole, (((0,), (0,)), ((), ())), preferred_element_type=F32)

    mixed_half = to_tokens(back_outs).astype(BF16)
    mixed = in_order(gather_xor(mixed_half, "tp"), tp_place, 1)
    output = middle + mixed.astype(F32)

    returned = to_tokens(back_rows)
    prob_grad = jnp.sum(
        returned[:, share_width:].reshape(tokens, 2 * tp_count, LANES // (2 * tp_count)), axis=1
    )[:, :expert_count]
    logit_grad = router_probs * (
        prob_grad - jnp.sum(router_probs * prob_grad, axis=-1, keepdims=True)
    )
    router_share = lax.dynamic_slice_in_dim(router_full, tp_place * share_width, share_width, 0)
    grad_half = returned[:, :share_width] + jnp.dot(
        logit_grad, router_share.T.astype(F32), precision=lax.Precision.HIGHEST,
        preferred_element_type=F32,
    )
    normed_two_grad = in_order(
        gather_xor(grad_half.astype(BF16), "tp"), tp_place, 1
    ).astype(F32)
    middle_part, gain_two_grad = norm_back(middle, scale_two, gain_values[1], normed_two_grad)
    middle_grad = out_grad.astype(F32) + middle_part
    middle_low = middle_grad.astype(BF16)
    attended_grad = jnp.dot(middle_low, out_flip, preferred_element_type=F32).astype(BF16)
    out_flip_grad = weight_grad(middle_low, attended)
    router_grad = jnp.dot(
        normed_two.T.astype(F32), logit_grad, precision=lax.Precision.HIGHEST,
        preferred_element_type=F32,
    )

    query_grad, key_part, value_part, offset_grad = attention_back(
        active, base, queries, key_values, attended_grad, totals, window, doc_row, doc_col
    )
    bias_part = lax.dot_general(
        offset_grad[:, :2, :].reshape(heads_here, window_width), table_onehot, NT,
        precision=lax.Precision.HIGHEST, preferred_element_type=F32,
    )
    bias_total = all_sum(all_sum(bias_part, "ctx"), "dp")

    def row_blocks(values):
        return [values[j * tokens : (j + 1) * tokens] for j in range(ctx_count)]

    key_total = scatter_sum(row_blocks(key_part), "ctx").astype(BF16)
    value_total = scatter_sum(row_blocks(value_part), "ctx").astype(BF16)
    qkv_rows_grad = jnp.concatenate([query_grad, key_total, value_total], axis=1)
    normed_one_grad = all_sum(mm(qkv_rows_grad, qkv_flat, NT).astype(BF16), "tp").astype(F32)
    input_part, gain_one_grad = norm_back(inputs, scale_one, gain_values[0], normed_one_grad)
    input_grad = middle_grad + input_part
    qkv_weight_grad = weight_grad(normed_one, qkv_rows_grad)

    tail_grad = jnp.pad(
        jnp.concatenate(
            [router_grad, jnp.stack([gain_one_grad, gain_two_grad], axis=1)], axis=1
        ),
        ((0, 0), (0, LANES - expert_count - 2)),
    ).astype(BF16)
    grad_pack = jnp.concatenate([qkv_weight_grad, out_flip_grad, tail_grad], axis=1)
    grad_pack = grad_pack.reshape(dp_count, ctx_count, own_rows, grad_pack.shape[1])
    ctx_parts = [
        lax.dynamic_slice_in_dim(grad_pack, ctx_place ^ j, 1, 1)[:, 0] for j in range(ctx_count)
    ]
    ctx_total = scatter_sum(ctx_parts, "ctx").astype(BF16)
    dp_parts = [
        lax.dynamic_slice_in_dim(ctx_total, dp_place ^ j, 1, 0)[0] for j in range(dp_count)
    ]
    pack_total = scatter_sum(dp_parts, "dp")
    qkv_total = pack_total[:, : 3 * width_here].reshape(own_rows, 3, width_here)
    out_total = pack_total[:, 3 * width_here : 4 * width_here].T
    tail_total = pack_total[:, 4 * width_here :]
    router_total = tail_total[:, :expert_count]
    gains_total = tail_total[:, expert_count : expert_count + 2].T

    qkv_new = adamw_step(qkv_weight.astype(F32), qkv_total, qkv_first, qkv_second, MAIN_RATE)
    out_new = adamw_step(out_weight.astype(F32), out_total, out_first, out_second, MAIN_RATE)
    router_new = adamw_step(
        router.astype(F32), router_total, router_first, router_second, MAIN_RATE
    )
    gains_new = adamw_step(
        norm_gains.astype(F32), gains_total, gains_first, gains_second, MAIN_RATE
    )
    bias_new = adamw_step(position_bias, bias_total, bias_first, bias_second, BIAS_RATE)
    in_new = adamw_step(expert_in.astype(F32), in_total, in_first, in_second, MAIN_RATE)
    down_new = adamw_step(expert_down.astype(F32), down_total, down_first, down_second, MAIN_RATE)
    return (
        output,
        input_grad,
        qkv_total,
        *qkv_new,
        out_total,
        *out_new,
        router_total,
        *router_new,
        gains_total,
        *gains_new,
        bias_total,
        *bias_new,
        in_total,
        *in_new,
        down_total,
        *down_new,
    )


def solution(mesh):
    token_rows = P(("dp", "ctx"), None)
    qkv = P(("dp", "ctx"), None, "tp")
    out = P("tp", ("dp", "ctx"))
    gains = P(None, ("dp", "ctx"))
    bias = P("tp", None)
    expert_in = P("dp", None, "ctx", "tp")
    expert_down = P("dp", "tp", "ctx")
    placed = (
        token_rows, token_rows, P("dp", "ctx"), token_rows, P(),
        qkv, out, token_rows, gains, bias, expert_in, expert_down,
        qkv, qkv, out, out, token_rows, token_rows, gains, gains, bias, bias,
        expert_in, expert_in, expert_down, expert_down,
    )
    return jax.shard_map(
        shards,
        mesh=mesh,
        in_specs=placed,
        out_specs=(token_rows, token_rows)
        + (qkv,) * 4
        + (out,) * 4
        + (token_rows,) * 4
        + (gains,) * 4
        + (bias,) * 4
        + (expert_in,) * 4
        + (expert_down,) * 4,
        check_vma=False,
    )
```

profile of v0, /device:TPU:0, one launch (start us, length us, event | category | flops | bytes accessed | tf_op | source)
XLA Modules:
  0.0 845.4 jit_solution(12751639913154004970)
XLA Ops:
  17.5 34.9 %shard_map.481.refs_0_ = bf16[256,2176]{1,0:T(8,128)(2,1)} custom-call(s32[1]{0:T(128)} %bitcast.5.place_ref, bf16[64,2176]{1,0:T(8,128)(2,1)} %copy-done.37, bf16[64,2176]{1,0:T(8,128)(2,1)} %copy-done.65, bf16[64,2176]{1,0:T(8,128)(2,1)} %copy-done.64, bf16[64,2176]{1,0:T(8,128)(2,1)} %copy-done.66), custom_call_target="tpu_custom_call" | custom-call | tf_op jit(solution)/shard_map/pallas_call | solution.py:115
  64.1 40.1 %collective-permute-done.7.refs_2_ = bf16[256,2176]{1,0:T(8,128)(2,1)} collective-permute-done((bf16[256,2176]{1,0:T(8,128)(2,1)}, bf16[256,2176]{1,0:T(8,128)(2,1)}, u32[]{:S(2)}, u32[]{:S(2)}) %collective-permute-start.7) | collective-permute-done | bytes 1114144 | tf_op jit(solution)/shard_map/ppermute | solution.py:56
  109.3 3.7 collective-permute-done.6.refs_1_
  113.0 23.2 %collective-permute-done.8.refs_3_ = bf16[256,2176]{1,0:T(8,128)(2,1)} collective-permute-done((bf16[256,2176]{1,0:T(8,128)(2,1)}, bf16[256,2176]{1,0:T(8,128)(2,1)}, u32[]{:S(2)}, u32[]{:S(2)}) %collective-permute-start.8) | collective-permute-done | bytes 1114144 | tf_op jit(solution)/shard_map/ppermute | solution.py:56
  136.1 136.1 %shard_map.482 = bf16[1024,2176]{1,0:T(8,128)(2,1)} custom-call(s32[1]{0:T(128)} %bitcast.4.place_ref, bf16[256,2176]{1,0:T(8,128)(2,1)} %shard_map.481.refs_0_, bf16[256,2176]{1,0:T(8,128)(2,1)} %collective-permute-done.6.refs_1_, bf16[256,2176]{1,0:T(8,128)(2,1)} %collective-permute-done.7.refs_2_, bf16[256,2176]{1,0:T(8,128)(2,1)} %collective-permute-done.8.refs_3_), custom_call_target="tpu_custom_call" | custom-call | tf_op jit(solution)/shard_map/pallas_call | solution.py:115
  277.8 9.7 %fusion.11.key_ref.value_ref = bf16[2048,1024]{1,0:T(8,128)(2,1)} fusion(f32[1024]{0:T(1024)S(1)} %get-tuple-element.253, f32[2048]{0:T(1024)S(1)} %add_rsqrt_fusion, bf16[1024,2176]{1,0:T(8,128)(2,1)} %shard_map.482, bf16[512,1024]{1,0:T(8,128)(2,1)} %collective-permute-done.11, bf16[512,1024]{1,0:T(8,128)(2,1)} %collective-permute-done.10, ...), kind=kOutput, calls=%fused_computation.22 | convolution fusion | flops 4320133120 | bytes 10498048 | tf_op jit(solution)/shard_map/dot_general | solution.py:608
  291.0 24.9 %attention_forward.1 = (bf16[512,512]{1,0:T(8,128)(2,1)}, f32[4,8,512]{2,1,0:T(8,128)}) custom-call(s32[2,8]{1,0:T(2,128)} %and_convert_fusion.active_ref, s32[8]{0:T(128)} %sub.31.base_ref, bf16[512,512]{1,0:T(8,128)(2,1)} %convolution_convert_fusion.8.query_ref, bf16[2048,1024]{1,0:T(8,128)(2,1)} %fusion.11.key_ref.value_ref, ...), custom_call_target="tpu_custom_call" | custom-call | tf_op jit(solution)/shard_map/attention_forward/pallas_call | solution.py:331
  316.6 3.2 slice_bitcast_fusion.6
  322.1 7.1 collective-permute-done.12
  330.4 3.1 collective-permute-start.22
  343.2 12.7 %expert_block.4 = (bf16[1280,1024]{1,0:T(8,128)(2,1)}, bf16[1280,1024]{1,0:T(8,128)(2,1)}, bf16[1280,1408]{1,0:T(8,128)(2,1)}, bf16[1280,1408]{1,0:T(8,128)(2,1)...) custom-call(s32[3]{0:T(128)} %pad_add_fusion.place_ref, ...), custom_call_target="tpu_custom_call" | custom-call | tf_op jit(solution)/shard_map/expert_block/pallas_call | solution.py:468
  370.2 6.6 collective-permute-done.20
  384.5 29.2 %collective-permute-done.21.rows_ref = bf16[320,1024]{1,0:T(8,128)(2,1)} collective-permute-done((bf16[320,1024]{1,0:T(8,128)(2,1)}, bf16[320,1024]{1,0:T(8,128)(2,1)}, u32[]{:S(2)}, u32[]{:S(2)}) %collective-permute-start.21) | collective-permute-done | bytes 655392 | tf_op jit(solution)/shard_map/ppermute | solution.py:56
  413.6 12.9 %expert_block.5 = (bf16[1280,1024]{1,0:T(8,128)(2,1)}, bf16[1280,1024]{1,0:T(8,128)(2,1)}, bf16[1280,1408]{1,0:T(8,128)(2,1)}, bf16[1280,1408]{1,0:T(8,128)(2,1)...) custom-call(s32[3]{0:T(128)} %pad_add_fusion.place_ref, ...), custom_call_target="tpu_custom_call", output_to_operand_aliasing={{0}: (12, {}), {1}: (13, {}), {2}: (14, {}), {3}: (15, {}),... | custom-call | tf_op jit(solution)/shard_map/expert_block/pallas_call | solution.py:468
  426.6 36.8 %collective-permute-done.25.rows_ref = bf16[320,1024]{1,0:T(8,128)(2,1)} collective-permute-done((bf16[320,1024]{1,0:T(8,128)(2,1)}, bf16[320,1024]{1,0:T(8,128)(2,1)}, u32[]{:S(2)}, u32[]{:S(2)}) %collective-permute-start.25) | collective-permute-done | bytes 655392 | tf_op jit(solution)/shard_map/ppermute | solution.py:56
  463.4 12.7 %expert_block.6 = (bf16[1280,1024]{1,0:T(8,128)(2,1)}, bf16[1280,1024]{1,0:T(8,128)(2,1)}, bf16[1280,1408]{1,0:T(8,128)(2,1)}, bf16[1280,1408]{1,0:T(8,128)(2,1)...) custom-call(s32[3]{0:T(128)} %pad_add_fusion.place_ref, ...), custom_call_target="tpu_custom_call", output_to_operand_aliasing={{0}: (12, {}), {1}: (13, {}), {2}: (14, {}), {3}: (15, {}),... | custom-call | tf_op jit(solution)/shard_map/expert_block/pallas_call | solution.py:468
  477.0 13.2 %expert_block.7 = (bf16[1280,1024]{1,0:T(8,128)(2,1)}, bf16[1280,1024]{1,0:T(8,128)(2,1)}, bf16[1280,1408]{1,0:T(8,128)(2,1)}, bf16[1280,1408]{1,0:T(8,128)(2,1)...) custom-call(s32[3]{0:T(128)} %pad_add_fusion.place_ref, ...), custom_call_target="tpu_custom_call", output_to_operand_aliasing={{0}: (12, {}), {1}: (13, {}), {2}: (14, {}), {3}: (15, {}),... | custom-call | tf_op jit(solution)/shard_map/expert_block/pallas_call | solution.py:468
  490.2 6.9 convolution_convert_fusion.1
  500.2 4.5 convolution_convert_fusion.3
  506.1 4.7 convolution_convert_fusion.2
  517.0 6.1 collective-permute-done.23
  524.0 6.1 collective-permute-done.27
  531.0 6.1 collective-permute-done.31
  538.1 7.8 collective-permute-done.35
  546.1 8.6 %collective-permute-done.37 = bf16[320,640]{1,0:T(8,128)(2,1)S(1)} collective-permute-done((bf16[320,640]{1,0:T(8,128)(2,1)S(1)}, bf16[320,640]{1,0:T(8,128)(2,1)S(1)}, u32[]{:S(2)}, u32[]{:S(2)}) %collective-permute-start.37) | collective-permute-done | bytes 409632 | tf_op jit(solution)/shard_map/ppermute | solution.py:56
  556.8 5.7 collective-permute-done.39
  563.1 6.1 collective-permute-done.28
  569.2 6.2 collective-permute-start.38
  582.8 20.5 %collective-permute-done.38 = bf16[320,640]{1,0:T(8,128)(2,1)S(1)} collective-permute-done((bf16[320,640]{1,0:T(8,128)(2,1)S(1)}, bf16[320,640]{1,0:T(8,128)(2,1)S(1)}, u32[]{:S(2)}, u32[]{:S(2)}) %collective-permute-start.38) | collective-permute-done | bytes 409632 | tf_op jit(solution)/shard_map/ppermute | solution.py:56
  610.3 7.2 collective-permute-done.41
  622.2 39.4 %attention_backward.1 = (bf16[512,512]{1,0:T(8,128)(2,1)}, bf16[2048,512]{1,0:T(8,128)(2,1)}, bf16[2048,512]{1,0:T(8,128)(2,1)}, f32[4,8,2560]{2,1,0:T(8,128)}) custom-call(s32[2,8]{1,0:T(2,128)} %and_convert_fusion.active_ref, s32[8]{0:T(128)} %sub.31.base_ref, bf16[512,512]{1,0:T(8,128)(2,1)} %convolution_convert_fusion.8.query_ref, ...), custom_call_target="tpu_custom_call" | custom-call | tf_op jit(solution)/shard_map/attention_backward/pallas_call | solution.py:360
  668.8 14.7 %collective-permute-start.57 = (f32[8,32]{1,0:T(8,128)S(1)}, f32[8,32]{1,0:T(8,128)S(1)}, u32[]{:S(2)}, u32[]{:S(2)}) collective-permute-start(f32[8,32]{1,0:T(8,128)S(1)} %add.392), channel_id=1, source_target_pairs={{0,8},{8,0},{16,24},{24,16},{1,9},{9,1},{17,25},{25,17},{2,10},{10... | collective-permute-start | bytes 3080 | tf_op jit(solution)/shard_map/ppermute | solution.py:56
  691.1 9.3 %collective-permute-done.44 = bf16[512,512]{1,0:T(8,128)(2,1)S(1)} collective-permute-done((bf16[512,512]{1,0:T(8,128)(2,1)S(1)}, bf16[512,512]{1,0:T(8,128)(2,1)S(1)}, u32[]{:S(2)}, u32[]{:S(2)}) %collective-permute-start.44) | collective-permute-done | bytes 524320 | tf_op jit(solution)/shard_map/ppermute | solution.py:56
  701.5 10.1 %collective-permute-done.47 = bf16[512,512]{1,0:T(8,128)(2,1)S(1)} collective-permute-done((bf16[512,512]{1,0:T(8,128)(2,1)S(1)}, bf16[512,512]{1,0:T(8,128)(2,1)S(1)}, u32[]{:S(2)}, u32[]{:S(2)}) %collective-permute-start.47) | collective-permute-done | bytes 524320 | tf_op jit(solution)/shard_map/ppermute | solution.py:56
  715.8 11.2 %collective-permute-done.67 = bf16[1408,256]{1,0:T(8,128)(2,1)S(1)} collective-permute-done((bf16[1408,256]{1,0:T(8,128)(2,1)S(1)}, bf16[1408,256]{1,0:T(8,128)(2,1)S(1)}, u32[]{:S(2)}, u32[]{:S(2)}) %collective-permute-start.67) | collective-permute-done | bytes 720928 | tf_op jit(solution)/shard_map/ppermute | solution.py:56
  730.3 12.2 %collective-permute-done.61 = bf16[256,1408]{1,0:T(8,128)(2,1)S(1)} collective-permute-done((bf16[256,1408]{1,0:T(8,128)(2,1)S(1)}, bf16[256,1408]{1,0:T(8,128)(2,1)S(1)}, u32[]{:S(2)}, u32[]{:S(2)}) %collective-permute-start.61) | collective-permute-done | bytes 720928 | tf_op jit(solution)/shard_map/ppermute | solution.py:56
  745.5 3.6 convolution_convert_fusion
  757.2 3.2 fusion.77
  760.4 4.2 add_multiply_fusion.1
  766.9 4.5 add_multiply_fusion
  771.4 3.6 copy.253
  775.0 3.6 copy.221
  778.7 14.7 %collective-permute-done.51 = bf16[4,64,2176]{2,1,0:T(8,128)(2,1)} collective-permute-done((bf16[4,64,2176]{2,1,0:T(8,128)(2,1)}, bf16[4,64,2176]{2,1,0:T(8,128)(2,1)}, u32[]{:S(2)}, u32[]{:S(2)}) %collective-permute-start.51) | collective-permute-done | bytes 1114144 | tf_op jit(solution)/shard_map/ppermute | solution.py:56
  793.3 3.6 copy.222
  796.9 3.8 fusion.6
  805.2 3.6 maximum_bitcast_fusion
  823.0 3.6 fusion.22
  827.9 6.8 collective-permute-done.54
  (483 shorter events, 180.7 us)
Async XLA Ops:
  6.4 51.7 %collective-permute-start.10 = (bf16[512,1024]{1,0:T(8,128)(2,1)}, bf16[512,1024]{1,0:T(8,128)(2,1)}, u32[]{:S(2)}, u32[]{:S(2)}) collective-permute-start(bf16[512,1024]{1,0:T(8,128)(2,1)} %param.26), channel_id=1, source_target_pairs={{0,4},{2,6},{4,0},{6,2},{1,5},{3,7},{5,1},{7,3},{8,12},{10,14},{12... | collective-permute-start | bytes 3145736 | tf_op jit(solution)/shard_map/ppermute | solution.py:56
  6.5 99.1 %collective-permute-start.9 = (bf16[512,1024]{1,0:T(8,128)(2,1)}, bf16[512,1024]{1,0:T(8,128)(2,1)}, u32[]{:S(2)}, u32[]{:S(2)}) collective-permute-start(bf16[512,1024]{1,0:T(8,128)(2,1)} %param.26), channel_id=1, source_target_pairs={{0,2},{2,0},{4,6},{6,4},{1,3},{3,1},{5,7},{7,5},{8,10},{10,8},{12,... | collective-permute-start | bytes 3145736 | tf_op jit(solution)/shard_map/ppermute | solution.py:56
  6.9 53.0 %collective-permute-start = (s32[1,512]{1,0:T(1,128)}, s32[1,512]{1,0:T(1,128)S(1)}, u32[]{:S(2)}, u32[]{:S(2)}) collective-permute-start(s32[1,512]{1,0:T(1,128)} %param.28), channel_id=1, source_target_pairs={{0,2},{2,0},{4,6},{6,4},{1,3},{3,1},{5,7},{7,5},{8,10},{10,8},{12,... | collective-permute-start | bytes 6152 | tf_op jit(solution)/shard_map/ppermute | solution.py:56
  15.0 45.6 %collective-permute-start.1 = (s32[1,512]{1,0:T(1,128)S(1)}, s32[1,512]{1,0:T(1,128)S(1)}, u32[]{:S(2)}, u32[]{:S(2)}) collective-permute-start(s32[1,512]{1,0:T(1,128)S(1)} %copy-done.90), channel_id=1, source_target_pairs={{0,4},{2,6},{4,0},{6,2},{1,5},{3,7},{5,1},{7,3},{8,12},{10,14},{12... | collective-permute-start | bytes 6152 | tf_op jit(solution)/shard_map/ppermute | solution.py:56
  52.4 51.7 %collective-permute-start.7 = (bf16[256,2176]{1,0:T(8,128)(2,1)}, bf16[256,2176]{1,0:T(8,128)(2,1)}, u32[]{:S(2)}, u32[]{:S(2)}) collective-permute-start(bf16[256,2176]{1,0:T(8,128)(2,1)} %shard_map.481.refs_0_), channel_id=1, source_target_pairs={{0,16},{8,24},{16,0},{24,8},{1,17},{9,25},{17,1},{25,9},{2,18},{10... | collective-permute-start | bytes 3342344 | tf_op jit(solution)/shard_map/ppermute | solution.py:56
  58.1 47.5 %collective-permute-start.11 = (bf16[512,1024]{1,0:T(8,128)(2,1)}, bf16[512,1024]{1,0:T(8,128)(2,1)}, u32[]{:S(2)}, u32[]{:S(2)}) collective-permute-start(bf16[512,1024]{1,0:T(8,128)(2,1)} %collective-permute-done.10), channel_id=1, source_target_pairs={{0,2},{2,0},{4,6},{6,4},{1,3},{3,1},{5,7},{7,5},{8,10},{10,8},{12,... | collective-permute-start | bytes 3145736 | tf_op jit(solution)/shard_map/ppermute | solution.py:56
  59.9 273.6 %collective-permute-start.15 = (bf16[2,256,1408]{2,1,0:T(8,128)(2,1)S(1)}, bf16[2,256,1408]{2,1,0:T(8,128)(2,1)S(1)}, u32[]{:S(2)}, u32[]{:S(2)}) collective-permute-start(bf16[2,256,1408]{2,1,0:T(8,128)(2,1)S(1)} %bitcast.173), channel_id=1, source_target_pairs={{0,4},{2,6},{4,0},{6,2},{1,5},{3,7},{5,1},{7,3},{8,12},{10,14},{12... | collective-permute-start | bytes 4325384 | tf_op jit(solution)/shard_map/ppermute | solution.py:56
  62.4 50.5 %collective-permute-start.6 = (bf16[256,2176]{1,0:T(8,128)(2,1)}, bf16[256,2176]{1,0:T(8,128)(2,1)}, u32[]{:S(2)}, u32[]{:S(2)}) collective-permute-start(bf16[256,2176]{1,0:T(8,128)(2,1)} %shard_map.481.refs_0_), channel_id=1, source_target_pairs={{0,8},{8,0},{16,24},{24,16},{1,9},{9,1},{17,25},{25,17},{2,10},{10... | collective-permute-start | bytes 3342344 | tf_op jit(solution)/shard_map/ppermute | solution.py:56
  104.1 32.0 %collective-permute-start.8 = (bf16[256,2176]{1,0:T(8,128)(2,1)}, bf16[256,2176]{1,0:T(8,128)(2,1)}, u32[]{:S(2)}, u32[]{:S(2)}) collective-permute-start(bf16[256,2176]{1,0:T(8,128)(2,1)} %collective-permute-done.7.refs_2_), channel_id=1, source_target_pairs={{0,8},{8,0},{16,24},{24,16},{1,9},{9,1},{17,25},{25,17},{2,10},{10... | collective-permute-start | bytes 3342344 | tf_op jit(solution)/shard_map/ppermute | solution.py:56
  105.6 236.0 %collective-permute-start.14 = (bf16[2,256,1408]{2,1,0:T(8,128)(2,1)S(1)}, bf16[2,256,1408]{2,1,0:T(8,128)(2,1)}, u32[]{:S(2)}, u32[]{:S(2)}) collective-permute-start(bf16[2,256,1408]{2,1,0:T(8,128)(2,1)S(1)} %bitcast.174), channel_id=1, source_target_pairs={{0,2},{2,0},{4,6},{6,4},{1,3},{3,1},{5,7},{7,5},{8,10},{10,8},{12,... | collective-permute-start | bytes 4325384 | tf_op jit(solution)/shard_map/ppermute | solution.py:56
  105.6 224.7 %collective-permute-start.18 = (bf16[1408,256]{1,0:T(8,128)(2,1)}, bf16[1408,256]{1,0:T(8,128)(2,1)}, u32[]{:S(2)}, u32[]{:S(2)}) collective-permute-start(bf16[1408,256]{1,0:T(8,128)(2,1)} %bitcast.175), channel_id=1, source_target_pairs={{0,4},{2,6},{4,0},{6,2},{1,5},{3,7},{5,1},{7,3},{8,12},{10,14},{12... | collective-permute-start | bytes 2162696 | tf_op jit(solution)/shard_map/ppermute | solution.py:56
  276.2 57.4 %collective-permute-start.13 = (bf16[1024,512]{1,0:T(8,128)(2,1)}, bf16[1024,512]{1,0:T(8,128)(2,1)}, u32[]{:S(2)}, u32[]{:S(2)}) collective-permute-start(bf16[1024,512]{1,0:T(8,128)(2,1)} %slice.254), channel_id=1, source_target_pairs={{0,1},{1,0},{2,3},{3,2},{4,5},{5,4},{6,7},{7,6},{8,9},{9,8},{10,11... | collective-permute-start | bytes 3145736 | tf_op jit(solution)/shard_map/ppermute | solution.py:56
  330.4 38.9 %collective-permute-start.22 = (bf16[320,1024]{1,0:T(8,128)(2,1)}, bf16[320,1024]{1,0:T(8,128)(2,1)}, u32[]{:S(2)}, u32[]{:S(2)}) collective-permute-start(bf16[320,1024]{1,0:T(8,128)(2,1)} %get-tuple-element.298), channel_id=1, source_target_pairs={{0,8},{8,0},{16,24},{24,16},{1,9},{9,1},{17,25},{25,17},{2,10},{10... | collective-permute-start | bytes 1966088 | tf_op jit(solution)/shard_map/ppermute | solution.py:56
  357.8 19.8 %collective-permute-start.34 = (bf16[320,640]{1,0:T(8,128)(2,1)}, bf16[320,640]{1,0:T(8,128)(2,1)}, u32[]{:S(2)}, u32[]{:S(2)}) collective-permute-start(bf16[320,640]{1,0:T(8,128)(2,1)} %slice_bitcast_fusion.11), channel_id=1, source_target_pairs={{0,1},{1,0},{2,3},{3,2},{4,5},{5,4},{6,7},{7,6},{8,9},{9,8},{10,11... | collective-permute-start | bytes 1228808 | tf_op jit(solution)/shard_map/ppermute | solution.py:56
  360.4 16.4 %collective-permute-start.20 = (bf16[320,512]{1,0:T(8,128)(2,1)}, bf16[320,512]{1,0:T(8,128)(2,1)}, u32[]{:S(2)}, u32[]{:S(2)}) collective-permute-start(bf16[320,512]{1,0:T(8,128)(2,1)} %slice_bitcast_fusion.15), channel_id=1, source_target_pairs={{0,1},{1,0},{2,3},{3,2},{4,5},{5,4},{6,7},{7,6},{8,9},{9,8},{10,11... | collective-permute-start | bytes 983048 | tf_op jit(solution)/shard_map/ppermute | solution.py:56
  361.5 65.0 %collective-permute-start.26 = (bf16[320,1024]{1,0:T(8,128)(2,1)}, bf16[320,1024]{1,0:T(8,128)(2,1)S(1)}, u32[]{:S(2)}, u32[]{:S(2)}) collective-permute-start(bf16[320,1024]{1,0:T(8,128)(2,1)} %get-tuple-element.297), channel_id=1, source_target_pairs={{0,16},{8,24},{16,0},{24,8},{1,17},{9,25},{17,1},{25,9},{2,18},{10... | collective-permute-start | bytes 1966088 | tf_op jit(solution)/shard_map/ppermute | solution.py:56
  362.6 113.6 %collective-permute-start.30 = (bf16[320,1024]{1,0:T(8,128)(2,1)}, bf16[320,1024]{1,0:T(8,128)(2,1)S(1)}, u32[]{:S(2)}, u32[]{:S(2)}) collective-permute-start(bf16[320,1024]{1,0:T(8,128)(2,1)} %get-tuple-element.296), channel_id=1, source_target_pairs={{0,24},{8,16},{16,8},{24,0},{1,25},{9,17},{17,9},{25,1},{2,26},{10... | collective-permute-start | bytes 1966088 | tf_op jit(solution)/shard_map/ppermute | solution.py:56
  369.3 44.3 %collective-permute-start.21 = (bf16[320,1024]{1,0:T(8,128)(2,1)}, bf16[320,1024]{1,0:T(8,128)(2,1)}, u32[]{:S(2)}, u32[]{:S(2)}) collective-permute-start(bf16[320,1024]{1,0:T(8,128)(2,1)} %get-tuple-element.302), channel_id=1, source_target_pairs={{0,8},{8,0},{16,24},{24,16},{1,9},{9,1},{17,25},{25,17},{2,10},{10... | collective-permute-start | bytes 1966088 | tf_op jit(solution)/shard_map/ppermute | solution.py:56
  376.7 86.7 %collective-permute-start.25 = (bf16[320,1024]{1,0:T(8,128)(2,1)}, bf16[320,1024]{1,0:T(8,128)(2,1)}, u32[]{:S(2)}, u32[]{:S(2)}) collective-permute-start(bf16[320,1024]{1,0:T(8,128)(2,1)} %get-tuple-element.301), channel_id=1, source_target_pairs={{0,16},{8,24},{16,0},{24,8},{1,17},{9,25},{17,1},{25,9},{2,18},{10... | collective-permute-start | bytes 1966088 | tf_op jit(solution)/shard_map/ppermute | solution.py:56
  377.6 98.5 %collective-permute-start.29 = (bf16[320,1024]{1,0:T(8,128)(2,1)}, bf16[320,1024]{1,0:T(8,128)(2,1)}, u32[]{:S(2)}, u32[]{:S(2)}) collective-permute-start(bf16[320,1024]{1,0:T(8,128)(2,1)} %get-tuple-element.300), channel_id=1, source_target_pairs={{0,24},{8,16},{16,8},{24,0},{1,25},{9,17},{17,9},{25,1},{2,26},{10... | collective-permute-start | bytes 1966088 | tf_op jit(solution)/shard_map/ppermute | solution.py:56
  498.2 79.0 %collective-permute-start.66 = (bf16[1408,256]{1,0:T(8,128)(2,1)S(1)}, bf16[1408,256]{1,0:T(8,128)(2,1)S(1)}, u32[]{:S(2)}, u32[]{:S(2)}) collective-permute-start(bf16[1408,256]{1,0:T(8,128)(2,1)S(1)} %get-tuple-element.290), channel_id=1, source_target_pairs={{0,2},{2,0},{4,6},{6,4},{1,3},{3,1},{5,7},{7,5},{8,10},{10,8},{12,... | collective-permute-start | bytes 2162696 | tf_op jit(solution)/shard_map/ppermute | solution.py:56
  513.4 16.7 %collective-permute-start.27 = (bf16[320,512]{1,0:T(8,128)(2,1)S(1)}, bf16[320,512]{1,0:T(8,128)(2,1)S(1)}, u32[]{:S(2)}, u32[]{:S(2)}) collective-permute-start(bf16[320,512]{1,0:T(8,128)(2,1)S(1)} %slice_bitcast_fusion.13), channel_id=1, source_target_pairs={{0,1},{1,0},{2,3},{3,2},{4,5},{5,4},{6,7},{7,6},{8,9},{9,8},{10,11... | collective-permute-start | bytes 983048 | tf_op jit(solution)/shard_map/ppermute | solution.py:56
  514.7 22.5 %collective-permute-start.31 = (bf16[320,512]{1,0:T(8,128)(2,1)S(1)}, bf16[320,512]{1,0:T(8,128)(2,1)S(1)}, u32[]{:S(2)}, u32[]{:S(2)}) collective-permute-start(bf16[320,512]{1,0:T(8,128)(2,1)S(1)} %slice_bitcast_fusion.12), channel_id=1, source_target_pairs={{0,1},{1,0},{2,3},{3,2},{4,5},{5,4},{6,7},{7,6},{8,9},{9,8},{10,11... | collective-permute-start | bytes 983048 | tf_op jit(solution)/shard_map/ppermute | solution.py:56
  515.6 30.3 %collective-permute-start.35 = (bf16[320,640]{1,0:T(8,128)(2,1)S(1)}, bf16[320,640]{1,0:T(8,128)(2,1)S(1)}, u32[]{:S(2)}, u32[]{:S(2)}) collective-permute-start(bf16[320,640]{1,0:T(8,128)(2,1)S(1)} %slice_bitcast_fusion.10), channel_id=1, source_target_pairs={{0,1},{1,0},{2,3},{3,2},{4,5},{5,4},{6,7},{7,6},{8,9},{9,8},{10,11... | collective-permute-start | bytes 1228808 | tf_op jit(solution)/shard_map/ppermute | solution.py:56
  523.1 31.6 %collective-permute-start.37 = (bf16[320,640]{1,0:T(8,128)(2,1)S(1)}, bf16[320,640]{1,0:T(8,128)(2,1)S(1)}, u32[]{:S(2)}, u32[]{:S(2)}) collective-permute-start(bf16[320,640]{1,0:T(8,128)(2,1)S(1)} %slice_bitcast_fusion.9), channel_id=1, source_target_pairs={{0,1},{1,0},{2,3},{3,2},{4,5},{5,4},{6,7},{7,6},{8,9},{9,8},{10,11... | collective-permute-start | bytes 1228808 | tf_op jit(solution)/shard_map/ppermute | solution.py:56
  530.1 32.3 %collective-permute-start.39 = (bf16[320,640]{1,0:T(8,128)(2,1)S(1)}, bf16[320,640]{1,0:T(8,128)(2,1)S(1)}, u32[]{:S(2)}, u32[]{:S(2)}) collective-permute-start(bf16[320,640]{1,0:T(8,128)(2,1)S(1)} %slice_bitcast_fusion.8), channel_id=1, source_target_pairs={{0,1},{1,0},{2,3},{3,2},{4,5},{5,4},{6,7},{7,6},{8,9},{9,8},{10,11... | collective-permute-start | bytes 1228808 | tf_op jit(solution)/shard_map/ppermute | solution.py:56
  537.1 25.4 %collective-permute-start.24 = (bf16[320,512]{1,0:T(8,128)(2,1)S(1)}, bf16[320,512]{1,0:T(8,128)(2,1)S(1)}, u32[]{:S(2)}, u32[]{:S(2)}) collective-permute-start(bf16[320,512]{1,0:T(8,128)(2,1)S(1)} %fusion.85), channel_id=1, source_target_pairs={{0,8},{8,0},{16,24},{24,16},{1,9},{9,1},{17,25},{25,17},{2,10},{10... | collective-permute-start | bytes 983048 | tf_op jit(solution)/shard_map/ppermute | solution.py:56
  545.9 23.3 %collective-permute-start.28 = (bf16[320,512]{1,0:T(8,128)(2,1)S(1)}, bf16[320,512]{1,0:T(8,128)(2,1)S(1)}, u32[]{:S(2)}, u32[]{:S(2)}) collective-permute-start(bf16[320,512]{1,0:T(8,128)(2,1)S(1)} %fusion.84), channel_id=1, source_target_pairs={{0,16},{8,24},{16,0},{24,8},{1,17},{9,25},{17,1},{25,9},{2,18},{10... | collective-permute-start | bytes 983048 | tf_op jit(solution)/shard_map/ppermute | solution.py:56
  562.4 44.0 %collective-permute-start.60 = (bf16[256,1408]{1,0:T(8,128)(2,1)}, bf16[256,1408]{1,0:T(8,128)(2,1)}, u32[]{:S(2)}, u32[]{:S(2)}) collective-permute-start(bf16[256,1408]{1,0:T(8,128)(2,1)} %get-tuple-element.292), channel_id=1, source_target_pairs={{0,2},{2,0},{4,6},{6,4},{1,3},{3,1},{5,7},{7,5},{8,10},{10,8},{12,... | collective-permute-start | bytes 2162696 | tf_op jit(solution)/shard_map/ppermute | solution.py:56
  562.5 102.6 %collective-permute-start.63 = (bf16[256,1408]{1,0:T(8,128)(2,1)}, bf16[256,1408]{1,0:T(8,128)(2,1)}, u32[]{:S(2)}, u32[]{:S(2)}) collective-permute-start(bf16[256,1408]{1,0:T(8,128)(2,1)} %get-tuple-element.294), channel_id=1, source_target_pairs={{0,2},{2,0},{4,6},{6,4},{1,3},{3,1},{5,7},{7,5},{8,10},{10,8},{12,... | collective-permute-start | bytes 2162696 | tf_op jit(solution)/shard_map/ppermute | solution.py:56
  569.2 34.1 %collective-permute-start.38 = (bf16[320,640]{1,0:T(8,128)(2,1)S(1)}, bf16[320,640]{1,0:T(8,128)(2,1)S(1)}, u32[]{:S(2)}, u32[]{:S(2)}) collective-permute-start(bf16[320,640]{1,0:T(8,128)(2,1)S(1)} %fusion.80), channel_id=1, source_target_pairs={{0,16},{8,24},{16,0},{24,8},{1,17},{9,25},{17,1},{25,9},{2,18},{10... | collective-permute-start | bytes 1228808 | tf_op jit(solution)/shard_map/ppermute | solution.py:56
  577.2 26.2 %collective-permute-start.40 = (bf16[320,640]{1,0:T(8,128)(2,1)S(1)}, bf16[320,640]{1,0:T(8,128)(2,1)S(1)}, u32[]{:S(2)}, u32[]{:S(2)}) collective-permute-start(bf16[320,640]{1,0:T(8,128)(2,1)S(1)} %fusion.79), channel_id=1, source_target_pairs={{0,24},{8,16},{16,8},{24,0},{1,25},{9,17},{17,9},{25,1},{2,26},{10... | collective-permute-start | bytes 1228808 | tf_op jit(solution)/shard_map/ppermute | solution.py:56
  582.0 26.8 %collective-permute-start.33 = (bf16[512,512]{1,0:T(8,128)(2,1)}, bf16[512,512]{1,0:T(8,128)(2,1)}, u32[]{:S(2)}, u32[]{:S(2)}) collective-permute-start(bf16[512,512]{1,0:T(8,128)(2,1)} %fusion.64), channel_id=1, source_target_pairs={{0,1},{1,0},{2,3},{3,2},{4,5},{5,4},{6,7},{7,6},{8,9},{9,8},{10,11... | collective-permute-start | bytes 1572872 | tf_op jit(solution)/shard_map/ppermute | solution.py:56
  664.4 21.0 %collective-permute-start.43 = (bf16[512,512]{1,0:T(8,128)(2,1)S(1)}, bf16[512,512]{1,0:T(8,128)(2,1)S(1)}, u32[]{:S(2)}, u32[]{:S(2)}) collective-permute-start(bf16[512,512]{1,0:T(8,128)(2,1)S(1)} %get-tuple-element.306), channel_id=1, source_target_pairs={{0,2},{2,0},{4,6},{6,4},{1,3},{3,1},{5,7},{7,5},{8,10},{10,8},{12,... | collective-permute-start | bytes 1572872 | tf_op jit(solution)/shard_map/ppermute | solution.py:56
  664.9 21.5 %collective-permute-start.46 = (bf16[512,512]{1,0:T(8,128)(2,1)S(1)}, bf16[512,512]{1,0:T(8,128)(2,1)S(1)}, u32[]{:S(2)}, u32[]{:S(2)}) collective-permute-start(bf16[512,512]{1,0:T(8,128)(2,1)S(1)} %get-tuple-element.308), channel_id=1, source_target_pairs={{0,2},{2,0},{4,6},{6,4},{1,3},{3,1},{5,7},{7,5},{8,10},{10,8},{12,... | collective-permute-start | bytes 1572872 | tf_op jit(solution)/shard_map/ppermute | solution.py:56
  668.8 16.6 %collective-permute-start.57 = (f32[8,32]{1,0:T(8,128)S(1)}, f32[8,32]{1,0:T(8,128)S(1)}, u32[]{:S(2)}, u32[]{:S(2)}) collective-permute-start(f32[8,32]{1,0:T(8,128)S(1)} %add.392), channel_id=1, source_target_pairs={{0,8},{8,0},{16,24},{24,16},{1,9},{9,1},{17,25},{25,17},{2,10},{10... | collective-permute-start | bytes 3080 | tf_op jit(solution)/shard_map/ppermute | solution.py:56
  684.8 15.8 %collective-permute-start.45 = (bf16[512,512]{1,0:T(8,128)(2,1)S(1)}, bf16[512,512]{1,0:T(8,128)(2,1)S(1)}, u32[]{:S(2)}, u32[]{:S(2)}) collective-permute-start(bf16[512,512]{1,0:T(8,128)(2,1)S(1)} %get-tuple-element.307), channel_id=1, source_target_pairs={{0,2},{2,0},{4,6},{6,4},{1,3},{3,1},{5,7},{7,5},{8,10},{10,8},{12,... | collective-permute-start | bytes 1572872 | tf_op jit(solution)/shard_map/ppermute | solution.py:56
  685.5 14.8 %collective-permute-start.44 = (bf16[512,512]{1,0:T(8,128)(2,1)S(1)}, bf16[512,512]{1,0:T(8,128)(2,1)S(1)}, u32[]{:S(2)}, u32[]{:S(2)}) collective-permute-start(bf16[512,512]{1,0:T(8,128)(2,1)S(1)} %add_convert_fusion.6), channel_id=1, source_target_pairs={{0,4},{2,6},{4,0},{6,2},{1,5},{3,7},{5,1},{7,3},{8,12},{10,14},{12... | collective-permute-start | bytes 1572872 | tf_op jit(solution)/shard_map/ppermute | solution.py:56
  686.7 24.9 %collective-permute-start.47 = (bf16[512,512]{1,0:T(8,128)(2,1)S(1)}, bf16[512,512]{1,0:T(8,128)(2,1)S(1)}, u32[]{:S(2)}, u32[]{:S(2)}) collective-permute-start(bf16[512,512]{1,0:T(8,128)(2,1)S(1)} %add_convert_fusion.4), channel_id=1, source_target_pairs={{0,4},{2,6},{4,0},{6,2},{1,5},{3,7},{5,1},{7,3},{8,12},{10,14},{12... | collective-permute-start | bytes 1572872 | tf_op jit(solution)/shard_map/ppermute | solution.py:56
  689.9 24.7 %collective-permute-start.65 = (bf16[1408,256]{1,0:T(8,128)(2,1)S(1)}, bf16[1408,256]{1,0:T(8,128)(2,1)S(1)}, u32[]{:S(2)}, u32[]{:S(2)}) collective-permute-start(bf16[1408,256]{1,0:T(8,128)(2,1)S(1)} %copy-done.50), channel_id=1, source_target_pairs={{0,2},{2,0},{4,6},{6,4},{1,3},{3,1},{5,7},{7,5},{8,10},{10,8},{12,... | collective-permute-start | bytes 2162696 | tf_op jit(solution)/shard_map/ppermute | solution.py:56
  690.5 39.8 %collective-permute-start.59 = (bf16[256,1408]{1,0:T(8,128)(2,1)S(1)}, bf16[256,1408]{1,0:T(8,128)(2,1)S(1)}, u32[]{:S(2)}, u32[]{:S(2)}) collective-permute-start(bf16[256,1408]{1,0:T(8,128)(2,1)S(1)} %copy-done.49), channel_id=1, source_target_pairs={{0,2},{2,0},{4,6},{6,4},{1,3},{3,1},{5,7},{7,5},{8,10},{10,8},{12,... | collective-permute-start | bytes 2162696 | tf_op jit(solution)/shard_map/ppermute | solution.py:56
  700.4 56.3 %collective-permute-start.62 = (bf16[256,1408]{1,0:T(8,128)(2,1)}, bf16[256,1408]{1,0:T(8,128)(2,1)}, u32[]{:S(2)}, u32[]{:S(2)}) collective-permute-start(bf16[256,1408]{1,0:T(8,128)(2,1)} %get-tuple-element.293), channel_id=1, source_target_pairs={{0,2},{2,0},{4,6},{6,4},{1,3},{3,1},{5,7},{7,5},{8,10},{10,8},{12,... | collective-permute-start | bytes 2162696 | tf_op jit(solution)/shard_map/ppermute | solution.py:56
  700.6 26.4 %collective-permute-start.67 = (bf16[1408,256]{1,0:T(8,128)(2,1)S(1)}, bf16[1408,256]{1,0:T(8,128)(2,1)S(1)}, u32[]{:S(2)}, u32[]{:S(2)}) collective-permute-start(bf16[1408,256]{1,0:T(8,128)(2,1)S(1)} %copy-done.47), channel_id=1, source_target_pairs={{0,4},{2,6},{4,0},{6,2},{1,5},{3,7},{5,1},{7,3},{8,12},{10,14},{12... | collective-permute-start | bytes 2162696 | tf_op jit(solution)/shard_map/ppermute | solution.py:56
  711.6 30.9 %collective-permute-start.61 = (bf16[256,1408]{1,0:T(8,128)(2,1)S(1)}, bf16[256,1408]{1,0:T(8,128)(2,1)S(1)}, u32[]{:S(2)}, u32[]{:S(2)}) collective-permute-start(bf16[256,1408]{1,0:T(8,128)(2,1)S(1)} %copy-done.48), channel_id=1, source_target_pairs={{0,4},{2,6},{4,0},{6,2},{1,5},{3,7},{5,1},{7,3},{8,12},{10,14},{12... | collective-permute-start | bytes 2162696 | tf_op jit(solution)/shard_map/ppermute | solution.py:56
  714.6 42.6 %collective-permute-start.64 = (bf16[256,1408]{1,0:T(8,128)(2,1)}, bf16[256,1408]{1,0:T(8,128)(2,1)}, u32[]{:S(2)}, u32[]{:S(2)}) collective-permute-start(bf16[256,1408]{1,0:T(8,128)(2,1)} %add_convert_fusion.1), channel_id=1, source_target_pairs={{0,4},{2,6},{4,0},{6,2},{1,5},{3,7},{5,1},{7,3},{8,12},{10,14},{12... | collective-permute-start | bytes 2162696 | tf_op jit(solution)/shard_map/ppermute | solution.py:56
  727.0 23.4 %collective-permute-start.48 = (bf16[512,1024]{1,0:T(8,128)(2,1)S(1)}, bf16[512,1024]{1,0:T(8,128)(2,1)S(1)}, u32[]{:S(2)}, u32[]{:S(2)}) collective-permute-start(bf16[512,1024]{1,0:T(8,128)(2,1)S(1)} %fusion.50), channel_id=1, source_target_pairs={{0,1},{1,0},{2,3},{3,2},{4,5},{5,4},{6,7},{7,6},{8,9},{9,8},{10,11... | collective-permute-start | bytes 3145736 | tf_op jit(solution)/shard_map/ppermute | solution.py:56
  766.0 27.3 %collective-permute-start.51 = (bf16[4,64,2176]{2,1,0:T(8,128)(2,1)}, bf16[4,64,2176]{2,1,0:T(8,128)(2,1)}, u32[]{:S(2)}, u32[]{:S(2)}) collective-permute-start(bf16[4,64,2176]{2,1,0:T(8,128)(2,1)} %fusion.20), channel_id=1, source_target_pairs={{0,4},{2,6},{4,0},{6,2},{1,5},{3,7},{5,1},{7,3},{8,12},{10,14},{12... | collective-permute-start | bytes 3342344 | tf_op jit(solution)/shard_map/ppermute | solution.py:56
  810.8 15.8 %collective-permute-start.52 = (bf16[64,2176]{1,0:T(8,128)(2,1)}, bf16[64,2176]{1,0:T(8,128)(2,1)}, u32[]{:S(2)}, u32[]{:S(2)}) collective-permute-start(bf16[64,2176]{1,0:T(8,128)(2,1)} %bitcast.195), channel_id=1, source_target_pairs={{0,8},{8,0},{16,24},{24,16},{1,9},{9,1},{17,25},{25,17},{2,10},{10... | collective-permute-start | bytes 835592 | tf_op jit(solution)/shard_map/ppermute | solution.py:56
  (128 other events, 1671.2 us)
where the time goes:
time: 853 us; the launch traced here: 845 us
  waiting for transfers between devices  291 us (34%)
  Pallas kernels  287 us (34%)
  starting transfers between devices  75.7 us (9%)
  other arithmetic  75.3 us (9%)
  local copies, waits for them, and re-layouts  65 us (8%)
  matrix products  48.9 us (6%)
    ppermute x68, waiting for transfers between devices, swap(): return lax.ppermute(values, axis, [(i, i ^ bits) for i in range(count)])  291 us
    pallas_call x2, Pallas kernels, assemble(): pl.pallas_call(assemble_kernel, out_shape=jax.ShapeDtypeStruct((count * r...  171 us
    ppermute x68, starting transfers between devices, swap(): return lax.ppermute(values, axis, [(i, i ^ bits) for i in range(count)])  75.7 us
    pallas_call x4, Pallas kernels, expert_block(): pl.pallas_call(functools.partial(expert_kernel, experts, count, shares),...  51.6 us
    pallas_call x1, Pallas kernels, attention_back(): pl.pallas_call(attention_back_kernel, grid=(pairs,), in_specs=[specs['sme...  39.4 us
    pallas_call x1, Pallas kernels, attention(): pl.pallas_call(attention_kernel, grid=(pairs,), in_specs=[specs['smem'],...  24.9 us
    dot_general x5, matrix products, weight_grad(): lax.dot_general(left, right, (((0,), (0,)), ((), ())), preferred_element_...  21.5 us
    unnamed x233, local copies, waits for them, and re-layouts  20.4 us
  transfers between devices with their start and end apart: 68, of which 29 were waited for; matrix products, arithmetic and copies ran while one was open for 18% of the time, Pallas kernels for 32%

commit v1 on v0

--- a/solution.py
+++ b/solution.py
@@ -97,29 +97,62 @@
     return jnp.concatenate(pieces, axis=dim)
 
 
-def assemble_kernel(place_ref, *refs):
-    pieces, whole, sems = refs[:-2], refs[-2], refs[-1]
-    rows = pieces[0].shape[0]
-    copies = []
-    for m, piece in enumerate(pieces):
-        start = pl.multiple_of((place_ref[0] ^ m) * rows, rows)
-        copies.append(pltpu.make_async_copy(piece, whole.at[pl.ds(start, rows)], sems.at[m]))
-    for copy in copies:
+MESH = pl.DeviceIdType.MESH
+
+
+class Wire:
+    def __init__(self, sends, receives):
+        self.sends, self.receives, self.count, self.copies = sends, receives, 0, []
+
+    def send(self, source, target, **device):
+        copy = pltpu.make_async_remote_copy(
+            src_ref=source,
+            dst_ref=target,
+            send_sem=self.sends.at[self.count],
+            recv_sem=self.receives.at[self.count],
+            device_id=device,
+            device_id_type=MESH,
+        )
         copy.start()
-    for copy in copies:
-        copy.wait()
-
-
-def assemble(pieces, place):
-    count, rows = len(pieces), pieces[0].shape[0]
-    return pl.pallas_call(
-        assemble_kernel,
-        out_shape=jax.ShapeDtypeStruct((count * rows,) + pieces[0].shape[1:], pieces[0].dtype),
-        in_specs=[pl.BlockSpec(memory_space=pltpu.SMEM)]
-        + [pl.BlockSpec(memory_space=pl.ANY)] * count,
-        out_specs=pl.BlockSpec(memory_space=pl.ANY),
-        scratch_shapes=[pltpu.SemaphoreType.DMA((count,))],
-    )(place.reshape(1), *pieces)
+        self.count += 1
+        self.copies.append(copy)
+        return Arrival(copy)
+
+    def finish(self):
+        for copy in self.copies:
+            copy.wait_send()
+
+
+class Arrival:
+    def __init__(self, copy):
+        self.copy, self.waited = copy, False
+
+    def wait(self):
+        if not self.waited:
+            self.copy.wait_recv()
+        self.waited = True
+
+
+def greet(partners):
+    barrier = pltpu.get_barrier_semaphore()
+    for device in partners:
+        pl.semaphore_signal(barrier, inc=1, device_id=device, device_id_type=MESH)
+    pl.semaphore_wait(barrier, len(partners))
+
+
+def bits_down(count):
+    bits, bit = [], count >> 1
+    while bit:
+        bits.append(bit)
+        bit >>= 1
+    return bits
+
+
+def xor_order(count):
+    order = [0]
+    for bit in bits_down(count):
+        order = order + [k | bit for k in order]
+    return order
 
 
 NT = (((1,), (1,)), ((), ()))
@@ -387,10 +420,263 @@
     )(active, base, queries, key_values, key_values, grads, totals, window, doc_row, doc_col)
 
 
+def start_kernel(
+    experts, dp_count, ctx_count, pack_ref, hidden_ref, docs_ref,
+    query_ref, pair_ref, normed_ref, weight_out, own_ref, lanes_ref, gains_ref, docs_out,
+    weights, hidden, docs, sends, receives, out_sem,
+):
+    d, c = lax.axis_index("dp"), lax.axis_index("ctx")
+    rows = pack_ref.shape[0]
+    tokens, width = query_ref.shape
+    greet(
+        [{"ctx": c ^ m} for m in range(1, ctx_count)]
+        + [{"dp": d ^ bit} for bit in bits_down(dp_count)]
+    )
+    wire = Wire(sends, receives)
+
+    def shard(m, j):
+        index = (d ^ m) * ctx_count + (c ^ j)
+        return weights.at[pl.ds(pl.multiple_of(index * rows, rows), rows)]
+
+    weights[pl.ds(pl.multiple_of((d * ctx_count + c) * rows, rows), rows), :] = pack_ref[...]
+    docs_sent = [wire.send(docs_ref, docs.at[m], ctx=c ^ m) for m in range(1, ctx_count)]
+    sides = [0]
+    hidden_sent = {}
+    for bit in bits_down(ctx_count)[:-1]:
+        arrivals = [wire.send(shard(0, j), shard(0, j), ctx=c ^ bit) for j in sides]
+        for m in [0] + list(hidden_sent):
+            source = hidden_ref if m == 0 else hidden.at[m]
+            if m:
+                hidden_sent[m].wait()
+            hidden_sent[m | bit] = wire.send(source, hidden.at[m | bit], ctx=c ^ bit)
+        for copy in arrivals:
+            copy.wait()
+        sides = sides + [j | bit for j in sides]
+    hidden_sent[1] = wire.send(hidden_ref, hidden.at[1], ctx=c ^ 1)
+    groups, crossed = {}, []
+    for m in xor_order(dp_count):
+        if m:
+            for copy in groups[m]:
+                copy.wait()
+        for bit in bits_down(dp_count):
+            if m & (2 * bit - 1) == 0:
+                groups[m | bit] = [
+                    wire.send(shard(m, j), shard(m, j), dp=d ^ bit) for j in sides
+                ]
+        crossed += [wire.send(shard(m, j), shard(m, j), ctx=c ^ 1) for j in sides]
+        if m == 0:
+            for k in [k for k in hidden_sent if k > 1]:
+                hidden_sent[k].wait()
+                hidden_sent[k | 1] = wire.send(hidden.at[k], hidden.at[k | 1], ctx=c ^ 1)
+    for copy in crossed:
+        copy.wait()
+    keep = pltpu.make_async_copy(weights.at[:, : 3 * width], weight_out, out_sem.at[0])
+    keep.start()
+    keep_own = pltpu.make_async_copy(weights.at[:, 3 * width + LANES :], own_ref, out_sem.at[1])
+    keep_own.start()
+    small = weights[:, 3 * width : 3 * width + LANES].astype(F32)
+    lane = lax.broadcasted_iota(jnp.int32, small.shape, 1)
+    lanes_ref[...] = jnp.where(lane < experts, small, 0.0).astype(BF16)
+    gain_one = jnp.sum(jnp.where(lane == experts, small, 0.0), axis=1, keepdims=True)
+    gain_two = jnp.sum(jnp.where(lane == experts + 1, small, 0.0), axis=1, keepdims=True)
+    both = jnp.where(lane == 0, gain_one, jnp.where(lane == 1, gain_two, 0.0)).T
+    gains_ref[...] = both[:8]
+    gain = both[0:1]
+    docs_out[0] = docs_ref[...]
+    for m in range(ctx_count):
+        if m:
+            docs_sent[m - 1].wait()
+            docs_out[m] = docs[m]
+            hidden_sent[m].wait()
+        values = (hidden[m] if m else hidden_ref[...]).astype(F32)
+        scale = lax.rsqrt(jnp.mean(values * values, axis=-1, keepdims=True) + NORM_EPS)
+        normed = (values * scale * gain).astype(BF16)
+        pair_ref[m * tokens : (m + 1) * tokens, :] = mm(
+            normed, weights[:, width : 3 * width]
+        ).astype(BF16)
+        if m == 0:
+            normed_ref[...] = normed
+            query_ref[...] = mm(normed, weights[:, :width]).astype(BF16)
+    keep.wait()
+    keep_own.wait()
+    wire.finish()
+
+
+def start(pack, hidden, docs, width, experts):
+    tokens = hidden.shape[0]
+    columns = pack.shape[1]
+    dp_count, ctx_count = lax.axis_size("dp"), lax.axis_size("ctx")
+    copies = 2 * (ctx_count - 1) + ctx_count // 2 + dp_count * ctx_count
+    vmem = pl.BlockSpec(memory_space=pltpu.VMEM)
+    hbm = pl.BlockSpec(memory_space=pl.ANY)
+    return pl.pallas_call(
+        functools.partial(start_kernel, experts, dp_count, ctx_count),
+        in_specs=[vmem] * 3,
+        out_specs=[vmem, vmem, vmem, hbm, hbm, vmem, vmem, vmem],
+        out_shape=[
+            jax.ShapeDtypeStruct((tokens, width), BF16),
+            jax.ShapeDtypeStruct((tokens * ctx_count, 2 * width), BF16),
+            jax.ShapeDtypeStruct((tokens, D), BF16),
+            jax.ShapeDtypeStruct((D, 3 * width), BF16),
+            jax.ShapeDtypeStruct((D, width), BF16),
+            jax.ShapeDtypeStruct((D, LANES), BF16),
+            jax.ShapeDtypeStruct((8, D), F32),
+            jax.ShapeDtypeStruct((ctx_count, 8, tokens), jnp.int32),
+        ],
+        scratch_shapes=[
+            pltpu.VMEM((D, columns), BF16),
+            pltpu.VMEM((ctx_count, tokens, D), BF16),
+            pltpu.VMEM((ctx_count, 8, tokens), jnp.int32),
+            pltpu.SemaphoreType.DMA((copies,)),
+            pltpu.SemaphoreType.DMA((copies,)),
+            pltpu.SemaphoreType.DMA((2,)),
+        ],
+        compiler_params=pltpu.CompilerParams(
+            vmem_limit_bytes=VMEM_CAP, collective_id=1, has_side_effects=True
+        ),
+        name="start",
+    )(pack, hidden, docs)
+
+
+def middle_kernel(shares, place_ref, *refs):
+    attended, outs = refs[:shares], refs[shares : 2 * shares]
+    (hidden_ref, gains_ref, lanes_ref, picker_ref,
+     middle_ref, normed_ref, probs_ref, send_ref, weights, mixed) = refs[2 * shares :]
+    share, experts = place_ref[2], place_ref[3]
+    width = attended[0].shape[1]
+    for m in range(shares):
+        part = pl.ds(pl.multiple_of((share ^ m) * width, width), width)
+        mixed[:, part] = attended[m][...]
+        weights[:, part] = outs[m][...]
+    middle = hidden_ref[...].astype(F32) + mm(mixed[...], weights[...], NT)
+    middle_ref[...] = middle
+    scale = lax.rsqrt(jnp.mean(middle * middle, axis=-1, keepdims=True) + NORM_EPS)
+    normed = (middle * scale * gains_ref[1:2, :]).astype(BF16)
+    normed_ref[...] = normed
+    logits = mm(normed, lanes_ref[...])
+    lane = lax.broadcasted_iota(jnp.int32, logits.shape, 1)
+    logits = jnp.where(lane < experts, logits, NEG_FILL)
+    powers = jnp.exp(logits - jnp.max(logits, axis=1, keepdims=True))
+    probs_ref[...] = powers / jnp.sum(powers, axis=1, keepdims=True)
+    slots = send_ref.shape[1]
+    for m in range(send_ref.shape[0]):
+        send_ref[m] = mm(picker_ref[m * slots : (m + 1) * slots, :], normed).astype(BF16)
+
+
+def middle_step(places, attended, outs, hidden, gains, lanes, picker, blocks):
+    shares, (tokens, width) = len(attended), attended[0].shape
+    vmem = pl.BlockSpec(memory_space=pltpu.VMEM)
+    return pl.pallas_call(
+        functools.partial(middle_kernel, shares),
+        in_specs=[pl.BlockSpec(memory_space=pltpu.SMEM)] + [vmem] * (2 * shares + 4),
+        out_specs=[vmem] * 4,
+        out_shape=[
+            jax.ShapeDtypeStruct((tokens, D), F32),
+            jax.ShapeDtypeStruct((tokens, D), BF16),
+            jax.ShapeDtypeStruct((tokens, LANES), F32),
+            jax.ShapeDtypeStruct((blocks, picker.shape[0] // blocks, D), BF16),
+        ],
+        scratch_shapes=[
+            pltpu.VMEM((D, width * shares), BF16),
+            pltpu.VMEM((tokens, width * shares), BF16),
+        ],
+        compiler_params=pltpu.CompilerParams(vmem_limit_bytes=VMEM_CAP),
+        name="middle_step",
+    )(places, *attended, *outs, hidden, gains, lanes, picker)
+
+
+def return_kernel(shares, place_ref, *refs):
+    parts = refs[:-6]
+    picker_ref, probs_ref, lanes_ref, grad_ref, logit_ref, back = refs[-6:]
+    share, experts = place_ref[2], place_ref[3]
+    slots = parts[0].shape[0]
+    width = grad_ref.shape[1]
+    for m, part in enumerate(parts):
+        back[m * slots : (m + 1) * slots, :] = part[...]
+    returned = mm(picker_ref[...], back[...])
+    tail = returned[:, width:]
+    lane = lax.broadcasted_iota(jnp.int32, tail.shape, 1)
+    step = LANES // (2 * shares)
+    prob_grad = tail
+    for k in range(1, 2 * shares):
+        prob_grad = prob_grad + pltpu.roll(tail, LANES - k * step, 1)
+    probs = probs_ref[...]
+    prob_grad = jnp.where(lane < experts, prob_grad, 0.0)
+    logit = probs * (prob_grad - jnp.sum(probs * prob_grad, axis=1, keepdims=True))
+    logit_ref[...] = logit
+    lanes = lanes_ref[pl.ds(pl.multiple_of(share * width, width), width), :]
+    more = lax.dot_general(
+        logit, lanes.astype(F32), NT, precision=lax.Precision.HIGHEST, preferred_element_type=F32
+    )
+    grad_ref[...] = (returned[:, :width] + more).astype(BF16)
+
+
+def return_step(places, parts, picker_flip, probs, lanes, shares):
+    tokens = picker_flip.shape[0]
+    slots, columns = parts[0].shape
+    vmem = pl.BlockSpec(memory_space=pltpu.VMEM)
+    return pl.pallas_call(
+        functools.partial(return_kernel, shares),
+        in_specs=[pl.BlockSpec(memory_space=pltpu.SMEM)] + [vmem] * (len(parts) + 3),
+        out_specs=[vmem] * 2,
+        out_shape=[
+            jax.ShapeDtypeStruct((tokens, columns - LANES), BF16),
+            jax.ShapeDtypeStruct((tokens, LANES), F32),
+        ],
+        scratch_shapes=[pltpu.VMEM((slots * len(parts), columns), BF16)],
+        compiler_params=pltpu.CompilerParams(vmem_limit_bytes=VMEM_CAP),
+        name="return_step",
+    )(places, *parts, picker_flip, probs, lanes)
+
+
+def middle_back_kernel(shares, place_ref, *refs):
+    halves = refs[:shares]
+    (middle_ref, out_grad_ref, gains_ref, own_ref,
+     grad_ref, low_ref, attended_ref, gain_ref, whole) = refs[shares:]
+    share = place_ref[2]
+    width = halves[0].shape[1]
+    for m in range(shares):
+        first = pl.multiple_of((share ^ m) * width, width)
+        whole[:, pl.ds(first, width)] = halves[m][...]
+    middle = middle_ref[...]
+    gradient = whole[...].astype(F32)
+    scale = lax.rsqrt(jnp.mean(middle * middle, axis=-1, keepdims=True) + NORM_EPS)
+    weighted = gains_ref[1:2, :] * gradient
+    inner = jnp.mean(middle * weighted, axis=-1, keepdims=True)
+    part = scale * weighted - middle * (scale * scale * scale) * inner
+    gain_ref[...] = fold_sum(gradient * middle * scale)
+    total = out_grad_ref[...].astype(F32) + part
+    grad_ref[...] = total
+    low = total.astype(BF16)
+    low_ref[...] = low
+    attended_ref[...] = mm(low, own_ref[...]).astype(BF16)
+
+
+def middle_back(places, halves, middle, out_grad, gains, own):
+    shares, tokens = len(halves), middle.shape[0]
+    vmem = pl.BlockSpec(memory_space=pltpu.VMEM)
+    return pl.pallas_call(
+        functools.partial(middle_back_kernel, shares),
+        in_specs=[pl.BlockSpec(memory_space=pltpu.SMEM)] + [vmem] * (shares + 4),
+        out_specs=[vmem] * 4,
+        out_shape=[
+            jax.ShapeDtypeStruct((tokens, D), F32),
+            jax.ShapeDtypeStruct((tokens, D), BF16),
+            jax.ShapeDtypeStruct((tokens, own.shape[1]), BF16),
+            jax.ShapeDtypeStruct((8, D), F32),
+        ],
+        scratch_shapes=[pltpu.VMEM((tokens, D), BF16)],
+        compiler_params=pltpu.CompilerParams(vmem_limit_bytes=VMEM_CAP),
+        name="middle_back",
+    )(places, *halves, middle, out_grad, gains, own)
+
+
 def expert_kernel(experts, count, shares, place_ref, rows_ref, grads_ref, router_ref, *refs):
     ins, downs = refs[:count], refs[count : 2 * count]
-    (rows_all, scaled_all, act_ref, gate_low_ref, up_low_ref, row_part, out_part,
-     in_all, down_all, sems) = refs[-10:]
+    in_all, down_all, sems = refs[-3:]
+    results = refs[-3 - 5 - 2 * shares : -3]
+    rows_all, scaled_all, act_ref, gate_low_ref, up_low_ref = results[:5]
+    row_parts, out_parts = results[5 : 5 + shares], results[5 + shares :]
     expert, ctx, share = place_ref[0], place_ref[1], place_ref[2]
     depth = ins[0].shape[1]
     ff = ins[0].shape[2]
@@ -438,21 +724,20 @@
         gate_low_ref[:, part] = (scaled * up * slope).astype(BF16)
         up_low_ref[:, part] = (scaled * bent).astype(BF16)
     share_width = D // shares
-    for j in range(count):
-        part = slice(j * depth, (j + 1) * depth)
-        first = (ctx ^ j) * depth
-        owner = (first // share_width) ^ share
-        spot = pl.ds(pl.multiple_of(first % share_width, depth), depth)
-        row = mm(gate_low_ref[...], in_all[0, part, :], NT)
-        row += mm(up_low_ref[...], in_all[1, part, :], NT)
-        row_part[owner, :, spot] = row.astype(BF16)
-        out_part[owner, :, spot] = (gate * mm(act_ref[...], down_all[:, part])).astype(BF16)
     high = dots.astype(BF16).astype(F32)
     stride = LANES // shares
     tail = jnp.where(lane == share * stride + expert, high, 0.0)
     tail = jnp.where(lane == share * stride + stride // 2 + expert, dots - high, tail)
     for m in range(shares):
-        row_part[m, :, share_width:] = tail.astype(BF16)
+        for i in range(share_width // depth):
+            piece = ((share ^ m) * (share_width // depth) + i) ^ ctx
+            part = pl.ds(pl.multiple_of(piece * depth, depth), depth)
+            spot = slice(i * depth, (i + 1) * depth)
+            row = mm(gate_low_ref[...], in_all[0, part, :], NT)
+            row += mm(up_low_ref[...], in_all[1, part, :], NT)
+            row_parts[m][:, spot] = row.astype(BF16)
+            out_parts[m][:, spot] = (gate * mm(act_ref[...], down_all[:, part])).astype(BF16)
+        row_parts[m][:, share_width:] = tail.astype(BF16)
 
 
 def expert_block(block, blocks, places, rows, grads, router, ins, downs, held, experts, shares):
@@ -471,12 +756,10 @@
         in_specs=[pl.BlockSpec(memory_space=pltpu.SMEM)]
         + [vmem] * 3
         + [hbm] * (2 * count + len(held)),
-        out_specs=[pl.BlockSpec((slots, size), at_block) for size in sizes] + [vmem] * 2,
+        out_specs=[pl.BlockSpec((slots, size), at_block) for size in sizes] + [vmem] * (2 * shares),
         out_shape=[jax.ShapeDtypeStruct((blocks * slots, size), BF16) for size in sizes]
-        + [
-            jax.ShapeDtypeStruct((shares, slots, share_width + LANES), BF16),
-            jax.ShapeDtypeStruct((shares, slots, share_width), BF16),
-        ],
+        + [jax.ShapeDtypeStruct((slots, share_width + LANES), BF16)] * shares
+        + [jax.ShapeDtypeStruct((slots, share_width), BF16)] * shares,
         scratch_shapes=[
             pltpu.VMEM((2, width, ff), BF16),
             pltpu.VMEM((ff, width), BF16),
@@ -526,24 +809,22 @@
     expert_count = router.shape[1]
     top_count = routes.shape[1]
     own_rows = router.shape[0]
-    share_width = D // tp_count
-
+
+    places = jnp.stack(
+        [dp_place, ctx_place, tp_place, jnp.int32(expert_count)]
+    ).astype(jnp.int32)
     tail_pack = jnp.pad(
         jnp.concatenate([router, norm_gains.T], axis=1), ((0, 0), (0, LANES - expert_count - 2))
     )
     pack = jnp.concatenate(
-        [qkv_weight.reshape(own_rows, 3 * width_here), out_weight.T, tail_pack], axis=1
-    )
-    hidden_pieces = gather_xor(hidden_in, "ctx")
-    ctx_pack = assemble(gather_xor(pack, "ctx"), ctx_place)
-    full_pack = assemble(gather_xor(ctx_pack, "dp"), dp_place)
-    docs_pieces = gather_xor(segments.reshape(1, -1), "ctx")
-    qkv_flat = full_pack[:, : 3 * width_here]
-    out_flip = full_pack[:, 3 * width_here : 4 * width_here]
-    small = full_pack[:, 4 * width_here :]
-    router_full = small[:, :expert_count]
-    gain_values = small[:, expert_count : expert_count + 2].T.astype(F32)
-    out_all = in_order(gather_xor(out_flip, "tp"), tp_place, 1)
+        [qkv_weight.reshape(own_rows, 3 * width_here), tail_pack, out_weight.T], axis=1
+    )
+    doc_row = jnp.broadcast_to(segments.reshape(1, tokens), (8, tokens))
+    queries, key_values, normed_one, qkv_flat, out_own, lanes, gains, docs = start(
+        pack, hidden_in, doc_row, width_here, expert_count
+    )
+    out_sides = gather_xor(out_own, "tp")
+    docs_all = docs[:, 0].reshape(length)
 
     capacity = max(2, min(tokens, 5 * top_count * tokens // (4 * expert_count)))
     flat_routes = routes.reshape(-1)
@@ -560,13 +841,21 @@
             (routes[:, k][None, None, :] == slot_expert[:, None, None])
             & (position[:, k][None, None, :] == slot_index[None, :, None])
         )
-    picker = chosen.astype(BF16)
-    send_grads = jnp.einsum(
-        "mct,td->mcd", picker, out_grad, preferred_element_type=F32
-    ).astype(BF16)
+    picker = chosen.astype(BF16).reshape(dp_count * capacity, tokens)
+    chosen_flip = jnp.zeros((tokens, dp_count, capacity), jnp.bool_)
+    for k in range(top_count):
+        chosen_flip = chosen_flip | (
+            (routes[:, k][:, None, None] == slot_expert[None, :, None])
+            & (position[:, k][:, None, None] == slot_index[None, None, :])
+        )
+    picker_flip = chosen_flip.astype(BF16).reshape(tokens, dp_count * capacity)
+    send_grads = mm(picker, out_grad).astype(BF16).reshape(dp_count, capacity, D)
+    send_grads, expert_in_late, expert_down_late, _, _ = lax.optimization_barrier(
+        (send_grads, expert_in[0], expert_down[0], queries, out_own)
+    )
     arrived_grads = [send_grads[0]] + [swap(send_grads[m], "dp", m) for m in range(1, dp_count)]
-    in_pieces = gather_xor(expert_in[0], "ctx")
-    down_pieces = gather_xor(expert_down[0], "ctx")
+    in_pieces = gather_xor(expert_in_late, "ctx")
+    down_pieces = gather_xor(expert_down_late, "ctx")
 
     rev_table = bucket_table[::-1]
     window_width = tokens + length
@@ -581,9 +870,7 @@
     )
     window = jnp.pad(window.reshape(pairs, 2, window_width), ((0, 0), (0, 6), (0, 0)))
     docs_row = segments.reshape(1, tokens)
-    docs_all = jnp.concatenate(docs_pieces, axis=1).reshape(length)
     doc_col = jnp.broadcast_to(docs_all[:, None], (length, LANES))
-    doc_row = jnp.broadcast_to(docs_row, (8, tokens))
     query_docs = docs_row.reshape(tokens // BLOCK, BLOCK)
     key_docs = docs_all.reshape(length // BLOCK, BLOCK)
     active = (
@@ -596,47 +883,24 @@
     ).reshape(-1)
     base = (length - LANES - block_rows).astype(jnp.int32)
 
-    hidden_all = jnp.concatenate(hidden_pieces, axis=0)
-    inputs = hidden_in.astype(F32)
-    scale_one = rms_scale(inputs)
-    normed_one = (inputs * scale_one * gain_values[0]).astype(BF16)
-    inputs_all = hidden_all.astype(F32)
-    normed_all = (inputs_all * rms_scale(inputs_all) * gain_values[0]).astype(BF16)
-    queries = jnp.dot(
-        normed_one, qkv_flat[:, :width_here], preferred_element_type=F32
-    ).astype(BF16)
-    key_values = jnp.dot(
-        normed_all, qkv_flat[:, width_here:], preferred_element_type=F32
-    ).astype(BF16)
-
     attended, totals = attention(active, base, queries, key_values, window, doc_row, doc_col)
-    attended_all = in_order(gather_xor(attended, "tp"), tp_place, 1)
-    middle = inputs + mm(attended_all, out_all, NT)
-    scale_two = rms_scale(middle)
-    normed_two = (middle * scale_two * gain_values[1]).astype(BF16)
-    router_probs = jax.nn.softmax(
-        jnp.dot(normed_two, router_full, preferred_element_type=F32), axis=-1
-    )
-    send_rows = jnp.einsum(
-        "mct,td->mcd", picker, normed_two, preferred_element_type=F32
-    ).astype(BF16)
+    middle, normed_two, probs, send_rows = middle_step(
+        places, gather_xor(attended, "tp"), out_sides, hidden_in, gains, lanes, picker, dp_count
+    )
     arrived_rows = [send_rows[0]] + [swap(send_rows[m], "dp", m) for m in range(1, dp_count)]
 
-    router_lanes = jnp.where(
-        jnp.arange(LANES)[None, :] < expert_count, small, jnp.zeros_like(small)
-    )
-    places = jnp.stack([dp_place, ctx_place, tp_place]).astype(jnp.int32)
     held = ()
-    back_rows, back_outs = [], []
+    row_sums, out_parts = [], []
     for m in range(dp_count):
-        *held, row_part, out_part = expert_block(
-            m, dp_count, places, arrived_rows[m], arrived_grads[m], router_lanes,
+        results = expert_block(
+            m, dp_count, places, arrived_rows[m], arrived_grads[m], lanes,
             in_pieces, down_pieces, held, expert_count, tp_count,
         )
-        row_sum = scatter_sum([row_part[k] for k in range(tp_count)], "tp").astype(BF16)
-        out_sum = scatter_sum([out_part[k] for k in range(tp_count)], "tp").astype(BF16)
-        back_rows.append(swap(row_sum, "dp", m) if m else row_sum)
-        back_outs.append(swap(out_sum, "dp", m) if m else out_sum)
+        held = results[:5]
+        row_sums.append(scatter_sum(results[5 : 5 + tp_count], "tp").astype(BF16))
+        out_parts.append(results[5 + tp_count :])
+    back_rows = row_sums[:1] + [swap(row_sums[m], "dp", m) for m in range(1, dp_count)]
+    held, _ = lax.optimization_barrier((held, row_sums))
     rows_all, scaled_all, act_all, gate_low_all, up_low_all = held
 
     def rows_by_ctx(values):
@@ -663,39 +927,23 @@
     down_total = scatter_sum(columns_by_ctx(weight_grad(act_all, scaled_all)), "ctx")[None]
     in_total = jnp.stack([gate_total, up_total], axis=0)[None]
 
-    def to_tokens(parts):
-        whole = jnp.concatenate(parts, axis=0)
-        flat = picker.reshape(dp_count * capacity, tokens)
-        return lax.dot_general(flat, whole, (((0,), (0,)), ((), ())), preferred_element_type=F32)
-
-    mixed_half = to_tokens(back_outs).astype(BF16)
+    grad_half, logit_grad = return_step(places, back_rows, picker_flip, probs, lanes, tp_count)
+    middle_grad, middle_low, attended_grad, gain_two_grad = middle_back(
+        places, gather_xor(grad_half, "tp"), middle, out_grad, gains, out_own
+    )
+    out_parts, _ = lax.optimization_barrier((out_parts, middle_grad))
+    out_sums = [scatter_sum(parts, "tp").astype(BF16) for parts in out_parts]
+    back_outs = out_sums[:1] + [swap(out_sums[m], "dp", m) for m in range(1, dp_count)]
+    mixed_half = mm(picker_flip, jnp.concatenate(back_outs, axis=0)).astype(BF16)
     mixed = in_order(gather_xor(mixed_half, "tp"), tp_place, 1)
     output = middle + mixed.astype(F32)
-
-    returned = to_tokens(back_rows)
-    prob_grad = jnp.sum(
-        returned[:, share_width:].reshape(tokens, 2 * tp_count, LANES // (2 * tp_count)), axis=1
+    out_flip_grad = weight_grad(middle_low, attended)
+    router_grad = lax.dot_general(
+        normed_two.astype(F32), logit_grad, (((0,), (0,)), ((), ())),
+        precision=lax.Precision.HIGHEST, preferred_element_type=F32,
     )[:, :expert_count]
-    logit_grad = router_probs * (
-        prob_grad - jnp.sum(router_probs * prob_grad, axis=-1, keepdims=True)
-    )
-    router_share = lax.dynamic_slice_in_dim(router_full, tp_place * share_width, share_width, 0)
-    grad_half = returned[:, :share_width] + jnp.dot(
-        logit_grad, router_share.T.astype(F32), precision=lax.Precision.HIGHEST,
-        preferred_element_type=F32,
-    )
-    normed_two_grad = in_order(
-        gather_xor(grad_half.astype(BF16), "tp"), tp_place, 1
-    ).astype(F32)
-    middle_part, gain_two_grad = norm_back(middle, scale_two, gain_values[1], normed_two_grad)
-    middle_grad = out_grad.astype(F32) + middle_part
-    middle_low = middle_grad.astype(BF16)
-    attended_grad = jnp.dot(middle_low, out_flip, preferred_element_type=F32).astype(BF16)
-    out_flip_grad = weight_grad(middle_low, attended)
-    router_grad = jnp.dot(
-        normed_two.T.astype(F32), logit_grad, precision=lax.Precision.HIGHEST,
-        preferred_element_type=F32,
-    )
+    inputs = hidden_in.astype(F32)
+    scale_one = rms_scale(inputs)
 
     query_grad, key_part, value_part, offset_grad = attention_back(
         active, base, queries, key_values, attended_grad, totals, window, doc_row, doc_col
@@ -713,13 +961,13 @@
     value_total = scatter_sum(row_blocks(value_part), "ctx").astype(BF16)
     qkv_rows_grad = jnp.concatenate([query_grad, key_total, value_total], axis=1)
     normed_one_grad = all_sum(mm(qkv_rows_grad, qkv_flat, NT).astype(BF16), "tp").astype(F32)
-    input_part, gain_one_grad = norm_back(inputs, scale_one, gain_values[0], normed_one_grad)
+    input_part, gain_one_grad = norm_back(inputs, scale_one, gains[0], normed_one_grad)
     input_grad = middle_grad + input_part
     qkv_weight_grad = weight_grad(normed_one, qkv_rows_grad)
 
     tail_grad = jnp.pad(
         jnp.concatenate(
-            [router_grad, jnp.stack([gain_one_grad, gain_two_grad], axis=1)], axis=1
+            [router_grad, jnp.stack([gain_one_grad, jnp.sum(gain_two_grad, axis=0)], axis=1)], axis=1
         ),
         ((0, 0), (0, LANES - expert_count - 2)),
     ).astype(BF16)

time: 853 us -> 647 us (0.76)
  waiting for transfers between devices: 291 us -> 156 us
  Pallas kernels: 287 us -> 189 us
  starting transfers between devices: 75.7 us -> 113 us
  matrix products: 48.9 us -> 30.7 us
  local copies, waits for them, and re-layouts: 65 us -> 75.6 us
    ppermute x68 -> x56, waiting for transfers between devices: 291 us -> 156 us  [swap(): return lax.ppermute(values, axis, [(i, i ^ bits) for i in range(count)])]
    pallas_call x2 -> x4, Pallas kernels: 171 us -> 80.7 us  [the longest x1 62.1 us: start(): pl.pallas_call(functools.partial(start_kernel, experts, dp_count, ctx_cou...]
    ppermute x68 -> x56, starting transfers between devices: 75.7 us -> 113 us  [swap(): return lax.ppermute(values, axis, [(i, i ^ bits) for i in range(count)])]
    dot_general x10 -> x1, matrix products: 23.7 us -> 1.6 us  [shards(): lax.dot_general(normed_two.astype(F32), logit_grad, (((0,), (0,)), ((), (...]
    unnamed x233 -> x191, local copies, waits for them, and re-layouts: 20.4 us -> 23.6 us
  transfers between devices with their start and end apart: 68 -> 56, of which waited for: 29 -> 22; matrix products, arithmetic and copies ran while one was open for 18% -> 23% of each run, Pallas kernels for 32% -> 18%
where the time goes in v1:
time: 647 us; the launch traced here: 639 us
  Pallas kernels  189 us (29%)
  waiting for transfers between devices  156 us (24%)
  starting transfers between devices  113 us (17%)
  local copies, waits for them, and re-layouts  75.6 us (12%)
  other arithmetic  73.1 us (11%)
  matrix products  30.7 us (5%)
    ppermute x56, waiting for transfers between devices, swap(): return lax.ppermute(values, axis, [(i, i ^ bits) for i in range(count)])  156 us
    ppermute x56, starting transfers between devices, swap(): return lax.ppermute(values, axis, [(i, i ^ bits) for i in range(count)])  113 us
    pallas_call x1, Pallas kernels, start(): pl.pallas_call(functools.partial(start_kernel, experts, dp_count, ctx_cou...  62.1 us
    pallas_call x4, Pallas kernels, expert_block(): pl.pallas_call(functools.partial(expert_kernel, experts, count, shares),...  52.6 us
    pallas_call x1, Pallas kernels, attention_back(): pl.pallas_call(attention_back_kernel, grid=(pairs,), in_specs=[specs['sme...  34 us
    unnamed x191, local copies, waits for them, and re-layouts  23.6 us
    pallas_call x1, Pallas kernels, attention(): pl.pallas_call(attention_kernel, grid=(pairs,), in_specs=[specs['smem'],...  21.4 us
    dot_general x5, matrix products, weight_grad(): lax.dot_general(left, right, (((0,), (0,)), ((), ())), preferred_element_...  20.4 us
  transfers between devices with their start and end apart: 56, of which 22 were waited for; matrix products, arithmetic and copies ran while one was open for 23% of the time, Pallas kernels for 18%

profile of v1, /device:TPU:0, one launch (start us, length us, event | category | flops | bytes accessed | tf_op | source)
XLA Modules:
  0.0 639.4 jit_solution(12351409408864693225)
XLA Ops:
  5.3 62.1 %start.1 = (bf16[512,512]{1,0:T(8,128)(2,1)}, bf16[2048,1024]{1,0:T(8,128)(2,1)}, bf16[512,1024]{1,0:T(8,128)(2,1)}, bf16[1024,1536]{1,0:T(8,128)(2,1)}, bf16[10...) custom-call(bf16[64,2176]{1,0:T(8,128)(2,1)} %fusion.38.pack_ref, ...), custom_call_target="tpu_custom_call" | custom-call | tf_op jit(solution)/shard_map/start/pallas_call | solution.py:512
  101.5 21.4 %attention_forward.1 = (bf16[512,512]{1,0:T(8,128)(2,1)}, f32[4,8,512]{2,1,0:T(8,128)}) custom-call(s32[2,8]{1,0:T(2,128)} %and_convert_fusion.active_ref, s32[8]{0:T(128)} %sub.12.base_ref, bf16[512,512]{1,0:T(8,128)(2,1)} %get-tuple-element.107.query_ref, bf16[2048,1024]{1,0:T(8,128)(2,1)} %get-tuple-element.108.key_ref.value_ref, ...), custom_call_target="tpu_custom_call" | custom-call | tf_op jit(solution)/shard_map/attention_forward/pallas_call | solution.py:364
  123.9 13.0 %collective-permute-done.refs_1_ = bf16[512,512]{1,0:T(8,128)(2,1)} collective-permute-done((bf16[512,512]{1,0:T(8,128)(2,1)}, bf16[512,512]{1,0:T(8,128)(2,1)}, u32[]{:S(2)}, u32[]{:S(2)}) %collective-permute-start) | collective-permute-done | bytes 524320 | tf_op jit(solution)/shard_map/ppermute | solution.py:56
  140.7 4.8 collective-permute-start.9
  147.3 7.6 %middle_step.1 = (f32[512,1024]{1,0:T(8,128)}, bf16[512,1024]{1,0:T(8,128)(2,1)}, f32[512,128]{1,0:T(8,128)}, bf16[4,320,1024]{2,1,0:T(8,128)(2,1)}) custom-call(s32[4]{0:T(128)} %pad_add_fusion.place_ref, bf16[512,512]{1,0:T(8,128)(2,1)} %get-tuple-element.109.refs_0_, bf16[512,512]{1,0:T(8,128)(2,1)} %collective-permute-done.refs_1_, ...), custom_call_target="tpu_custom_call" | custom-call | tf_op jit(solution)/shard_map/middle_step/pallas_call | solution.py:569
  155.0 3.2 slice_bitcast_fusion.1
  162.5 6.1 collective-permute-start.11
  168.7 4.0 collective-permute-start.13
  173.1 12.6 %expert_block.4 = (bf16[1280,1024]{1,0:T(8,128)(2,1)}, bf16[1280,1024]{1,0:T(8,128)(2,1)}, bf16[1280,1408]{1,0:T(8,128)(2,1)}, bf16[1280,1408]{1,0:T(8,128)(2,1)...) custom-call(s32[4]{0:T(128)} %pad_add_fusion.place_ref, ...), custom_call_target="tpu_custom_call" | custom-call | tf_op jit(solution)/shard_map/expert_block/pallas_call | solution.py:753
  185.7 6.5 %collective-permute-done.8.rows_ref = bf16[320,1024]{1,0:T(8,128)(2,1)} collective-permute-done((bf16[320,1024]{1,0:T(8,128)(2,1)}, bf16[320,1024]{1,0:T(8,128)(2,1)}, u32[]{:S(2)}, u32[]{:S(2)}) %collective-permute-start.8) | collective-permute-done | bytes 655392 | tf_op jit(solution)/shard_map/ppermute | solution.py:56
  192.3 13.3 %expert_block.5 = (bf16[1280,1024]{1,0:T(8,128)(2,1)}, bf16[1280,1024]{1,0:T(8,128)(2,1)}, bf16[1280,1408]{1,0:T(8,128)(2,1)}, bf16[1280,1408]{1,0:T(8,128)(2,1)...) custom-call(s32[4]{0:T(128)} %pad_add_fusion.place_ref, ...), custom_call_target="tpu_custom_call", output_to_operand_aliasing={{0}: (12, {}), {1}: (13, {}), {2}: (14, {}), {3}: (15, {}),... | custom-call | tf_op jit(solution)/shard_map/expert_block/pallas_call | solution.py:753
  205.6 35.1 %collective-permute-done.11.grads_ref = bf16[320,1024]{1,0:T(8,128)(2,1)S(1)} collective-permute-done((bf16[320,1024]{1,0:T(8,128)(2,1)}, bf16[320,1024]{1,0:T(8,128)(2,1)S(1)}, u32[]{:S(2)}, u32[]{:S(2)}) %collective-permute-start.11) | collective-permute-done | bytes 655392 | tf_op jit(solution)/shard_map/ppermute | solution.py:56
  240.7 14.1 %collective-permute-done.10.rows_ref = bf16[320,1024]{1,0:T(8,128)(2,1)} collective-permute-done((bf16[320,1024]{1,0:T(8,128)(2,1)}, bf16[320,1024]{1,0:T(8,128)(2,1)}, u32[]{:S(2)}, u32[]{:S(2)}) %collective-permute-start.10) | collective-permute-done | bytes 655392 | tf_op jit(solution)/shard_map/ppermute | solution.py:56
  254.8 13.1 %expert_block.6 = (bf16[1280,1024]{1,0:T(8,128)(2,1)}, bf16[1280,1024]{1,0:T(8,128)(2,1)}, bf16[1280,1408]{1,0:T(8,128)(2,1)}, bf16[1280,1408]{1,0:T(8,128)(2,1)...) custom-call(s32[4]{0:T(128)} %pad_add_fusion.place_ref, ...), custom_call_target="tpu_custom_call", output_to_operand_aliasing={{0}: (12, {}), {1}: (13, {}), {2}: (14, {}), {3}: (15, {}),... | custom-call | tf_op jit(solution)/shard_map/expert_block/pallas_call | solution.py:753
  269.0 13.6 %expert_block.7 = (bf16[1280,1024]{1,0:T(8,128)(2,1)}, bf16[1280,1024]{1,0:T(8,128)(2,1)}, bf16[1280,1408]{1,0:T(8,128)(2,1)}, bf16[1280,1408]{1,0:T(8,128)(2,1)...) custom-call(s32[4]{0:T(128)} %pad_add_fusion.place_ref, ...), custom_call_target="tpu_custom_call", output_to_operand_aliasing={{0}: (12, {}), {1}: (13, {}), {2}: (14, {}), {3}: (15, {}),... | custom-call | tf_op jit(solution)/shard_map/expert_block/pallas_call | solution.py:753
  294.3 4.2 collective-permute-start.20
  298.5 4.2 collective-permute-done.17
  302.8 15.8 %collective-permute-start.18 = (bf16[320,640]{1,0:T(8,128)(2,1)S(1)}, bf16[320,640]{1,0:T(8,128)(2,1)S(1)}, u32[]{:S(2)}, u32[]{:S(2)}) collective-permute-start(bf16[320,640]{1,0:T(8,128)(2,1)S(1)} %add_convert_fusion.8), channel_id=1, source_target_pairs={{0,16},{8,24},{16,0},{24,8},{1,17},{9,25},{17,1},{25,9},{2,18},{10... | collective-permute-start | bytes 1228808 | tf_op jit(solution)/shard_map/ppermute | solution.py:56
  318.8 7.0 %collective-permute-start.16 = (bf16[320,640]{1,0:T(8,128)(2,1)S(1)}, bf16[320,640]{1,0:T(8,128)(2,1)S(1)}, u32[]{:S(2)}, u32[]{:S(2)}) collective-permute-start(bf16[320,640]{1,0:T(8,128)(2,1)S(1)} %add_convert_fusion.9), channel_id=1, source_target_pairs={{0,8},{8,0},{16,24},{24,16},{1,9},{9,1},{17,25},{25,17},{2,10},{10... | collective-permute-start | bytes 1228808 | tf_op jit(solution)/shard_map/ppermute | solution.py:56
  326.6 5.8 convolution_convert_fusion.2
  335.8 4.7 convolution_convert_fusion.4
  340.5 4.6 convolution_convert_fusion.3
  349.8 5.4 return_step.1
  362.2 8.8 %collective-permute-done.21.refs_1_ = bf16[512,512]{1,0:T(8,128)(2,1)S(1)} collective-permute-done((bf16[512,512]{1,0:T(8,128)(2,1)}, bf16[512,512]{1,0:T(8,128)(2,1)S(1)}, u32[]{:S(2)}, u32[]{:S(2)}) %collective-permute-start.21) | collective-permute-done | bytes 524320 | tf_op jit(solution)/shard_map/ppermute | solution.py:56
  371.8 5.6 middle_back.1
  377.3 34.0 %attention_backward.1 = (bf16[512,512]{1,0:T(8,128)(2,1)}, bf16[2048,512]{1,0:T(8,128)(2,1)}, bf16[2048,512]{1,0:T(8,128)(2,1)}, f32[4,8,2560]{2,1,0:T(8,128)}) custom-call(s32[2,8]{1,0:T(2,128)} %and_convert_fusion.active_ref, s32[8]{0:T(128)} %sub.12.base_ref, bf16[512,512]{1,0:T(8,128)(2,1)} %get-tuple-element.107.query_ref, ...), custom_call_target="tpu_custom_call" | custom-call | tf_op jit(solution)/shard_map/attention_backward/pallas_call | solution.py:393
  415.3 3.2 collective-permute-start.44
  420.1 11.2 %collective-permute-start.45 = (f32[8,32]{1,0:T(8,128)S(1)}, f32[8,32]{1,0:T(8,128)S(1)}, u32[]{:S(2)}, u32[]{:S(2)}) collective-permute-start(f32[8,32]{1,0:T(8,128)S(1)} %add.355), channel_id=1, source_target_pairs={{0,8},{8,0},{16,24},{24,16},{1,9},{9,1},{17,25},{25,17},{2,10},{10... | collective-permute-start | bytes 3080 | tf_op jit(solution)/shard_map/ppermute | solution.py:56
  433.6 8.1 %collective-permute-start.46 = (f32[8,32]{1,0:T(8,128)S(1)}, f32[8,32]{1,0:T(8,128)S(1)}, u32[]{:S(2)}, u32[]{:S(2)}) collective-permute-start(f32[8,32]{1,0:T(8,128)S(1)} %add.356), channel_id=1, source_target_pairs={{0,16},{8,24},{16,0},{24,8},{1,17},{9,25},{17,1},{25,9},{2,18},{10... | collective-permute-start | bytes 3080 | tf_op jit(solution)/shard_map/ppermute | solution.py:56
  447.8 6.4 %collective-permute-done.23 = bf16[320,512]{1,0:T(8,128)(2,1)S(1)} collective-permute-done((bf16[320,512]{1,0:T(8,128)(2,1)}, bf16[320,512]{1,0:T(8,128)(2,1)S(1)}, u32[]{:S(2)}, u32[]{:S(2)}) %collective-permute-start.23) | collective-permute-done | bytes 327712 | tf_op jit(solution)/shard_map/ppermute | solution.py:56
  455.5 5.5 collective-permute-done.25
  470.3 13.5 %collective-permute-done.55 = bf16[1408,256]{1,0:T(8,128)(2,1)S(1)} collective-permute-done((bf16[1408,256]{1,0:T(8,128)(2,1)}, bf16[1408,256]{1,0:T(8,128)(2,1)S(1)}, u32[]{:S(2)}, u32[]{:S(2)}) %collective-permute-start.55) | collective-permute-done | bytes 720928 | tf_op jit(solution)/shard_map/ppermute | solution.py:56
  484.6 4.3 add_multiply_fusion.1
  489.0 6.0 collective-permute-done.32
  497.3 8.9 %collective-permute-done.35 = bf16[512,512]{1,0:T(8,128)(2,1)S(1)} collective-permute-done((bf16[512,512]{1,0:T(8,128)(2,1)S(1)}, bf16[512,512]{1,0:T(8,128)(2,1)S(1)}, u32[]{:S(2)}, u32[]{:S(2)}) %collective-permute-start.35) | collective-permute-done | bytes 524320 | tf_op jit(solution)/shard_map/ppermute | solution.py:56
  509.6 6.0 collective-permute-start.26
  515.6 6.1 collective-permute-done.49
  525.5 6.1 collective-permute-start.28
  536.9 3.5 convolution_convert_fusion.1
  548.0 4.7 add_multiply_fusion
  562.5 9.9 %collective-permute-done.29 = bf16[512,512]{1,0:T(8,128)(2,1)S(1)} collective-permute-done((bf16[512,512]{1,0:T(8,128)(2,1)S(1)}, bf16[512,512]{1,0:T(8,128)(2,1)S(1)}, u32[]{:S(2)}, u32[]{:S(2)}) %collective-permute-start.29) | collective-permute-done | bytes 524320 | tf_op jit(solution)/shard_map/ppermute | solution.py:56
  576.0 3.6 copy.216
  581.4 3.6 copy.217
  585.0 3.8 fusion.3
  592.8 3.6 convert_add_fusion.2
  606.5 7.4 %collective-permute-start.42 = (bf16[64,2176]{1,0:T(8,128)(2,1)}, bf16[64,2176]{1,0:T(8,128)(2,1)}, u32[]{:S(2)}, u32[]{:S(2)}) collective-permute-start(bf16[64,2176]{1,0:T(8,128)(2,1)} %copy.222), channel_id=1, source_target_pairs={{0,16},{8,24},{16,0},{24,8},{1,17},{9,25},{17,1},{25,9},{2,18},{10... | collective-permute-start | bytes 835592 | tf_op jit(solution)/shard_map/ppermute | solution.py:56
  613.9 4.2 fusion.8
  619.4 6.6 %collective-permute-done.42 = bf16[64,2176]{1,0:T(8,128)(2,1)} collective-permute-done((bf16[64,2176]{1,0:T(8,128)(2,1)}, bf16[64,2176]{1,0:T(8,128)(2,1)}, u32[]{:S(2)}, u32[]{:S(2)}) %collective-permute-start.42) | collective-permute-done | bytes 278560 | tf_op jit(solution)/shard_map/ppermute | solution.py:56
  (388 shorter events, 170.1 us)
Async XLA Ops:
  67.4 73.3 %collective-permute-start.1 = (bf16[1024,512]{1,0:T(8,128)(2,1)}, bf16[1024,512]{1,0:T(8,128)(2,1)}, u32[]{:S(2)}, u32[]{:S(2)}) collective-permute-start(bf16[1024,512]{1,0:T(8,128)(2,1)} %get-tuple-element.110.refs_2_.refs_5_), channel_id=1, source_target_pairs={{0,1},{1,0},{2,3},{3,2},{4,5},{5,4},{6,7},{7,6},{8,9},{9,8},{10,11... | collective-permute-start | bytes 3145736 | tf_op jit(solution)/shard_map/ppermute | solution.py:56
  75.6 47.9 %collective-permute-start.3 = (bf16[2,256,1408]{2,1,0:T(8,128)(2,1)S(1)}, bf16[2,256,1408]{2,1,0:T(8,128)(2,1)S(1)}, u32[]{:S(2)}, u32[]{:S(2)}) collective-permute-start(bf16[2,256,1408]{2,1,0:T(8,128)(2,1)S(1)} %bitcast.132), channel_id=1, source_target_pairs={{0,4},{2,6},{4,0},{6,2},{1,5},{3,7},{5,1},{7,3},{8,12},{10,14},{12... | collective-permute-start | bytes 4325384 | tf_op jit(solution)/shard_map/ppermute | solution.py:56
  77.4 59.5 %collective-permute-start.6 = (bf16[1408,256]{1,0:T(8,128)(2,1)}, bf16[1408,256]{1,0:T(8,128)(2,1)}, u32[]{:S(2)}, u32[]{:S(2)}) collective-permute-start(bf16[1408,256]{1,0:T(8,128)(2,1)} %bitcast.20.refs_4_), channel_id=1, source_target_pairs={{0,4},{2,6},{4,0},{6,2},{1,5},{3,7},{5,1},{7,3},{8,12},{10,14},{12... | collective-permute-start | bytes 2162696 | tf_op jit(solution)/shard_map/ppermute | solution.py:56
  122.8 14.1 %collective-permute-start = (bf16[512,512]{1,0:T(8,128)(2,1)}, bf16[512,512]{1,0:T(8,128)(2,1)}, u32[]{:S(2)}, u32[]{:S(2)}) collective-permute-start(bf16[512,512]{1,0:T(8,128)(2,1)} %get-tuple-element.109.refs_0_), channel_id=1, source_target_pairs={{0,1},{1,0},{2,3},{3,2},{4,5},{5,4},{6,7},{7,6},{8,9},{9,8},{10,11... | collective-permute-start | bytes 1572872 | tf_op jit(solution)/shard_map/ppermute | solution.py:56
  123.4 45.3 %collective-permute-start.2 = (bf16[2,256,1408]{2,1,0:T(8,128)(2,1)S(1)}, bf16[2,256,1408]{2,1,0:T(8,128)(2,1)}, u32[]{:S(2)}, u32[]{:S(2)}) collective-permute-start(bf16[2,256,1408]{2,1,0:T(8,128)(2,1)S(1)} %bitcast.133), channel_id=1, source_target_pairs={{0,2},{2,0},{4,6},{6,4},{1,3},{3,1},{5,7},{7,5},{8,10},{10,8},{12,... | collective-permute-start | bytes 4325384 | tf_op jit(solution)/shard_map/ppermute | solution.py:56
  123.4 49.3 %collective-permute-start.4 = (bf16[2,256,1408]{2,1,0:T(8,128)(2,1)S(1)}, bf16[2,256,1408]{2,1,0:T(8,128)(2,1)}, u32[]{:S(2)}, u32[]{:S(2)}) collective-permute-start(bf16[2,256,1408]{2,1,0:T(8,128)(2,1)S(1)} %collective-permute-done.3.refs_2_), channel_id=1, source_target_pairs={{0,2},{2,0},{4,6},{6,4},{1,3},{3,1},{5,7},{7,5},{8,10},{10,8},{12,... | collective-permute-start | bytes 4325384 | tf_op jit(solution)/shard_map/ppermute | solution.py:56
  136.9 25.6 %collective-permute-start.5 = (bf16[1408,256]{1,0:T(8,128)(2,1)}, bf16[1408,256]{1,0:T(8,128)(2,1)}, u32[]{:S(2)}, u32[]{:S(2)}) collective-permute-start(bf16[1408,256]{1,0:T(8,128)(2,1)} %bitcast.20.refs_4_), channel_id=1, source_target_pairs={{0,2},{2,0},{4,6},{6,4},{1,3},{3,1},{5,7},{7,5},{8,10},{10,8},{12,... | collective-permute-start | bytes 2162696 | tf_op jit(solution)/shard_map/ppermute | solution.py:56
  136.9 31.7 %collective-permute-start.7 = (bf16[1408,256]{1,0:T(8,128)(2,1)}, bf16[1408,256]{1,0:T(8,128)(2,1)}, u32[]{:S(2)}, u32[]{:S(2)}) collective-permute-start(bf16[1408,256]{1,0:T(8,128)(2,1)} %collective-permute-done.6.refs_6_), channel_id=1, source_target_pairs={{0,2},{2,0},{4,6},{6,4},{1,3},{3,1},{5,7},{7,5},{8,10},{10,8},{12,... | collective-permute-start | bytes 2162696 | tf_op jit(solution)/shard_map/ppermute | solution.py:56
  140.7 20.1 %collective-permute-start.9 = (bf16[320,1024]{1,0:T(8,128)(2,1)}, bf16[320,1024]{1,0:T(8,128)(2,1)}, u32[]{:S(2)}, u32[]{:S(2)}) collective-permute-start(bf16[320,1024]{1,0:T(8,128)(2,1)} %get-tuple-element.375), channel_id=1, source_target_pairs={{0,8},{8,0},{16,24},{24,16},{1,9},{9,1},{17,25},{25,17},{2,10},{10... | collective-permute-start | bytes 1966088 | tf_op jit(solution)/shard_map/ppermute | solution.py:56
  160.8 31.5 %collective-permute-start.8 = (bf16[320,1024]{1,0:T(8,128)(2,1)}, bf16[320,1024]{1,0:T(8,128)(2,1)}, u32[]{:S(2)}, u32[]{:S(2)}) collective-permute-start(bf16[320,1024]{1,0:T(8,128)(2,1)} %get-tuple-element.379), channel_id=1, source_target_pairs={{0,8},{8,0},{16,24},{24,16},{1,9},{9,1},{17,25},{25,17},{2,10},{10... | collective-permute-start | bytes 1966088 | tf_op jit(solution)/shard_map/ppermute | solution.py:56
  162.5 78.2 %collective-permute-start.11 = (bf16[320,1024]{1,0:T(8,128)(2,1)}, bf16[320,1024]{1,0:T(8,128)(2,1)S(1)}, u32[]{:S(2)}, u32[]{:S(2)}) collective-permute-start(bf16[320,1024]{1,0:T(8,128)(2,1)} %get-tuple-element.374), channel_id=1, source_target_pairs={{0,16},{8,24},{16,0},{24,8},{1,17},{9,25},{17,1},{25,9},{2,18},{10... | collective-permute-start | bytes 1966088 | tf_op jit(solution)/shard_map/ppermute | solution.py:56
  168.6 86.2 %collective-permute-start.10 = (bf16[320,1024]{1,0:T(8,128)(2,1)}, bf16[320,1024]{1,0:T(8,128)(2,1)}, u32[]{:S(2)}, u32[]{:S(2)}) collective-permute-start(bf16[320,1024]{1,0:T(8,128)(2,1)} %get-tuple-element.378), channel_id=1, source_target_pairs={{0,16},{8,24},{16,0},{24,8},{1,17},{9,25},{17,1},{25,9},{2,18},{10... | collective-permute-start | bytes 1966088 | tf_op jit(solution)/shard_map/ppermute | solution.py:56
  168.7 99.2 %collective-permute-start.13 = (bf16[320,1024]{1,0:T(8,128)(2,1)}, bf16[320,1024]{1,0:T(8,128)(2,1)S(1)}, u32[]{:S(2)}, u32[]{:S(2)}) collective-permute-start(bf16[320,1024]{1,0:T(8,128)(2,1)} %get-tuple-element.373), channel_id=1, source_target_pairs={{0,24},{8,16},{16,8},{24,0},{1,25},{9,17},{17,9},{25,1},{2,26},{10... | collective-permute-start | bytes 1966088 | tf_op jit(solution)/shard_map/ppermute | solution.py:56
  172.7 95.2 %collective-permute-start.12 = (bf16[320,1024]{1,0:T(8,128)(2,1)}, bf16[320,1024]{1,0:T(8,128)(2,1)S(1)}, u32[]{:S(2)}, u32[]{:S(2)}) collective-permute-start(bf16[320,1024]{1,0:T(8,128)(2,1)} %get-tuple-element.377), channel_id=1, source_target_pairs={{0,24},{8,16},{16,8},{24,0},{1,25},{9,17},{17,9},{25,1},{2,26},{10... | collective-permute-start | bytes 1966088 | tf_op jit(solution)/shard_map/ppermute | solution.py:56
  282.5 11.7 %collective-permute-start.19 = (bf16[320,640]{1,0:T(8,128)(2,1)}, bf16[320,640]{1,0:T(8,128)(2,1)S(1)}, u32[]{:S(2)}, u32[]{:S(2)}) collective-permute-start(bf16[320,640]{1,0:T(8,128)(2,1)} %get-tuple-element.148), channel_id=1, source_target_pairs={{0,1},{1,0},{2,3},{3,2},{4,5},{5,4},{6,7},{7,6},{8,9},{9,8},{10,11... | collective-permute-start | bytes 1228808 | tf_op jit(solution)/shard_map/ppermute | solution.py:56
  290.1 12.7 %collective-permute-start.17 = (bf16[320,640]{1,0:T(8,128)(2,1)}, bf16[320,640]{1,0:T(8,128)(2,1)S(1)}, u32[]{:S(2)}, u32[]{:S(2)}) collective-permute-start(bf16[320,640]{1,0:T(8,128)(2,1)} %get-tuple-element.146), channel_id=1, source_target_pairs={{0,1},{1,0},{2,3},{3,2},{4,5},{5,4},{6,7},{7,6},{8,9},{9,8},{10,11... | collective-permute-start | bytes 1228808 | tf_op jit(solution)/shard_map/ppermute | solution.py:56
  292.2 26.5 %collective-permute-start.15 = (bf16[320,640]{1,0:T(8,128)(2,1)}, bf16[320,640]{1,0:T(8,128)(2,1)S(1)}, u32[]{:S(2)}, u32[]{:S(2)}) collective-permute-start(bf16[320,640]{1,0:T(8,128)(2,1)} %get-tuple-element.144), channel_id=1, source_target_pairs={{0,1},{1,0},{2,3},{3,2},{4,5},{5,4},{6,7},{7,6},{8,9},{9,8},{10,11... | collective-permute-start | bytes 1228808 | tf_op jit(solution)/shard_map/ppermute | solution.py:56
  292.7 33.0 %collective-permute-start.14 = (bf16[320,640]{1,0:T(8,128)(2,1)}, bf16[320,640]{1,0:T(8,128)(2,1)S(1)}, u32[]{:S(2)}, u32[]{:S(2)}) collective-permute-start(bf16[320,640]{1,0:T(8,128)(2,1)} %get-tuple-element.142), channel_id=1, source_target_pairs={{0,1},{1,0},{2,3},{3,2},{4,5},{5,4},{6,7},{7,6},{8,9},{9,8},{10,11... | collective-permute-start | bytes 1228808 | tf_op jit(solution)/shard_map/ppermute | solution.py:56
  294.3 53.4 %collective-permute-start.20 = (bf16[320,640]{1,0:T(8,128)(2,1)S(1)}, bf16[320,640]{1,0:T(8,128)(2,1)S(1)}, u32[]{:S(2)}, u32[]{:S(2)}) collective-permute-start(bf16[320,640]{1,0:T(8,128)(2,1)S(1)} %add_convert_fusion.7), channel_id=1, source_target_pairs={{0,24},{8,16},{16,8},{24,0},{1,25},{9,17},{17,9},{25,1},{2,26},{10... | collective-permute-start | bytes 1228808 | tf_op jit(solution)/shard_map/ppermute | solution.py:56
  302.8 45.0 %collective-permute-start.18 = (bf16[320,640]{1,0:T(8,128)(2,1)S(1)}, bf16[320,640]{1,0:T(8,128)(2,1)S(1)}, u32[]{:S(2)}, u32[]{:S(2)}) collective-permute-start(bf16[320,640]{1,0:T(8,128)(2,1)S(1)} %add_convert_fusion.8), channel_id=1, source_target_pairs={{0,16},{8,24},{16,0},{24,8},{1,17},{9,25},{17,1},{25,9},{2,18},{10... | collective-permute-start | bytes 1228808 | tf_op jit(solution)/shard_map/ppermute | solution.py:56
  318.8 29.6 %collective-permute-start.16 = (bf16[320,640]{1,0:T(8,128)(2,1)S(1)}, bf16[320,640]{1,0:T(8,128)(2,1)S(1)}, u32[]{:S(2)}, u32[]{:S(2)}) collective-permute-start(bf16[320,640]{1,0:T(8,128)(2,1)S(1)} %add_convert_fusion.9), channel_id=1, source_target_pairs={{0,8},{8,0},{16,24},{24,16},{1,9},{9,1},{17,25},{25,17},{2,10},{10... | collective-permute-start | bytes 1228808 | tf_op jit(solution)/shard_map/ppermute | solution.py:56
  333.8 23.1 %collective-permute-start.54 = (bf16[1408,256]{1,0:T(8,128)(2,1)}, bf16[1408,256]{1,0:T(8,128)(2,1)}, u32[]{:S(2)}, u32[]{:S(2)}) collective-permute-start(bf16[1408,256]{1,0:T(8,128)(2,1)} %get-tuple-element.368), channel_id=1, source_target_pairs={{0,2},{2,0},{4,6},{6,4},{1,3},{3,1},{5,7},{7,5},{8,10},{10,8},{12,... | collective-permute-start | bytes 2162696 | tf_op jit(solution)/shard_map/ppermute | solution.py:56
  334.7 134.4 %collective-permute-start.53 = (bf16[1408,256]{1,0:T(8,128)(2,1)}, bf16[1408,256]{1,0:T(8,128)(2,1)S(1)}, u32[]{:S(2)}, u32[]{:S(2)}) collective-permute-start(bf16[1408,256]{1,0:T(8,128)(2,1)} %get-tuple-element.367), channel_id=1, source_target_pairs={{0,2},{2,0},{4,6},{6,4},{1,3},{3,1},{5,7},{7,5},{8,10},{10,8},{12,... | collective-permute-start | bytes 2162696 | tf_op jit(solution)/shard_map/ppermute | solution.py:56
  347.7 13.0 %collective-permute-start.48 = (bf16[256,1408]{1,0:T(8,128)(2,1)}, bf16[256,1408]{1,0:T(8,128)(2,1)}, u32[]{:S(2)}, u32[]{:S(2)}) collective-permute-start(bf16[256,1408]{1,0:T(8,128)(2,1)} %get-tuple-element.370), channel_id=1, source_target_pairs={{0,2},{2,0},{4,6},{6,4},{1,3},{3,1},{5,7},{7,5},{8,10},{10,8},{12,... | collective-permute-start | bytes 2162696 | tf_op jit(solution)/shard_map/ppermute | solution.py:56
  347.8 161.8 %collective-permute-start.47 = (bf16[256,1408]{1,0:T(8,128)(2,1)}, bf16[256,1408]{1,0:T(8,128)(2,1)}, u32[]{:S(2)}, u32[]{:S(2)}) collective-permute-start(bf16[256,1408]{1,0:T(8,128)(2,1)} %get-tuple-element.369), channel_id=1, source_target_pairs={{0,2},{2,0},{4,6},{6,4},{1,3},{3,1},{5,7},{7,5},{8,10},{10,8},{12,... | collective-permute-start | bytes 2162696 | tf_op jit(solution)/shard_map/ppermute | solution.py:56
  349.3 63.4 %collective-permute-start.51 = (bf16[256,1408]{1,0:T(8,128)(2,1)}, bf16[256,1408]{1,0:T(8,128)(2,1)}, u32[]{:S(2)}, u32[]{:S(2)}) collective-permute-start(bf16[256,1408]{1,0:T(8,128)(2,1)} %get-tuple-element.372), channel_id=1, source_target_pairs={{0,2},{2,0},{4,6},{6,4},{1,3},{3,1},{5,7},{7,5},{8,10},{10,8},{12,... | collective-permute-start | bytes 2162696 | tf_op jit(solution)/shard_map/ppermute | solution.py:56
  356.9 14.1 %collective-permute-start.21 = (bf16[512,512]{1,0:T(8,128)(2,1)}, bf16[512,512]{1,0:T(8,128)(2,1)S(1)}, u32[]{:S(2)}, u32[]{:S(2)}) collective-permute-start(bf16[512,512]{1,0:T(8,128)(2,1)} %get-tuple-element.150.refs_0_), channel_id=1, source_target_pairs={{0,1},{1,0},{2,3},{3,2},{4,5},{5,4},{6,7},{7,6},{8,9},{9,8},{10,11... | collective-permute-start | bytes 1572872 | tf_op jit(solution)/shard_map/ppermute | solution.py:56
  419.6 47.5 %collective-permute-start.31 = (bf16[512,512]{1,0:T(8,128)(2,1)}, bf16[512,512]{1,0:T(8,128)(2,1)}, u32[]{:S(2)}, u32[]{:S(2)}) collective-permute-start(bf16[512,512]{1,0:T(8,128)(2,1)} %get-tuple-element.384), channel_id=1, source_target_pairs={{0,2},{2,0},{4,6},{6,4},{1,3},{3,1},{5,7},{7,5},{8,10},{10,8},{12,... | collective-permute-start | bytes 1572872 | tf_op jit(solution)/shard_map/ppermute | solution.py:56
  420.1 13.5 %collective-permute-start.45 = (f32[8,32]{1,0:T(8,128)S(1)}, f32[8,32]{1,0:T(8,128)S(1)}, u32[]{:S(2)}, u32[]{:S(2)}) collective-permute-start(f32[8,32]{1,0:T(8,128)S(1)} %add.355), channel_id=1, source_target_pairs={{0,8},{8,0},{16,24},{24,16},{1,9},{9,1},{17,25},{25,17},{2,10},{10... | collective-permute-start | bytes 3080 | tf_op jit(solution)/shard_map/ppermute | solution.py:56
  433.1 11.3 %collective-permute-start.22 = (bf16[320,512]{1,0:T(8,128)(2,1)}, bf16[320,512]{1,0:T(8,128)(2,1)}, u32[]{:S(2)}, u32[]{:S(2)}) collective-permute-start(bf16[320,512]{1,0:T(8,128)(2,1)} %get-tuple-element.153), channel_id=1, source_target_pairs={{0,1},{1,0},{2,3},{3,2},{4,5},{5,4},{6,7},{7,6},{8,9},{9,8},{10,11... | collective-permute-start | bytes 983048 | tf_op jit(solution)/shard_map/ppermute | solution.py:56
  444.5 16.5 %collective-permute-start.25 = (bf16[320,512]{1,0:T(8,128)(2,1)}, bf16[320,512]{1,0:T(8,128)(2,1)S(1)}, u32[]{:S(2)}, u32[]{:S(2)}) collective-permute-start(bf16[320,512]{1,0:T(8,128)(2,1)} %get-tuple-element.157), channel_id=1, source_target_pairs={{0,1},{1,0},{2,3},{3,2},{4,5},{5,4},{6,7},{7,6},{8,9},{9,8},{10,11... | collective-permute-start | bytes 983048 | tf_op jit(solution)/shard_map/ppermute | solution.py:56
  464.5 19.3 %collective-permute-start.55 = (bf16[1408,256]{1,0:T(8,128)(2,1)}, bf16[1408,256]{1,0:T(8,128)(2,1)S(1)}, u32[]{:S(2)}, u32[]{:S(2)}) collective-permute-start(bf16[1408,256]{1,0:T(8,128)(2,1)} %add_convert_fusion), channel_id=1, source_target_pairs={{0,4},{2,6},{4,0},{6,2},{1,5},{3,7},{5,1},{7,3},{8,12},{10,14},{12... | collective-permute-start | bytes 2162696 | tf_op jit(solution)/shard_map/ppermute | solution.py:56
  467.1 21.9 %collective-permute-start.30 = (bf16[512,512]{1,0:T(8,128)(2,1)}, bf16[512,512]{1,0:T(8,128)(2,1)S(1)}, u32[]{:S(2)}, u32[]{:S(2)}) collective-permute-start(bf16[512,512]{1,0:T(8,128)(2,1)} %get-tuple-element.383), channel_id=1, source_target_pairs={{0,2},{2,0},{4,6},{6,4},{1,3},{3,1},{5,7},{7,5},{8,10},{10,8},{12,... | collective-permute-start | bytes 1572872 | tf_op jit(solution)/shard_map/ppermute | solution.py:56
  468.3 27.7 %collective-permute-start.33 = (bf16[512,512]{1,0:T(8,128)(2,1)}, bf16[512,512]{1,0:T(8,128)(2,1)S(1)}, u32[]{:S(2)}, u32[]{:S(2)}) collective-permute-start(bf16[512,512]{1,0:T(8,128)(2,1)} %get-tuple-element.385), channel_id=1, source_target_pairs={{0,2},{2,0},{4,6},{6,4},{1,3},{3,1},{5,7},{7,5},{8,10},{10,8},{12,... | collective-permute-start | bytes 1572872 | tf_op jit(solution)/shard_map/ppermute | solution.py:56
  469.0 26.0 %collective-permute-start.32 = (bf16[512,512]{1,0:T(8,128)(2,1)S(1)}, bf16[512,512]{1,0:T(8,128)(2,1)S(1)}, u32[]{:S(2)}, u32[]{:S(2)}) collective-permute-start(bf16[512,512]{1,0:T(8,128)(2,1)S(1)} %add_convert_fusion.6), channel_id=1, source_target_pairs={{0,4},{2,6},{4,0},{6,2},{1,5},{3,7},{5,1},{7,3},{8,12},{10,14},{12... | collective-permute-start | bytes 1572872 | tf_op jit(solution)/shard_map/ppermute | solution.py:56
  483.8 22.5 %collective-permute-start.35 = (bf16[512,512]{1,0:T(8,128)(2,1)S(1)}, bf16[512,512]{1,0:T(8,128)(2,1)S(1)}, u32[]{:S(2)}, u32[]{:S(2)}) collective-permute-start(bf16[512,512]{1,0:T(8,128)(2,1)S(1)} %add_convert_fusion.4), channel_id=1, source_target_pairs={{0,4},{2,6},{4,0},{6,2},{1,5},{3,7},{5,1},{7,3},{8,12},{10,14},{12... | collective-permute-start | bytes 1572872 | tf_op jit(solution)/shard_map/ppermute | solution.py:56
  489.0 36.6 %collective-permute-start.50 = (bf16[256,1408]{1,0:T(8,128)(2,1)S(1)}, bf16[256,1408]{1,0:T(8,128)(2,1)S(1)}, u32[]{:S(2)}, u32[]{:S(2)}) collective-permute-start(bf16[256,1408]{1,0:T(8,128)(2,1)S(1)} %copy-done.37), channel_id=1, source_target_pairs={{0,2},{2,0},{4,6},{6,4},{1,3},{3,1},{5,7},{7,5},{8,10},{10,8},{12,... | collective-permute-start | bytes 2162696 | tf_op jit(solution)/shard_map/ppermute | solution.py:56
  495.0 26.7 %collective-permute-start.49 = (bf16[256,1408]{1,0:T(8,128)(2,1)S(1)}, bf16[256,1408]{1,0:T(8,128)(2,1)S(1)}, u32[]{:S(2)}, u32[]{:S(2)}) collective-permute-start(bf16[256,1408]{1,0:T(8,128)(2,1)S(1)} %add_convert_fusion.2), channel_id=1, source_target_pairs={{0,4},{2,6},{4,0},{6,2},{1,5},{3,7},{5,1},{7,3},{8,12},{10,14},{12... | collective-permute-start | bytes 2162696 | tf_op jit(solution)/shard_map/ppermute | solution.py:56
  496.0 37.9 %collective-permute-start.52 = (bf16[256,1408]{1,0:T(8,128)(2,1)S(1)}, bf16[256,1408]{1,0:T(8,128)(2,1)S(1)}, u32[]{:S(2)}, u32[]{:S(2)}) collective-permute-start(bf16[256,1408]{1,0:T(8,128)(2,1)S(1)} %copy-done.36), channel_id=1, source_target_pairs={{0,4},{2,6},{4,0},{6,2},{1,5},{3,7},{5,1},{7,3},{8,12},{10,14},{12... | collective-permute-start | bytes 2162696 | tf_op jit(solution)/shard_map/ppermute | solution.py:56
  506.3 49.9 %collective-permute-start.24 = (bf16[320,512]{1,0:T(8,128)(2,1)}, bf16[320,512]{1,0:T(8,128)(2,1)}, u32[]{:S(2)}, u32[]{:S(2)}) collective-permute-start(bf16[320,512]{1,0:T(8,128)(2,1)} %add_convert_fusion.13), channel_id=1, source_target_pairs={{0,8},{8,0},{16,24},{24,16},{1,9},{9,1},{17,25},{25,17},{2,10},{10... | collective-permute-start | bytes 983048 | tf_op jit(solution)/shard_map/ppermute | solution.py:56
  509.6 46.5 %collective-permute-start.26 = (bf16[320,512]{1,0:T(8,128)(2,1)}, bf16[320,512]{1,0:T(8,128)(2,1)}, u32[]{:S(2)}, u32[]{:S(2)}) collective-permute-start(bf16[320,512]{1,0:T(8,128)(2,1)} %add_convert_fusion.12), channel_id=1, source_target_pairs={{0,16},{8,24},{16,0},{24,8},{1,17},{9,25},{17,1},{25,9},{2,18},{10... | collective-permute-start | bytes 983048 | tf_op jit(solution)/shard_map/ppermute | solution.py:56
  521.7 18.8 %collective-permute-start.36 = (bf16[512,1024]{1,0:T(8,128)(2,1)S(1)}, bf16[512,1024]{1,0:T(8,128)(2,1)S(1)}, u32[]{:S(2)}, u32[]{:S(2)}) collective-permute-start(bf16[512,1024]{1,0:T(8,128)(2,1)S(1)} %convolution_convert_fusion.5), channel_id=1, source_target_pairs={{0,1},{1,0},{2,3},{3,2},{4,5},{5,4},{6,7},{7,6},{8,9},{9,8},{10,11... | collective-permute-start | bytes 3145736 | tf_op jit(solution)/shard_map/ppermute | solution.py:56
  525.5 30.6 %collective-permute-start.28 = (bf16[320,512]{1,0:T(8,128)(2,1)}, bf16[320,512]{1,0:T(8,128)(2,1)}, u32[]{:S(2)}, u32[]{:S(2)}) collective-permute-start(bf16[320,512]{1,0:T(8,128)(2,1)} %add_convert_fusion.11), channel_id=1, source_target_pairs={{0,24},{8,16},{16,8},{24,0},{1,25},{9,17},{17,9},{25,1},{2,26},{10... | collective-permute-start | bytes 983048 | tf_op jit(solution)/shard_map/ppermute | solution.py:56
  552.7 23.3 %collective-permute-start.37 = (bf16[4,64,2176]{2,1,0:T(8,128)(2,1)}, bf16[4,64,2176]{2,1,0:T(8,128)(2,1)}, u32[]{:S(2)}, u32[]{:S(2)}) collective-permute-start(bf16[4,64,2176]{2,1,0:T(8,128)(2,1)} %get-tuple-element.362), channel_id=1, source_target_pairs={{0,2},{2,0},{4,6},{6,4},{1,3},{3,1},{5,7},{7,5},{8,10},{10,8},{12,... | collective-permute-start | bytes 3342344 | tf_op jit(solution)/shard_map/ppermute | solution.py:56
  554.1 27.3 %collective-permute-start.39 = (bf16[4,64,2176]{2,1,0:T(8,128)(2,1)}, bf16[4,64,2176]{2,1,0:T(8,128)(2,1)}, u32[]{:S(2)}, u32[]{:S(2)}) collective-permute-start(bf16[4,64,2176]{2,1,0:T(8,128)(2,1)} %fusion.6), channel_id=1, source_target_pairs={{0,4},{2,6},{4,0},{6,2},{1,5},{3,7},{5,1},{7,3},{8,12},{10,14},{12... | collective-permute-start | bytes 3342344 | tf_op jit(solution)/shard_map/ppermute | solution.py:56
  558.3 14.2 %collective-permute-start.29 = (bf16[512,512]{1,0:T(8,128)(2,1)S(1)}, bf16[512,512]{1,0:T(8,128)(2,1)S(1)}, u32[]{:S(2)}, u32[]{:S(2)}) collective-permute-start(bf16[512,512]{1,0:T(8,128)(2,1)S(1)} %fusion.24), channel_id=1, source_target_pairs={{0,1},{1,0},{2,3},{3,2},{4,5},{5,4},{6,7},{7,6},{8,9},{9,8},{10,11... | collective-permute-start | bytes 1572872 | tf_op jit(solution)/shard_map/ppermute | solution.py:56
  598.3 19.9 %collective-permute-start.40 = (bf16[64,2176]{1,0:T(8,128)(2,1)S(1)}, bf16[64,2176]{1,0:T(8,128)(2,1)}, u32[]{:S(2)}, u32[]{:S(2)}) collective-permute-start(bf16[64,2176]{1,0:T(8,128)(2,1)S(1)} %bitcast.143), channel_id=1, source_target_pairs={{0,8},{8,0},{16,24},{24,16},{1,9},{9,1},{17,25},{25,17},{2,10},{10... | collective-permute-start | bytes 835592 | tf_op jit(solution)/shard_map/ppermute | solution.py:56
  606.5 19.5 %collective-permute-start.42 = (bf16[64,2176]{1,0:T(8,128)(2,1)}, bf16[64,2176]{1,0:T(8,128)(2,1)}, u32[]{:S(2)}, u32[]{:S(2)}) collective-permute-start(bf16[64,2176]{1,0:T(8,128)(2,1)} %copy.222), channel_id=1, source_target_pairs={{0,16},{8,24},{16,0},{24,8},{1,17},{9,25},{17,1},{25,9},{2,18},{10... | collective-permute-start | bytes 835592 | tf_op jit(solution)/shard_map/ppermute | solution.py:56
  (96 other events, 1286.8 us)

commit v2 on v1

--- a/solution.py
+++ b/solution.py
@@ -31,6 +31,12 @@
 GELU_C = 0.044715
 
 
+def tree_sum(values):
+    while len(values) > 1:
+        values = [values[k] + values[k + 1] for k in range(0, len(values), 2)]
+    return values[0]
+
+
 def rms_scale(values):
     return lax.rsqrt(jnp.mean(values * values, axis=-1, keepdims=True) + NORM_EPS)
 
@@ -49,6 +55,10 @@
         first_new / FIX_ONE / (jnp.sqrt(second_new / FIX_TWO) + ADAM_EPS) + WEIGHT_DECAY * weight
     )
     return (first_new, second_new, update)
+
+
+def cost(micros):
+    return pl.CostEstimate(flops=int(micros * 1.15e9), bytes_accessed=1 << 20, transcendentals=0)
 
 
 def swap(values, axis, bits):
@@ -115,17 +125,22 @@
         )
         copy.start()
         self.count += 1
-        self.copies.append(copy)
-        return Arrival(copy)
+        self.copies.append(Arrival(copy))
+        return self.copies[-1]
 
     def finish(self):
         for copy in self.copies:
-            copy.wait_send()
+            copy.sent()
 
 
 class Arrival:
     def __init__(self, copy):
-        self.copy, self.waited = copy, False
+        self.copy, self.waited, self.gone = copy, False, False
+
+    def sent(self):
+        if not self.gone:
+            self.copy.wait_send()
+        self.gone = True
 
     def wait(self):
         if not self.waited:
@@ -382,6 +397,7 @@
             pltpu.VMEM((2, HEAD_DIM, BLOCK), F32),
         ],
         compiler_params=pltpu.CompilerParams(vmem_limit_bytes=VMEM_CAP),
+        cost_estimate=cost(25),
         name="attention_forward",
     )(active, base, queries, key_values, key_values, window, doc_row, doc_col)
 
@@ -416,6 +432,7 @@
             pltpu.VMEM((length, LANES), F32),
         ],
         compiler_params=pltpu.CompilerParams(vmem_limit_bytes=VMEM_CAP),
+        cost_estimate=cost(40),
         name="attention_backward",
     )(active, base, queries, key_values, key_values, grads, totals, window, doc_row, doc_col)
 
@@ -534,241 +551,532 @@
         compiler_params=pltpu.CompilerParams(
             vmem_limit_bytes=VMEM_CAP, collective_id=1, has_side_effects=True
         ),
+        cost_estimate=cost(60),
         name="start",
     )(pack, hidden, docs)
 
 
-def middle_kernel(shares, place_ref, *refs):
-    attended, outs = refs[:shares], refs[shares : 2 * shares]
-    (hidden_ref, gains_ref, lanes_ref, picker_ref,
-     middle_ref, normed_ref, probs_ref, send_ref, weights, mixed) = refs[2 * shares :]
-    share, experts = place_ref[2], place_ref[3]
-    width = attended[0].shape[1]
-    for m in range(shares):
-        part = pl.ds(pl.multiple_of((share ^ m) * width, width), width)
-        mixed[:, part] = attended[m][...]
-        weights[:, part] = outs[m][...]
-    middle = hidden_ref[...].astype(F32) + mm(mixed[...], weights[...], NT)
+TN = (((0,), (0,)), ((), ()))
+
+
+def bent_parts(value):
+    square = value * value
+    wave = jnp.tanh(GELU_K * value * (1.0 + GELU_C * square))
+    half = 0.5 * (1.0 + wave)
+    slope = half + 0.5 * value * (1.0 - wave * wave) * (GELU_K * (1.0 + 3.0 * GELU_C * square))
+    return value * half, slope
+
+
+def expert_kernel(
+    experts, dp_count, ctx_count, tp_count, attended_ref, hidden_ref, out_grad_ref, gains_ref,
+    lanes_ref, picker_ref, *refs,
+):
+    d, c, t = lax.axis_index("dp"), lax.axis_index("ctx"), lax.axis_index("tp")
+    outs, refs = refs[:tp_count], refs[tp_count:]
+    grads, refs = refs[:dp_count], refs[dp_count:]
+    ins, downs, refs = refs[:ctx_count], refs[ctx_count : 2 * ctx_count], refs[2 * ctx_count :]
+    (middle_ref, normed_ref, logit_ref, grad_ref, low_ref, attended_grad_ref, gain_ref, out_parts,
+     in_keep, down_keep, in_core, down_core,
+     mixed, out_all, in_all, down_all, rows_all, scaled_all, act_all, gate_all, up_all, send_rows,
+     row_parts, row_in, row_back, dot_parts, dot_in, dot_home, dot_back, probs, whole,
+     sends, receives, in_sems, keep_sems) = refs
+    tokens, width = attended_ref.shape
+    share = D // tp_count
+    slots = rows_all.shape[0] // dp_count
+    depth, ff = ins[0].shape[1], ins[0].shape[2]
+    shares = range(1, tp_count)
+    order = [0] + list(range(2, dp_count)) + [1]
+
+    local = []
+
+    def load(source, target):
+        copy = pltpu.make_async_copy(source, target, in_sems.at[len(local)])
+        copy.start()
+        local.append(copy)
+        return copy
+
+    out_copies = [
+        load(outs[m], out_all.at[:, pl.ds(pl.multiple_of((t ^ m) * width, width), width)])
+        for m in range(tp_count)
+    ]
+    weight_copies = []
+    for j in range(ctx_count):
+        part = slice(j * depth, (j + 1) * depth)
+        weight_copies.append(load(ins[j], in_all.at[:, part, :]))
+        weight_copies.append(load(downs[j], down_all.at[:, part]))
+    for m in range(dp_count):
+        weight_copies.append(load(grads[m], scaled_all.at[m * slots : (m + 1) * slots]))
+    own_lanes = pl.ds(pl.multiple_of(t * width, width), width)
+    mixed[:, own_lanes] = attended_ref[...]
+    greet(
+        [{"tp": t ^ k} for k in shares]
+        + [{"dp": d ^ m} for m in range(1, dp_count)]
+        + [{"ctx": c ^ 1}]
+    )
+    wire = Wire(sends, receives)
+    arrivals = [wire.send(mixed.at[:, own_lanes], mixed.at[:, own_lanes], tp=t ^ k) for k in shares]
+    for copy in out_copies:
+        copy.wait()
+    for copy in arrivals:
+        copy.wait()
+    middle = hidden_ref[...].astype(F32) + mm(mixed[...], out_all[...], NT)
     middle_ref[...] = middle
     scale = lax.rsqrt(jnp.mean(middle * middle, axis=-1, keepdims=True) + NORM_EPS)
     normed = (middle * scale * gains_ref[1:2, :]).astype(BF16)
     normed_ref[...] = normed
-    logits = mm(normed, lanes_ref[...])
-    lane = lax.broadcasted_iota(jnp.int32, logits.shape, 1)
-    logits = jnp.where(lane < experts, logits, NEG_FILL)
-    powers = jnp.exp(logits - jnp.max(logits, axis=1, keepdims=True))
-    probs_ref[...] = powers / jnp.sum(powers, axis=1, keepdims=True)
-    slots = send_ref.shape[1]
-    for m in range(send_ref.shape[0]):
-        send_ref[m] = mm(picker_ref[m * slots : (m + 1) * slots, :], normed).astype(BF16)
-
-
-def middle_step(places, attended, outs, hidden, gains, lanes, picker, blocks):
-    shares, (tokens, width) = len(attended), attended[0].shape
-    vmem = pl.BlockSpec(memory_space=pltpu.VMEM)
-    return pl.pallas_call(
-        functools.partial(middle_kernel, shares),
-        in_specs=[pl.BlockSpec(memory_space=pltpu.SMEM)] + [vmem] * (2 * shares + 4),
-        out_specs=[vmem] * 4,
-        out_shape=[
-            jax.ShapeDtypeStruct((tokens, D), F32),
-            jax.ShapeDtypeStruct((tokens, D), BF16),
-            jax.ShapeDtypeStruct((tokens, LANES), F32),
-            jax.ShapeDtypeStruct((blocks, picker.shape[0] // blocks, D), BF16),
-        ],
-        scratch_shapes=[
-            pltpu.VMEM((D, width * shares), BF16),
-            pltpu.VMEM((tokens, width * shares), BF16),
-        ],
-        compiler_params=pltpu.CompilerParams(vmem_limit_bytes=VMEM_CAP),
-        name="middle_step",
-    )(places, *attended, *outs, hidden, gains, lanes, picker)
-
-
-def return_kernel(shares, place_ref, *refs):
-    parts = refs[:-6]
-    picker_ref, probs_ref, lanes_ref, grad_ref, logit_ref, back = refs[-6:]
-    share, experts = place_ref[2], place_ref[3]
-    slots = parts[0].shape[0]
-    width = grad_ref.shape[1]
-    for m, part in enumerate(parts):
-        back[m * slots : (m + 1) * slots, :] = part[...]
-    returned = mm(picker_ref[...], back[...])
-    tail = returned[:, width:]
-    lane = lax.broadcasted_iota(jnp.int32, tail.shape, 1)
-    step = LANES // (2 * shares)
-    prob_grad = tail
-    for k in range(1, 2 * shares):
-        prob_grad = prob_grad + pltpu.roll(tail, LANES - k * step, 1)
-    probs = probs_ref[...]
-    prob_grad = jnp.where(lane < experts, prob_grad, 0.0)
-    logit = probs * (prob_grad - jnp.sum(probs * prob_grad, axis=1, keepdims=True))
+    own_share = pl.ds(pl.multiple_of(t * share, share), share)
+    far = {}
+
+    def block(m):
+        return slice(m * slots, (m + 1) * slots)
+
+    for m in order[1:] + [0]:
+        picked = mm(picker_ref[:, block(m)], normed_ref[...], TN).astype(BF16)
+        if m:
+            send_rows[m - 1] = picked
+            far[m] = wire.send(
+                send_rows.at[m - 1, :, own_share], rows_all.at[block(m), own_share], dp=d ^ m
+            )
+        else:
+            rows_all[block(0), :] = picked
+    lane = lax.broadcasted_iota(jnp.int32, (tokens, LANES), 1)
+
+    def router_probs(values):
+        logits = mm(values, lanes_ref[...])
+        where = lax.broadcasted_iota(jnp.int32, logits.shape, 1)
+        logits = jnp.where(where < experts, logits, NEG_FILL)
+        powers = jnp.exp(logits - jnp.max(logits, axis=1, keepdims=True))
+        return where, powers / jnp.sum(powers, axis=1, keepdims=True)
+
+    probs[...] = router_probs(normed_ref[...])[1]
+    for copy in weight_copies:
+        copy.wait()
+    columns = [pl.ds(pl.multiple_of((c ^ j) * depth, depth), depth) for j in range(ctx_count)]
+    spread, returned, dot_returned = {}, {}, {}
+
+    def forward(m):
+        far[m].wait()
+        half = rows_all.at[block(m), own_share]
+        spread[m] = [wire.send(half, half, tp=t ^ k) for k in shares]
+
+    def experts_on(m, hook):
+        here = block(m)
+        where, chance = router_probs(rows_all[here, :])
+        gate = jnp.sum(jnp.where(where == d, chance, 0.0), axis=1, keepdims=True)
+        rows = jnp.concatenate([rows_all[here, part] for part in columns], axis=1)
+        grad_rows = jnp.concatenate([scaled_all[here, part] for part in columns], axis=1)
+        rows_all[here, :] = rows
+        scaled_all[here, :] = (gate * grad_rows.astype(F32)).astype(BF16)
+        dots = jnp.zeros((slots, LANES), F32)
+        for first in range(0, ff, BLOCK):
+            part = slice(first, min(ff, first + BLOCK))
+            value = mm(rows, in_all[0, :, part])
+            up = mm(rows, in_all[1, :, part])
+            back = mm(grad_rows, down_all[part, :], NT)
+            bent, slope = bent_parts(value)
+            act = (bent * up).astype(BF16)
+            act_all[here, part] = act
+            dots += jnp.sum(act.astype(F32) * back, axis=1, keepdims=True)
+            scaled = gate * back
+            gate_all[here, part] = (scaled * up * slope).astype(BF16)
+            up_all[here, part] = (scaled * bent).astype(BF16)
+        if hook is not None:
+            hook()
+        dot_parts[m] = dots.T[:8]
+        dot_returned[m] = [
+            wire.send(dot_parts.at[m], dot_in.at[k - 1, m], tp=t ^ k) for k in shares
+        ]
+        for k in list(shares) + [0]:
+            for i in range(share // depth):
+                piece = ((t ^ k) * (share // depth) + i) ^ c
+                part = pl.ds(pl.multiple_of(piece * depth, depth), depth)
+                row = mm(gate_all[here, :], in_all[0, part, :], NT)
+                row += mm(up_all[here, :], in_all[1, part, :], NT)
+                row_parts[k, m, :, i * depth : (i + 1) * depth] = row.astype(BF16)
+            if k:
+                returned.setdefault(m, []).append(
+                    wire.send(row_parts.at[k, m], row_in.at[k - 1, m], tp=t ^ k)
+                )
+        for k in range(tp_count):
+            for i in range(share // depth):
+                piece = ((t ^ k) * (share // depth) + i) ^ c
+                part = pl.ds(pl.multiple_of(piece * depth, depth), depth)
+                out_parts[k, m, :, i * depth : (i + 1) * depth] = (
+                    gate * mm(act_all[here, :], down_all[:, part])
+                ).astype(BF16)
+
+    homeward = []
+
+    def send_home(m):
+        for copy in dot_returned[m]:
+            copy.wait()
+        dots = tree_sum([dot_parts[m]] + [dot_in[k - 1, m] for k in shares])
+        total = row_parts[0, m].astype(F32)
+        for k, copy in zip(shares, returned[m]):
+            copy.wait()
+            total = total + row_in[k - 1, m].astype(F32)
+        if m:
+            dot_home[m] = dots
+            row_parts[0, m] = total.astype(BF16)
+            homeward.append(wire.send(dot_home.at[m], dot_back.at[m], dp=d ^ m))
+            homeward.append(wire.send(row_parts.at[0, m], row_back.at[block(m)], dp=d ^ m))
+        else:
+            dot_back[0] = dots
+            row_back[block(0), :] = total.astype(BF16)
+
+    for i, m in enumerate(order):
+        for copy in spread.get(m, []):
+            copy.wait()
+            copy.sent()
+        hook = functools.partial(forward, order[i + 1]) if i + 1 < len(order) else None
+        experts_on(m, hook)
+        if i:
+            send_home(order[i - 1])
+
+    def in_grads(j):
+        part = slice(j * depth, (j + 1) * depth)
+        for side, right in enumerate((gate_all, up_all)):
+            in_all[side, part, :] = mm(rows_all[:, part], right[...], TN).astype(BF16)
+
+    keeps = []
+
+    def keep(source, target):
+        copy = pltpu.make_async_copy(source, target, keep_sems.at[len(keeps)])
+        copy.start()
+        keeps.append(copy)
+
+    near = []
+    in_grads(1)
+    send_home(order[-1])
+    for j in range(1, ctx_count, 2):
+        part = slice(j * depth, (j + 1) * depth)
+        if j > 1:
+            in_grads(j)
+        near.append(wire.send(in_all.at[:, part, :], in_core.at[j // 2], ctx=c ^ 1))
+    for first in range(0, ff, BLOCK):
+        part = slice(first, min(ff, first + BLOCK))
+        down_all[part, :] = mm(act_all[:, part], scaled_all[...], TN).astype(BF16)
+    for j in range(ctx_count):
+        part = slice(j * depth, (j + 1) * depth)
+        if j % 2:
+            near.append(wire.send(down_all.at[:, part], down_core.at[j // 2], ctx=c ^ 1))
+        else:
+            keep(down_all.at[:, part], down_keep.at[j // 2])
+    for j in range(0, ctx_count, 2):
+        in_grads(j)
+        keep(in_all.at[:, j * depth : (j + 1) * depth, :], in_keep.at[j // 2])
+
+    for copy in homeward:
+        copy.wait()
+    result = mm(picker_ref[...], row_back[...])
+    prob_grad = jnp.zeros((tokens, LANES), F32)
+    for m in range(dp_count):
+        high = dot_back[m].astype(BF16)
+        rest = dot_back[m] - high.astype(F32)
+        middle_part = rest.astype(BF16)
+        tiny = (rest - middle_part.astype(F32)).astype(BF16)
+        total = mm(picker_ref[:, block(m)], high, NT)
+        total += mm(picker_ref[:, block(m)], middle_part, NT)
+        total += mm(picker_ref[:, block(m)], tiny, NT)
+        prob_grad = jnp.where(lane == (d ^ m), total[:, 0:1], prob_grad)
+    chance = probs[...]
+    logit = chance * (prob_grad - jnp.sum(chance * prob_grad, axis=1, keepdims=True))
     logit_ref[...] = logit
-    lanes = lanes_ref[pl.ds(pl.multiple_of(share * width, width), width), :]
     more = lax.dot_general(
-        logit, lanes.astype(F32), NT, precision=lax.Precision.HIGHEST, preferred_element_type=F32
-    )
-    grad_ref[...] = (returned[:, :width] + more).astype(BF16)
-
-
-def return_step(places, parts, picker_flip, probs, lanes, shares):
-    tokens = picker_flip.shape[0]
-    slots, columns = parts[0].shape
-    vmem = pl.BlockSpec(memory_space=pltpu.VMEM)
-    return pl.pallas_call(
-        functools.partial(return_kernel, shares),
-        in_specs=[pl.BlockSpec(memory_space=pltpu.SMEM)] + [vmem] * (len(parts) + 3),
-        out_specs=[vmem] * 2,
-        out_shape=[
-            jax.ShapeDtypeStruct((tokens, columns - LANES), BF16),
-            jax.ShapeDtypeStruct((tokens, LANES), F32),
-        ],
-        scratch_shapes=[pltpu.VMEM((slots * len(parts), columns), BF16)],
-        compiler_params=pltpu.CompilerParams(vmem_limit_bytes=VMEM_CAP),
-        name="return_step",
-    )(places, *parts, picker_flip, probs, lanes)
-
-
-def middle_back_kernel(shares, place_ref, *refs):
-    halves = refs[:shares]
-    (middle_ref, out_grad_ref, gains_ref, own_ref,
-     grad_ref, low_ref, attended_ref, gain_ref, whole) = refs[shares:]
-    share = place_ref[2]
-    width = halves[0].shape[1]
-    for m in range(shares):
-        first = pl.multiple_of((share ^ m) * width, width)
-        whole[:, pl.ds(first, width)] = halves[m][...]
+        logit, lanes_ref[own_share, :].astype(F32), NT, precision=lax.Precision.HIGHEST,
+        preferred_element_type=F32,
+    )
+    whole[:, own_share] = (result + more).astype(BF16)
+    arrivals = [wire.send(whole.at[:, own_share], whole.at[:, own_share], tp=t ^ k) for k in shares]
+    for copy in arrivals:
+        copy.wait()
     middle = middle_ref[...]
     gradient = whole[...].astype(F32)
     scale = lax.rsqrt(jnp.mean(middle * middle, axis=-1, keepdims=True) + NORM_EPS)
     weighted = gains_ref[1:2, :] * gradient
     inner = jnp.mean(middle * weighted, axis=-1, keepdims=True)
-    part = scale * weighted - middle * (scale * scale * scale) * inner
     gain_ref[...] = fold_sum(gradient * middle * scale)
-    total = out_grad_ref[...].astype(F32) + part
+    total = out_grad_ref[...].astype(F32) + (
+        scale * weighted - middle * (scale * scale * scale) * inner
+    )
     grad_ref[...] = total
-    low = total.astype(BF16)
-    low_ref[...] = low
-    attended_ref[...] = mm(low, own_ref[...]).astype(BF16)
-
-
-def middle_back(places, halves, middle, out_grad, gains, own):
-    shares, tokens = len(halves), middle.shape[0]
+    low_ref[...] = total.astype(BF16)
+    attended_grad_ref[...] = mm(low_ref[...], out_all[:, own_lanes]).astype(BF16)
+    for copy in keeps:
+        copy.wait()
+    for copy in near:
+        copy.wait()
+    wire.finish()
+
+
+def expert_step(
+    attended, hidden, out_grad, gains, lanes, picker_flip, outs, grads, ins, downs, experts
+):
+    dp_count, ctx_count, tp_count = (lax.axis_size(a) for a in ("dp", "ctx", "tp"))
+    tokens, width = attended.shape
+    slots = grads[0].shape[0]
+    share = D // tp_count
+    depth, ff = ins[0].shape[1], ins[0].shape[2]
+    all_slots = dp_count * slots
+    half = ctx_count // 2
+    others = tp_count - 1
+    copies = others * (2 + 3 * dp_count) + 3 * dp_count + 2 * half
+    vmem = pl.BlockSpec(memory_space=pltpu.VMEM)
+    hbm = pl.BlockSpec(memory_space=pl.ANY)
+    shape = jax.ShapeDtypeStruct
+    return pl.pallas_call(
+        functools.partial(expert_kernel, experts, dp_count, ctx_count, tp_count),
+        in_specs=[vmem] * 6 + [hbm] * (tp_count + dp_count + 2 * ctx_count),
+        out_specs=[vmem] * 8 + [hbm] * 4,
+        out_shape=[
+            shape((tokens, D), F32),
+            shape((tokens, D), BF16),
+            shape((tokens, LANES), F32),
+            shape((tokens, D), F32),
+            shape((tokens, D), BF16),
+            shape((tokens, width), BF16),
+            shape((8, D), F32),
+            shape((tp_count, dp_count, slots, share), BF16),
+            shape((half, 2, depth, ff), BF16),
+            shape((half, ff, depth), BF16),
+            shape((half, 2, depth, ff), BF16),
+            shape((half, ff, depth), BF16),
+        ],
+        scratch_shapes=[
+            pltpu.VMEM((tokens, tp_count * width), BF16),
+            pltpu.VMEM((D, tp_count * width), BF16),
+            pltpu.VMEM((2, D, ff), BF16),
+            pltpu.VMEM((ff, D), BF16),
+            pltpu.VMEM((all_slots, D), BF16),
+            pltpu.VMEM((all_slots, D), BF16),
+            pltpu.VMEM((all_slots, ff), BF16),
+            pltpu.VMEM((all_slots, ff), BF16),
+            pltpu.VMEM((all_slots, ff), BF16),
+            pltpu.VMEM((dp_count - 1, slots, D), BF16),
+            pltpu.VMEM((tp_count, dp_count, slots, share), BF16),
+            pltpu.VMEM((others, dp_count, slots, share), BF16),
+            pltpu.VMEM((all_slots, share), BF16),
+            pltpu.VMEM((dp_count, 8, slots), F32),
+            pltpu.VMEM((others, dp_count, 8, slots), F32),
+            pltpu.VMEM((dp_count, 8, slots), F32),
+            pltpu.VMEM((dp_count, 8, slots), F32),
+            pltpu.VMEM((tokens, LANES), F32),
+            pltpu.VMEM((tokens, D), BF16),
+            pltpu.SemaphoreType.DMA((copies,)),
+            pltpu.SemaphoreType.DMA((copies,)),
+            pltpu.SemaphoreType.DMA((tp_count + 2 * ctx_count + dp_count,)),
+            pltpu.SemaphoreType.DMA((ctx_count,)),
+        ],
+        compiler_params=pltpu.CompilerParams(
+            vmem_limit_bytes=VMEM_CAP, collective_id=3, has_side_effects=True
+        ),
+        cost_estimate=cost(120),
+        name="expert_step",
+    )(attended, hidden, out_grad, gains, lanes, picker_flip, *outs, *grads, *ins, *downs)
+
+
+def final_kernel(
+    experts, dp_count, ctx_count, tp_count,
+    query_grad_ref, key_ref, value_ref, normed_ref, weight_ref, low_ref, attended_ref,
+    normed_two_ref, logit_ref, hidden_ref, gains_ref, gain_two_ref, middle_grad_ref,
+    input_grad_ref, first_ref, second_ref,
+    key_in, send_far, far_in, first_all, second_all, first_core, second_core, first_sum,
+    second_sum, first_dp, second_dp, first_x, second_x, rows_all, token_grad, token_in,
+    gain_send, gain_in, sends, receives,
+):
+    d, c, t = lax.axis_index("dp"), lax.axis_index("ctx"), lax.axis_index("tp")
+    tokens, width = query_grad_ref.shape
+    dp_bits = bits_down(dp_count)[::-1]
+    far_bits = bits_down(ctx_count)[:-1][::-1]
+    far = list(range(0, ctx_count, 2))
+    greet(
+        [{"ctx": c ^ bit} for bit in bits_down(ctx_count)]
+        + [{"dp": d ^ bit} for bit in dp_bits]
+        + [{"tp": t ^ bit} for bit in bits_down(tp_count)]
+    )
+    wire = Wire(sends, receives)
+
+    near = []
+    for k in far[::-1]:
+        rows = slice((k + 1) * tokens, (k + 2) * tokens)
+        for side, ref in enumerate((key_ref, value_ref)):
+            near.append(wire.send(ref.at[rows], key_in.at[side, k // 2], ctx=c ^ 1))
+
+    def split(values):
+        return values.astype(BF16).reshape(dp_count, ctx_count, -1, values.shape[1])
+
+    first_all[:, :, :, :width] = split(mm(normed_ref[...], query_grad_ref[...], TN))
+    first_all[:, :, :, width:] = split(mm(low_ref[...], attended_ref[...], TN))
+
+    def cross(whole, landed):
+        return [wire.send(whole.at[:, c ^ (k + 1)], landed.at[k // 2], ctx=c ^ 1) for k in far]
+
+    def add_core(whole, landed, total, copies):
+        for k, copy in zip(far, copies):
+            copy.wait()
+            own = whole[:, pl.ds(c ^ k, 1)][:, 0]
+            total[k // 2] = (own.astype(F32) + landed[k // 2].astype(F32)).astype(BF16)
+
+    first_crossed = cross(first_all, first_core)
+    for copy in near:
+        copy.wait()
+    for k in far:
+        rows = slice(k * tokens, (k + 1) * tokens)
+        for side, ref in enumerate((key_ref, value_ref)):
+            send_far[side, k // 2] = (
+                ref[rows, :].astype(F32) + key_in[side, k // 2].astype(F32)
+            ).astype(BF16)
+    assert len(far_bits) == 1
+    far_copies = [
+        wire.send(send_far.at[side, 1], far_in.at[side], ctx=c ^ 2) for side in range(2)
+    ]
+
+    def dp_send(total, landed, level, bit, sides):
+        copies = []
+        for m in range(bit, dp_count, 2 * bit):
+            for k in sides:
+                spot = landed.at[level, k, d ^ m]
+                copies.append((m ^ bit, k, wire.send(total.at[k, d ^ m], spot, dp=d ^ bit)))
+        return copies
+
+    def dp_add(total, landed, level, copies):
+        for m, k, copy in copies:
+            copy.wait()
+            own = total[k, pl.ds(d ^ m, 1)][0]
+            other = landed[level, k, pl.ds(d ^ m, 1)][0]
+            total[k, pl.ds(d ^ m, 1)] = (own.astype(F32) + other.astype(F32)).astype(BF16)[None]
+
+    add_core(first_all, first_core, first_sum, first_crossed)
+    moving = dp_send(first_sum, first_dp, 0, dp_bits[0], range(len(far)))
+    token_grad[...] = mm(query_grad_ref[...], weight_ref[:, :width], NT)
+    logit = logit_ref[...]
+    logit_high = logit.astype(BF16)
+    logit_rest = logit - logit_high.astype(F32)
+    logit_low = logit_rest.astype(BF16)
+    logit_tiny = (logit_rest - logit_low.astype(F32)).astype(BF16)
+    router_grad = mm(normed_two_ref[...], logit_high, TN)
+    router_grad += mm(normed_two_ref[...], logit_low, TN)
+    router_grad += mm(normed_two_ref[...], logit_tiny, TN)
+    rows_all[:, :width] = query_grad_ref[...]
+    for level, bit in enumerate(dp_bits):
+        dp_add(first_sum, first_dp, level, moving)
+        if level + 1 < len(dp_bits):
+            moving = dp_send(
+                first_sum, first_dp, level + 1, dp_bits[level + 1], range(len(far))
+            )
+    first_far = wire.send(first_sum.at[1, d], first_x, ctx=c ^ 2)
+
+    for side in range(2):
+        far_copies[side].wait()
+        rows_all[:, (side + 1) * width : (side + 2) * width] = (
+            send_far[side, 0].astype(F32) + far_in[side].astype(F32)
+        ).astype(BF16)
+    part = token_grad[...] + mm(rows_all[:, width:], weight_ref[:, width:], NT)
+    part_low = part.astype(BF16)
+    inputs = hidden_ref[...].astype(F32)
+    scale = lax.rsqrt(jnp.mean(inputs * inputs, axis=-1, keepdims=True) + NORM_EPS)
+    gain_send[0] = fold_sum(part_low.astype(F32) * inputs * scale)
+    token_in[0] = part_low
+    gain_total = gain_send[0]
+    gain_copies, token_copies = [], []
+    tp_bits = bits_down(tp_count)[::-1]
+    gain_copies.append(wire.send(gain_send.at[0], gain_in.at[0], tp=t ^ tp_bits[0]))
+    token_copies.append(wire.send(token_in.at[0], token_in.at[1], tp=t ^ tp_bits[0]))
+    second_all[:, :, :, : 2 * width] = split(mm(normed_ref[...], rows_all[:, width:], TN))
+    for level, bit in enumerate(tp_bits):
+        if level:
+            gain_send[level] = gain_total
+            gain_copies.append(wire.send(gain_send.at[level], gain_in.at[level], tp=t ^ bit))
+        gain_copies[level].wait()
+        gain_total = gain_total + gain_in[level]
+    gain_one = jnp.sum(gain_total, axis=0, keepdims=True)
+    gain_two = jnp.sum(gain_two_ref[...], axis=0, keepdims=True)
+    row = lax.broadcasted_iota(jnp.int32, (LANES, D), 0)
+    gain_rows = jnp.where(row == experts, gain_one, jnp.where(row == experts + 1, gain_two, 0.0))
+    second_all[:, :, :, 2 * width :] = split(router_grad + gain_rows.T)
+    second_crossed = cross(second_all, second_core)
+
+    add_core(second_all, second_core, second_sum, second_crossed)
+    second_far = wire.send(second_sum.at[1], second_x, ctx=c ^ 2)
+    total = part_low.astype(F32)
+    for level, bit in enumerate(tp_bits):
+        if level:
+            token_in[2 * level] = total.astype(BF16)
+            total = token_in[2 * level].astype(F32)
+            token_copies.append(
+                wire.send(token_in.at[2 * level], token_in.at[2 * level + 1], tp=t ^ bit)
+            )
+        token_copies[level].wait()
+        total = total + token_in[2 * level + 1].astype(F32)
+    weighted = gains_ref[0:1, :] * total
+    inner = jnp.mean(inputs * weighted, axis=-1, keepdims=True)
+    input_grad_ref[...] = (
+        middle_grad_ref[...] + scale * weighted - inputs * (scale * scale * scale) * inner
+    )
+    first_far.wait()
+    first_ref[...] = first_sum[0, pl.ds(d, 1)][0].astype(F32) + first_x[...].astype(F32)
+    second_far.wait()
+    second_sum[0] = (second_sum[0].astype(F32) + second_x[...].astype(F32)).astype(BF16)
+    for level, bit in enumerate(dp_bits):
+        moving = dp_send(second_sum, second_dp, level, bit, [0])
+        dp_add(second_sum, second_dp, level, moving)
+    second_ref[...] = second_sum[0, pl.ds(d, 1)][0].astype(F32)
+    wire.finish()
+
+
+def final_step(
+    query_grad, key_part, value_part, normed, weight, low, attended, normed_two, logit, hidden,
+    gains, gain_two, middle_grad, experts,
+):
+    tokens, width = query_grad.shape
+    dp_count, ctx_count, tp_count = (lax.axis_size(a) for a in ("dp", "ctx", "tp"))
+    rows = D // (dp_count * ctx_count)
+    half = ctx_count // 2
+    levels = len(bits_down(dp_count))
+    tp_levels = len(bits_down(tp_count))
+    one, two = 2 * width, 2 * width + LANES
+    copies = 4 * half + 2 * half + 4 + 2 * tp_levels + (half + 1) * dp_count + 2
     vmem = pl.BlockSpec(memory_space=pltpu.VMEM)
     return pl.pallas_call(
-        functools.partial(middle_back_kernel, shares),
-        in_specs=[pl.BlockSpec(memory_space=pltpu.SMEM)] + [vmem] * (shares + 4),
-        out_specs=[vmem] * 4,
+        functools.partial(final_kernel, experts, dp_count, ctx_count, tp_count),
+        in_specs=[vmem] * 13,
+        out_specs=[vmem] * 3,
         out_shape=[
             jax.ShapeDtypeStruct((tokens, D), F32),
-            jax.ShapeDtypeStruct((tokens, D), BF16),
-            jax.ShapeDtypeStruct((tokens, own.shape[1]), BF16),
-            jax.ShapeDtypeStruct((8, D), F32),
+            jax.ShapeDtypeStruct((rows, one), F32),
+            jax.ShapeDtypeStruct((rows, two), F32),
         ],
-        scratch_shapes=[pltpu.VMEM((tokens, D), BF16)],
-        compiler_params=pltpu.CompilerParams(vmem_limit_bytes=VMEM_CAP),
-        name="middle_back",
-    )(places, *halves, middle, out_grad, gains, own)
-
-
-def expert_kernel(experts, count, shares, place_ref, rows_ref, grads_ref, router_ref, *refs):
-    ins, downs = refs[:count], refs[count : 2 * count]
-    in_all, down_all, sems = refs[-3:]
-    results = refs[-3 - 5 - 2 * shares : -3]
-    rows_all, scaled_all, act_ref, gate_low_ref, up_low_ref = results[:5]
-    row_parts, out_parts = results[5 : 5 + shares], results[5 + shares :]
-    expert, ctx, share = place_ref[0], place_ref[1], place_ref[2]
-    depth = ins[0].shape[1]
-    ff = ins[0].shape[2]
-
-    @pl.when(pl.program_id(0) == 0)
-    def _():
-        copies = []
-        for j in range(count):
-            part = pl.ds(j * depth, depth)
-            copies.append(pltpu.make_async_copy(ins[j], in_all.at[:, part, :], sems.at[0, j]))
-            copies.append(pltpu.make_async_copy(downs[j], down_all.at[:, part], sems.at[1, j]))
-        for copy in copies:
-            copy.start()
-        for copy in copies:
-            copy.wait()
-
-    slots = rows_ref.shape[0]
-    lane = lax.broadcasted_iota(jnp.int32, (slots, LANES), 1)
-    logits = jnp.where(lane < experts, mm(rows_ref[...], router_ref[...]), NEG_FILL)
-    powers = jnp.exp(logits - jnp.max(logits, axis=1, keepdims=True))
-    probs = powers / jnp.sum(powers, axis=1, keepdims=True)
-    gate = jnp.sum(jnp.where(lane == expert, probs, 0.0), axis=1, keepdims=True)
-    rows_all[...] = rows_ref[...]
-    scaled_all[...] = (gate * grads_ref[...].astype(F32)).astype(BF16)
-    order = [pl.ds(pl.multiple_of((ctx ^ j) * depth, depth), depth) for j in range(count)]
-    rows = jnp.concatenate([rows_ref[:, part] for part in order], axis=1)
-    grads = jnp.concatenate([grads_ref[:, part] for part in order], axis=1)
-    dots = jnp.zeros((slots, 1), F32)
-    for start in range(0, ff, BLOCK):
-        part = slice(start, min(ff, start + BLOCK))
-        value = mm(rows, in_all[0, :, part])
-        up = mm(rows, in_all[1, :, part])
-        back = mm(grads, down_all[part, :], NT)
-        square = value * value
-        wave = jnp.tanh(GELU_K * value * (1.0 + GELU_C * square))
-        half = 0.5 * (1.0 + wave)
-        bent = value * half
-        slope = half + 0.5 * value * (1.0 - wave * wave) * (
-            GELU_K * (1.0 + 3.0 * GELU_C * square)
-        )
-        act = (bent * up).astype(BF16)
-        act_ref[:, part] = act
-        dots += jnp.sum(act.astype(F32) * back, axis=1, keepdims=True)
-        scaled = gate * back
-        gate_low_ref[:, part] = (scaled * up * slope).astype(BF16)
-        up_low_ref[:, part] = (scaled * bent).astype(BF16)
-    share_width = D // shares
-    high = dots.astype(BF16).astype(F32)
-    stride = LANES // shares
-    tail = jnp.where(lane == share * stride + expert, high, 0.0)
-    tail = jnp.where(lane == share * stride + stride // 2 + expert, dots - high, tail)
-    for m in range(shares):
-        for i in range(share_width // depth):
-            piece = ((share ^ m) * (share_width // depth) + i) ^ ctx
-            part = pl.ds(pl.multiple_of(piece * depth, depth), depth)
-            spot = slice(i * depth, (i + 1) * depth)
-            row = mm(gate_low_ref[...], in_all[0, part, :], NT)
-            row += mm(up_low_ref[...], in_all[1, part, :], NT)
-            row_parts[m][:, spot] = row.astype(BF16)
-            out_parts[m][:, spot] = (gate * mm(act_ref[...], down_all[:, part])).astype(BF16)
-        row_parts[m][:, share_width:] = tail.astype(BF16)
-
-
-def expert_block(block, blocks, places, rows, grads, router, ins, downs, held, experts, shares):
-    slots, width = rows.shape
-    ff = ins[0].shape[2]
-    count = len(ins)
-    share_width = width // shares
-    vmem = pl.BlockSpec(memory_space=pltpu.VMEM)
-    hbm = pl.BlockSpec(memory_space=pl.ANY)
-    at_block = lambda i: (block, 0)
-    sizes = (width, width, ff, ff, ff)
-    aliases = {4 + 2 * count + k: k for k in range(5)} if held else {}
-    return pl.pallas_call(
-        functools.partial(expert_kernel, experts, count, shares),
-        grid=(1,),
-        in_specs=[pl.BlockSpec(memory_space=pltpu.SMEM)]
-        + [vmem] * 3
-        + [hbm] * (2 * count + len(held)),
-        out_specs=[pl.BlockSpec((slots, size), at_block) for size in sizes] + [vmem] * (2 * shares),
-        out_shape=[jax.ShapeDtypeStruct((blocks * slots, size), BF16) for size in sizes]
-        + [jax.ShapeDtypeStruct((slots, share_width + LANES), BF16)] * shares
-        + [jax.ShapeDtypeStruct((slots, share_width), BF16)] * shares,
         scratch_shapes=[
-            pltpu.VMEM((2, width, ff), BF16),
-            pltpu.VMEM((ff, width), BF16),
-            pltpu.SemaphoreType.DMA((2, count)),
+            pltpu.VMEM((2, half, tokens, width), BF16),
+            pltpu.VMEM((2, half, tokens, width), BF16),
+            pltpu.VMEM((2, tokens, width), BF16),
+            pltpu.VMEM((dp_count, ctx_count, rows, one), BF16),
+            pltpu.VMEM((dp_count, ctx_count, rows, two), BF16),
+            pltpu.VMEM((half, dp_count, rows, one), BF16),
+            pltpu.VMEM((half, dp_count, rows, two), BF16),
+            pltpu.VMEM((half, dp_count, rows, one), BF16),
+            pltpu.VMEM((half, dp_count, rows, two), BF16),
+            pltpu.VMEM((levels, half, dp_count, rows, one), BF16),
+            pltpu.VMEM((levels, 1, dp_count, rows, two), BF16),
+            pltpu.VMEM((rows, one), BF16),
+            pltpu.VMEM((dp_count, rows, two), BF16),
+            pltpu.VMEM((tokens, 3 * width), BF16),
+            pltpu.VMEM((tokens, D), F32),
+            pltpu.VMEM((2 * tp_levels, tokens, D), BF16),
+            pltpu.VMEM((tp_levels, 8, D), F32),
+            pltpu.VMEM((tp_levels, 8, D), F32),
+            pltpu.SemaphoreType.DMA((copies,)),
+            pltpu.SemaphoreType.DMA((copies,)),
         ],
-        input_output_aliases=aliases,
-        compiler_params=pltpu.CompilerParams(vmem_limit_bytes=VMEM_CAP),
-        name="expert_block",
-    )(places, rows, grads, router, *ins, *downs, *held)
+        compiler_params=pltpu.CompilerParams(
+            vmem_limit_bytes=VMEM_CAP, collective_id=2, has_side_effects=True
+        ),
+        cost_estimate=cost(87),
+        name="final_step",
+    )(
+        query_grad, key_part, value_part, normed, weight, low, attended, normed_two, logit,
+        hidden, gains, gain_two, middle_grad,
+    )
 
 
 def shards(
@@ -884,106 +1192,46 @@
     base = (length - LANES - block_rows).astype(jnp.int32)
 
     attended, totals = attention(active, base, queries, key_values, window, doc_row, doc_col)
-    middle, normed_two, probs, send_rows = middle_step(
-        places, gather_xor(attended, "tp"), out_sides, hidden_in, gains, lanes, picker, dp_count
-    )
-    arrived_rows = [send_rows[0]] + [swap(send_rows[m], "dp", m) for m in range(1, dp_count)]
-
-    held = ()
-    row_sums, out_parts = [], []
-    for m in range(dp_count):
-        results = expert_block(
-            m, dp_count, places, arrived_rows[m], arrived_grads[m], lanes,
-            in_pieces, down_pieces, held, expert_count, tp_count,
-        )
-        held = results[:5]
-        row_sums.append(scatter_sum(results[5 : 5 + tp_count], "tp").astype(BF16))
-        out_parts.append(results[5 + tp_count :])
-    back_rows = row_sums[:1] + [swap(row_sums[m], "dp", m) for m in range(1, dp_count)]
-    held, _ = lax.optimization_barrier((held, row_sums))
-    rows_all, scaled_all, act_all, gate_low_all, up_low_all = held
-
-    def rows_by_ctx(values):
-        depth = values.shape[0] // ctx_count
-        return [
-            lax.dynamic_slice_in_dim(values, (ctx_place ^ j) * depth, depth, 0)
-            for j in range(ctx_count)
-        ]
-
-    def columns_by_ctx(values):
-        depth = values.shape[1] // ctx_count
-        return [
-            lax.dynamic_slice_in_dim(values, (ctx_place ^ j) * depth, depth, 1)
-            for j in range(ctx_count)
-        ]
-
-    def weight_grad(left, right):
-        return lax.dot_general(
-            left, right, (((0,), (0,)), ((), ())), preferred_element_type=F32
-        ).astype(BF16)
-
-    gate_total = scatter_sum(rows_by_ctx(weight_grad(rows_all, gate_low_all)), "ctx")
-    up_total = scatter_sum(rows_by_ctx(weight_grad(rows_all, up_low_all)), "ctx")
-    down_total = scatter_sum(columns_by_ctx(weight_grad(act_all, scaled_all)), "ctx")[None]
-    in_total = jnp.stack([gate_total, up_total], axis=0)[None]
-
-    grad_half, logit_grad = return_step(places, back_rows, picker_flip, probs, lanes, tp_count)
-    middle_grad, middle_low, attended_grad, gain_two_grad = middle_back(
-        places, gather_xor(grad_half, "tp"), middle, out_grad, gains, out_own
-    )
-    out_parts, _ = lax.optimization_barrier((out_parts, middle_grad))
-    out_sums = [scatter_sum(parts, "tp").astype(BF16) for parts in out_parts]
-    back_outs = out_sums[:1] + [swap(out_sums[m], "dp", m) for m in range(1, dp_count)]
+    (middle, normed_two, logit_grad, middle_grad, middle_low, attended_grad, gain_two_grad,
+     out_parts, in_keep, down_keep, in_core, down_core) = expert_step(
+        attended, hidden_in, out_grad, gains, lanes, picker_flip, out_sides, arrived_grads,
+        in_pieces, down_pieces, expert_count,
+    )
+
+    def add_cores(kept, arrived, k):
+        return kept[k].astype(F32) + arrived[k].astype(F32)
+
+    in_far = [swap(add_cores(in_keep, in_core, 1).astype(BF16), "ctx", 2)]
+    down_far = [swap(add_cores(down_keep, down_core, 1).astype(BF16), "ctx", 2)]
+    out_far = [swap(out_parts[k], "tp", k) for k in range(1, tp_count)]
+    query_grad, key_part, value_part, offset_grad = attention_back(
+        active, base, queries, key_values, attended_grad, totals, window, doc_row, doc_col
+    )
+    bias_part = lax.dot_general(
+        offset_grad[:, :2, :].reshape(heads_here, window_width), table_onehot, NT,
+        precision=lax.Precision.HIGHEST, preferred_element_type=F32,
+    )
+    bias_total = all_sum(all_sum(bias_part, "ctx"), "dp")
+
+    query_grad, in_far, down_far, out_far = lax.optimization_barrier(
+        (query_grad, in_far, down_far, out_far)
+    )
+    in_total = (add_cores(in_keep, in_core, 0) + in_far[0].astype(F32))[None]
+    down_total = (add_cores(down_keep, down_core, 0) + down_far[0].astype(F32))[None]
+    out_sum = tree_sum([part.astype(F32) for part in [out_parts[0]] + out_far]).astype(BF16)
+    back_outs = [out_sum[0]] + [swap(out_sum[m], "dp", m) for m in range(1, dp_count)]
     mixed_half = mm(picker_flip, jnp.concatenate(back_outs, axis=0)).astype(BF16)
     mixed = in_order(gather_xor(mixed_half, "tp"), tp_place, 1)
     output = middle + mixed.astype(F32)
-    out_flip_grad = weight_grad(middle_low, attended)
-    router_grad = lax.dot_general(
-        normed_two.astype(F32), logit_grad, (((0,), (0,)), ((), ())),
-        precision=lax.Precision.HIGHEST, preferred_element_type=F32,
-    )[:, :expert_count]
-    inputs = hidden_in.astype(F32)
-    scale_one = rms_scale(inputs)
-
-    query_grad, key_part, value_part, offset_grad = attention_back(
-        active, base, queries, key_values, attended_grad, totals, window, doc_row, doc_col
-    )
-    bias_part = lax.dot_general(
-        offset_grad[:, :2, :].reshape(heads_here, window_width), table_onehot, NT,
-        precision=lax.Precision.HIGHEST, preferred_element_type=F32,
-    )
-    bias_total = all_sum(all_sum(bias_part, "ctx"), "dp")
-
-    def row_blocks(values):
-        return [values[j * tokens : (j + 1) * tokens] for j in range(ctx_count)]
-
-    key_total = scatter_sum(row_blocks(key_part), "ctx").astype(BF16)
-    value_total = scatter_sum(row_blocks(value_part), "ctx").astype(BF16)
-    qkv_rows_grad = jnp.concatenate([query_grad, key_total, value_total], axis=1)
-    normed_one_grad = all_sum(mm(qkv_rows_grad, qkv_flat, NT).astype(BF16), "tp").astype(F32)
-    input_part, gain_one_grad = norm_back(inputs, scale_one, gains[0], normed_one_grad)
-    input_grad = middle_grad + input_part
-    qkv_weight_grad = weight_grad(normed_one, qkv_rows_grad)
-
-    tail_grad = jnp.pad(
-        jnp.concatenate(
-            [router_grad, jnp.stack([gain_one_grad, jnp.sum(gain_two_grad, axis=0)], axis=1)], axis=1
-        ),
-        ((0, 0), (0, LANES - expert_count - 2)),
-    ).astype(BF16)
-    grad_pack = jnp.concatenate([qkv_weight_grad, out_flip_grad, tail_grad], axis=1)
-    grad_pack = grad_pack.reshape(dp_count, ctx_count, own_rows, grad_pack.shape[1])
-    ctx_parts = [
-        lax.dynamic_slice_in_dim(grad_pack, ctx_place ^ j, 1, 1)[:, 0] for j in range(ctx_count)
-    ]
-    ctx_total = scatter_sum(ctx_parts, "ctx").astype(BF16)
-    dp_parts = [
-        lax.dynamic_slice_in_dim(ctx_total, dp_place ^ j, 1, 0)[0] for j in range(dp_count)
-    ]
-    pack_total = scatter_sum(dp_parts, "dp")
-    qkv_total = pack_total[:, : 3 * width_here].reshape(own_rows, 3, width_here)
-    out_total = pack_total[:, 3 * width_here : 4 * width_here].T
-    tail_total = pack_total[:, 4 * width_here :]
+    input_grad, first_total, second_total = final_step(
+        query_grad, key_part, value_part, normed_one, qkv_flat, middle_low, attended, normed_two,
+        logit_grad, hidden_in, gains, gain_two_grad, middle_grad, expert_count,
+    )
+    qkv_total = jnp.concatenate(
+        [first_total[:, :width_here], second_total[:, : 2 * width_here]], axis=1
+    ).reshape(own_rows, 3, width_here)
+    out_total = first_total[:, width_here:].T
+    tail_total = second_total[:, 2 * width_here :]
     router_total = tail_total[:, :expert_count]
     gains_total = tail_total[:, expert_count : expert_count + 2].T
 

time: 647 us -> 525 us (0.81)
  Pallas kernels: 189 us -> 338 us
  waiting for transfers between devices: 156 us -> 50.1 us
  starting transfers between devices: 113 us -> 46.4 us
  local copies, waits for them, and re-layouts: 75.6 us -> 33.9 us
  other arithmetic: 73.1 us -> 40.9 us
  matrix products: 30.7 us -> 4.86 us
    pallas_call x7 -> x2, Pallas kernels: 71.2 us -> 220 us  [the longest x1 137 us: expert_step(): pl.pallas_call(functools.partial(expert_kernel, experts, dp_count, ctx_co...]
    ppermute x56 -> x21, waiting for transfers between devices: 156 us -> 50.1 us  [swap(): return lax.ppermute(values, axis, [(i, i ^ bits) for i in range(count)])]
    ppermute x56 -> x21, starting transfers between devices: 113 us -> 46.4 us  [swap(): return lax.ppermute(values, axis, [(i, i ^ bits) for i in range(count)])]
    dot_general x6 -> x0, matrix products: 22 us -> none  [the longest x5 20.4 us: weight_grad(): lax.dot_general(left, right, (((0,), (0,)), ((), ())), preferred_element_...]
    convert_element_type x19 -> x3, other arithmetic: 23 us -> 7.65 us  [the longest x1 3.38 us: shards(): in_far = [swap(add_cores(in_keep, in_core, 1).astype(BF16), 'ctx', 2)]]
    ppermute x5 -> x0, local copies, waits for them, and re-layouts: 12.5 us -> none  [swap(): return lax.ppermute(values, axis, [(i, i ^ bits) for i in range(count)])]
    dynamic_slice x7 -> x0, local copies, waits for them, and re-layouts: 9.99 us -> none  [the longest x3 4.34 us: shards(): lax.dynamic_slice_in_dim(ctx_total, dp_place ^ j, 1, 0)[0]]
    unnamed x191 -> x153, local copies, waits for them, and re-layouts: 23.6 us -> 14 us
  transfers between devices with their start and end apart: 56 -> 21, of which waited for: 22 -> 6; matrix products, arithmetic and copies ran while one was open for 23% -> 11% of each run, Pallas kernels for 18% -> 11%
where the time goes in v2:
time: 525 us; the launch traced here: 516 us
  Pallas kernels  338 us (64%)
  waiting for transfers between devices  50.1 us (10%)
  starting transfers between devices  46.4 us (9%)
  other arithmetic  40.9 us (8%)
  local copies, waits for them, and re-layouts  33.9 us (6%)
    pallas_call x1, Pallas kernels, expert_step(): pl.pallas_call(functools.partial(expert_kernel, experts, dp_count, ctx_co...  137 us
    pallas_call x1, Pallas kernels, final_step(): pl.pallas_call(functools.partial(final_kernel, experts, dp_count, ctx_cou...  83 us
    pallas_call x1, Pallas kernels, start(): pl.pallas_call(functools.partial(start_kernel, experts, dp_count, ctx_cou...  62 us
    ppermute x21, waiting for transfers between devices, swap(): return lax.ppermute(values, axis, [(i, i ^ bits) for i in range(count)])  50.1 us
    ppermute x21, starting transfers between devices, swap(): return lax.ppermute(values, axis, [(i, i ^ bits) for i in range(count)])  46.4 us
    pallas_call x1, Pallas kernels, attention_back(): pl.pallas_call(attention_back_kernel, grid=(pairs,), in_specs=[specs['sme...  34.3 us
    pallas_call x1, Pallas kernels, attention(): pl.pallas_call(attention_kernel, grid=(pairs,), in_specs=[specs['smem'],...  21.5 us
    unnamed x153, local copies, waits for them, and re-layouts  14 us
  transfers between devices with their start and end apart: 21, of which 6 were waited for; matrix products, arithmetic and copies ran while one was open for 11% of the time, Pallas kernels for 11%

profile of v2, /device:TPU:0, one launch (start us, length us, event | category | flops | bytes accessed | tf_op | source)
XLA Modules:
  0.0 516.2 jit_solution(4297458273290604605)
XLA Ops:
  2.4 1.6 fusion.23.pack_ref
  4.0 1.3 broadcast_in_dim.13.docs_ref.doc_row_ref
  5.3 62.0 %start.1 = (bf16[512,512]{1,0:T(8,128)(2,1)}, bf16[2048,1024]{1,0:T(8,128)(2,1)}, bf16[512,1024]{1,0:T(8,128)(2,1)}, bf16[1024,1536]{1,0:T(8,128)(2,1)}, bf16[10...) custom-call(bf16[64,2176]{1,0:T(8,128)(2,1)} %fusion.23.pack_ref, ...), custom_call_target="tpu_custom_call" | custom-call | flops 69000003584 | bytes 1048576 | tf_op jit(solution)/shard_map/start/pallas_call | solution.py:529
  67.3 1.6 collective-permute-start
  69.4 1.1 reduce-window.6
  72.7 1.5 convolution_convert_fusion
  74.8 1.7 collective-permute-start.5
  76.4 1.3 slice_bitcast_fusion.1
  77.7 1.8 collective-permute-start.1
  80.3 1.4 fusion.44
  88.6 1.6 pad.14.window_ref
  90.2 1.3 and_convert_fusion.active_ref
  91.6 17.1 %collective-permute-done.1.refs_3_ = bf16[320,1024]{1,0:T(8,128)(2,1)} collective-permute-done((bf16[320,1024]{1,0:T(8,128)(2,1)}, bf16[320,1024]{1,0:T(8,128)(2,1)}, u32[]{:S(2)}, u32[]{:S(2)}) %collective-permute-start.1) | collective-permute-done | bytes 655392 | tf_op jit(solution)/shard_map/ppermute | solution.py:66
  108.7 1.3 collective-permute-start.3
  110.8 2.0 broadcast_in_dim.15.doc_col_ref
  112.8 21.5 %attention_forward.1 = (bf16[512,512]{1,0:T(8,128)(2,1)}, f32[4,8,512]{2,1,0:T(8,128)}) custom-call(s32[2,8]{1,0:T(2,128)} %and_convert_fusion.active_ref, s32[8]{0:T(128)} %sub.9.base_ref, bf16[512,512]{1,0:T(8,128)(2,1)} %get-tuple-element.67.query_ref, bf16[2048,1024]{1,0:T(8,128)(2,1)} %get-tuple-element.68.key_ref.value_ref, ...), custom_call_target="tpu_custom_call" | custom-call | flops 28750000128 | bytes 1048576 | tf_op jit(solution)/shard_map/attention_forward/pallas_call | solution.py:379
  134.5 11.0 %collective-permute-start.7 = (bf16[1408,256]{1,0:T(8,128)(2,1)S(1)}, bf16[1408,256]{1,0:T(8,128)(2,1)S(1)}, u32[]{:S(2)}, u32[]{:S(2)}) collective-permute-start(bf16[1408,256]{1,0:T(8,128)(2,1)S(1)} %bitcast.135), channel_id=1, source_target_pairs={{0,2},{2,0},{4,6},{6,4},{1,3},{3,1},{5,7},{7,5},{8,10},{10,8},{12,... | collective-permute-start | bytes 2162696 | tf_op jit(solution)/shard_map/ppermute | solution.py:66
  147.7 1.2 convert_element_type.112.picker_ref
  151.2 137.4 %expert_step.1 = (f32[512,1024]{1,0:T(8,128)}, bf16[512,1024]{1,0:T(8,128)(2,1)}, f32[512,128]{1,0:T(8,128)}, f32[512,1024]{1,0:T(8,128)}, bf16[512,1024]{1,0:T(...) custom-call(bf16[512,512]{1,0:T(8,128)(2,1)} %get-tuple-element.69.a, ...), custom_call_target="tpu_custom_call" | custom-call | flops 138000007168 | bytes 1048576 | tf_op jit(solution)/shard_map/expert_step/pallas_call | solution.py:827
  288.7 3.4 fusion.5
  292.1 1.1 slice_bitcast_fusion
  293.2 3.5 collective-permute-start.12
  296.7 34.3 %attention_backward.1 = (bf16[512,512]{1,0:T(8,128)(2,1)}, bf16[2048,512]{1,0:T(8,128)(2,1)}, bf16[2048,512]{1,0:T(8,128)(2,1)}, f32[4,8,2560]{2,1,0:T(8,128)}) custom-call(s32[2,8]{1,0:T(2,128)} %and_convert_fusion.active_ref, s32[8]{0:T(128)} %sub.9.base_ref, bf16[512,512]{1,0:T(8,128)(2,1)} %get-tuple-element.67.query_ref, ...), custom_call_target="tpu_custom_call" | custom-call | flops 46000001024 | bytes 1048576 | tf_op jit(solution)/shard_map/attention_backward/pallas_call | solution.py:409
  332.5 14.3 %collective-permute-start.17 = (f32[8,32]{1,0:T(8,128)S(1)}, f32[8,32]{1,0:T(8,128)S(1)}, u32[]{:S(2)}, u32[]{:S(2)}) collective-permute-start(f32[8,32]{1,0:T(8,128)S(1)} %fusion.21), channel_id=1, source_target_pairs={{0,2},{2,0},{4,6},{6,4},{1,3},{3,1},{5,7},{7,5},{8,10},{10,8},{12,... | collective-permute-start | bytes 3080 | tf_op jit(solution)/shard_map/ppermute | solution.py:66
  346.8 2.1 fusion.17
  349.0 2.0 collective-permute-start.18
  351.0 16.3 %collective-permute-done.18 = f32[8,32]{1,0:T(8,128)S(1)} collective-permute-done((f32[8,32]{1,0:T(8,128)S(1)}, f32[8,32]{1,0:T(8,128)S(1)}, u32[]{:S(2)}, u32[]{:S(2)}) %collective-permute-start.18) | collective-permute-done | bytes 1056 | tf_op jit(solution)/shard_map/ppermute | solution.py:66
  367.3 1.7 collective-permute-start.19
  369.0 1.9 collective-permute-done.19
  371.3 4.1 collective-permute-done.20
  376.1 83.0 %final_step.1 = (f32[512,1024]{1,0:T(8,128)}, f32[64,1024]{1,0:T(8,128)}, f32[64,1152]{1,0:T(8,128)}) custom-call(bf16[512,512]{1,0:T(8,128)(2,1)} %get-tuple-element.86.query_grad_ref, bf16[2048,512]{1,0:T(8,128)(2,1)} %get-tuple-element.87.key_ref, bf16[2048,512]{1,0:T(8,128)(2,1)} %get-tuple-element.88.value_ref, ...), custom_call_target="tpu_custom_call" | custom-call | flops 100050001920 | bytes 1048576 | tf_op jit(solution)/shard_map/final_step/pallas_call | solution.py:1040
  460.1 1.4 slice_bitcast_fusion.10
  461.6 2.1 fusion.2
  463.7 1.1 slice_bitcast_fusion.8
  464.8 4.4 collective-permute-start.13
  469.9 1.4 sqrt_add_fusion.1
  472.1 1.5 sqrt_add_fusion
  474.5 4.0 fusion.27
  479.6 1.8 add_multiply_fusion.3
  481.5 5.9 %add_multiply_fusion = (f32[1,2,256,1408]{3,2,1,0:T(8,128)}, f32[1,2,256,1408]{3,2,1,0:T(8,128)}, f32[1,2,256,1408]{3,2,1,0:T(8,128)}) fusion(bf16[1,2,256,1408]{3,2,1,0:T(8,128)(2,1)S(1)} %copy-done.21, bf16[2,256,1408]{2,1,0:T(8,128)(2,1)S(1)} %copy-done.3, bf16[2,2,256,1408]{3,2,1,0:T(8,128)(2,1)S(1)} %copy-done.1, ...), kind=kLoop, calls=%fused_computation.7 | loop fusion | flops 14417920 | bytes 20185088 | tf_op jit(solution)/shard_map/mul | solution.py:54
  487.6 2.9 add_multiply_fusion.1
  495.7 1.3 add_multiply_fusion.2
  497.1 2.2 fusion.14
  499.3 1.7 collective-permute-start.16
  501.0 1.3 fusion.28
  502.3 9.9 %collective-permute-done.16 = bf16[512,512]{1,0:T(8,128)(2,1)S(1)} collective-permute-done((bf16[512,512]{1,0:T(8,128)(2,1)S(1)}, bf16[512,512]{1,0:T(8,128)(2,1)S(1)}, u32[]{:S(2)}, u32[]{:S(2)}) %collective-permute-start.16) | collective-permute-done | bytes 524320 | tf_op jit(solution)/shard_map/ppermute | solution.py:66
  512.3 1.6 convert_add_fusion.1
  514.7 1.3 copy.227
  (240 shorter events, 31.0 us)
Async XLA Ops:
  5.3 63.6 %copy-start.49 = (s32[512,2]{0,1:T(2,128)S(1)}, s32[512,2]{0,1:T(2,128)}, u32[]{:S(2)}) copy-start(s32[512,2]{0,1:T(2,128)} %param.29) | copy-start | bytes 12292
  67.3 82.2 %collective-permute-start = (bf16[1024,512]{1,0:T(8,128)(2,1)}, bf16[1024,512]{1,0:T(8,128)(2,1)}, u32[]{:S(2)}, u32[]{:S(2)}) collective-permute-start(bf16[1024,512]{1,0:T(8,128)(2,1)} %get-tuple-element.72.refs_0_), channel_id=1, source_target_pairs={{0,1},{1,0},{2,3},{3,2},{4,5},{5,4},{6,7},{7,6},{8,9},{9,8},{10,11... | collective-permute-start | bytes 3145736 | tf_op jit(solution)/shard_map/ppermute | solution.py:66
  74.2 8.1 %copy-start.52 = (s32[1,512]{1,0:T(1,128)S(1)}, s32[1,512]{1,0:T(1,128)}, u32[]{:S(2)}) copy-start(s32[1,512]{1,0:T(1,128)} %param.28) | copy-start | bytes 6148
  74.2 11.9 %copy-start.51 = (s32[4095]{0:T(1024)S(1)}, s32[4095]{0:T(1024)}, u32[]{:S(2)}) copy-start(s32[4095]{0:T(1024)} %param.30) | copy-start | bytes 49144
  74.2 36.5 %copy-start.23 = (bf16[1,1408,256]{2,1,0:T(8,128)(2,1)S(1)}, bf16[1,1408,256]{2,1,0:T(8,128)(2,1)}, u32[]{:S(2)}) copy-start(bf16[1,1408,256]{2,1,0:T(8,128)(2,1)} %param.37) | copy-start | bytes 2162692
  74.3 75.3 %collective-permute-start.4 = (bf16[2,256,1408]{2,1,0:T(8,128)(2,1)S(1)}, bf16[2,256,1408]{2,1,0:T(8,128)(2,1)}, u32[]{:S(2)}, u32[]{:S(2)}) collective-permute-start(bf16[2,256,1408]{2,1,0:T(8,128)(2,1)S(1)} %bitcast.129), channel_id=1, source_target_pairs={{0,2},{2,0},{4,6},{6,4},{1,3},{3,1},{5,7},{7,5},{8,10},{10,8},{12,... | collective-permute-start | bytes 4325384 | tf_op jit(solution)/shard_map/ppermute | solution.py:66
  74.8 36.0 %collective-permute-start.5 = (bf16[2,256,1408]{2,1,0:T(8,128)(2,1)S(1)}, bf16[2,256,1408]{2,1,0:T(8,128)(2,1)}, u32[]{:S(2)}, u32[]{:S(2)}) collective-permute-start(bf16[2,256,1408]{2,1,0:T(8,128)(2,1)S(1)} %bitcast.130), channel_id=1, source_target_pairs={{0,4},{2,6},{4,0},{6,2},{1,5},{3,7},{5,1},{7,3},{8,12},{10,14},{12... | collective-permute-start | bytes 4325384 | tf_op jit(solution)/shard_map/ppermute | solution.py:66
  77.7 30.9 %collective-permute-start.1 = (bf16[320,1024]{1,0:T(8,128)(2,1)}, bf16[320,1024]{1,0:T(8,128)(2,1)}, u32[]{:S(2)}, u32[]{:S(2)}) collective-permute-start(bf16[320,1024]{1,0:T(8,128)(2,1)} %get-tuple-element.252), channel_id=1, source_target_pairs={{0,8},{8,0},{16,24},{24,16},{1,9},{9,1},{17,25},{25,17},{2,10},{10... | collective-permute-start | bytes 1966088 | tf_op jit(solution)/shard_map/ppermute | solution.py:66
  79.5 31.2 %collective-permute-start.2 = (bf16[320,1024]{1,0:T(8,128)(2,1)S(1)}, bf16[320,1024]{1,0:T(8,128)(2,1)}, u32[]{:S(2)}, u32[]{:S(2)}) collective-permute-start(bf16[320,1024]{1,0:T(8,128)(2,1)S(1)} %get-tuple-element.251), channel_id=1, source_target_pairs={{0,16},{8,24},{16,0},{24,8},{1,17},{9,25},{17,1},{25,9},{2,18},{10... | collective-permute-start | bytes 1966088 | tf_op jit(solution)/shard_map/ppermute | solution.py:66
  108.7 25.8 %collective-permute-start.3 = (bf16[320,1024]{1,0:T(8,128)(2,1)S(1)}, bf16[320,1024]{1,0:T(8,128)(2,1)}, u32[]{:S(2)}, u32[]{:S(2)}) collective-permute-start(bf16[320,1024]{1,0:T(8,128)(2,1)S(1)} %get-tuple-element.250), channel_id=1, source_target_pairs={{0,24},{8,16},{16,8},{24,0},{1,25},{9,17},{17,9},{25,1},{2,26},{10... | collective-permute-start | bytes 1966088 | tf_op jit(solution)/shard_map/ppermute | solution.py:66
  110.7 34.8 %collective-permute-start.8 = (bf16[1408,256]{1,0:T(8,128)(2,1)S(1)}, bf16[1408,256]{1,0:T(8,128)(2,1)S(1)}, u32[]{:S(2)}, u32[]{:S(2)}) collective-permute-start(bf16[1408,256]{1,0:T(8,128)(2,1)S(1)} %bitcast.134), channel_id=1, source_target_pairs={{0,4},{2,6},{4,0},{6,2},{1,5},{3,7},{5,1},{7,3},{8,12},{10,14},{12... | collective-permute-start | bytes 2162696 | tf_op jit(solution)/shard_map/ppermute | solution.py:66
  110.7 39.7 %collective-permute-start.6 = (bf16[2,256,1408]{2,1,0:T(8,128)(2,1)}, bf16[2,256,1408]{2,1,0:T(8,128)(2,1)}, u32[]{:S(2)}, u32[]{:S(2)}) collective-permute-start(bf16[2,256,1408]{2,1,0:T(8,128)(2,1)} %collective-permute-done.5.refs_8_), channel_id=1, source_target_pairs={{0,2},{2,0},{4,6},{6,4},{1,3},{3,1},{5,7},{7,5},{8,10},{10,8},{12,... | collective-permute-start | bytes 4325384 | tf_op jit(solution)/shard_map/ppermute | solution.py:66
  112.8 21.5 %copy-start.46 = (s32[512]{0:T(512)S(1)}, s32[512]{0:T(512)}, u32[]{:S(2)}) copy-start(s32[512]{0:T(512)} %copy-done.45) | copy-start | bytes 6148
  112.8 21.5 %copy-start.48 = (s32[512]{0:T(512)S(1)}, s32[512]{0:T(512)}, u32[]{:S(2)}) copy-start(s32[512]{0:T(512)} %copy-done.47) | copy-start | bytes 6148
  112.8 32.8 %copy-start.42 = (s32[512,1]{0,1:T(1,128)S(1)}, s32[512,1]{0,1:T(1,128)}, u32[]{:S(2)}) copy-start(s32[512,1]{0,1:T(1,128)} %copy-done.41) | copy-start | bytes 6148
  112.8 32.8 %copy-start.44 = (s32[512,1]{0,1:T(1,128)S(1)}, s32[512,1]{0,1:T(1,128)}, u32[]{:S(2)}) copy-start(s32[512,1]{0,1:T(1,128)} %copy-done.43) | copy-start | bytes 6148
  112.8 32.8 %copy-start.59 = (s32[4]{0:T(128)S(1)}, s32[4]{0:T(128)}, u32[]{:S(2)}) copy-start(s32[4]{0:T(128)} %copy-done.58) | copy-start | bytes 52
  134.5 15.0 %collective-permute-start.7 = (bf16[1408,256]{1,0:T(8,128)(2,1)S(1)}, bf16[1408,256]{1,0:T(8,128)(2,1)S(1)}, u32[]{:S(2)}, u32[]{:S(2)}) collective-permute-start(bf16[1408,256]{1,0:T(8,128)(2,1)S(1)} %bitcast.135), channel_id=1, source_target_pairs={{0,2},{2,0},{4,6},{6,4},{1,3},{3,1},{5,7},{7,5},{8,10},{10,8},{12,... | collective-permute-start | bytes 2162696 | tf_op jit(solution)/shard_map/ppermute | solution.py:66
  145.5 4.0 collective-permute-start.9
  292.0 84.0 %collective-permute-start.10 = (bf16[2,256,1408]{2,1,0:T(8,128)(2,1)}, bf16[2,256,1408]{2,1,0:T(8,128)(2,1)S(1)}, u32[]{:S(2)}, u32[]{:S(2)}) collective-permute-start(bf16[2,256,1408]{2,1,0:T(8,128)(2,1)} %fusion.5), channel_id=1, source_target_pairs={{0,4},{2,6},{4,0},{6,2},{1,5},{3,7},{5,1},{7,3},{8,12},{10,14},{12... | collective-permute-start | bytes 4325384 | tf_op jit(solution)/shard_map/ppermute | solution.py:66
  293.2 82.9 %collective-permute-start.12 = (bf16[4,320,512]{2,1,0:T(8,128)(2,1)}, bf16[4,320,512]{2,1,0:T(8,128)(2,1)}, u32[]{:S(2)}, u32[]{:S(2)}) collective-permute-start(bf16[4,320,512]{2,1,0:T(8,128)(2,1)} %slice_bitcast_fusion), channel_id=1, source_target_pairs={{0,1},{1,0},{2,3},{3,2},{4,5},{5,4},{6,7},{7,6},{8,9},{9,8},{10,11... | collective-permute-start | bytes 3932168 | tf_op jit(solution)/shard_map/ppermute | solution.py:66
  296.7 35.5 %copy-start.40 = (s32[2560]{0:T(1024)S(1)}, s32[2560]{0:T(1024)}, u32[]{:S(2)}) copy-start(s32[2560]{0:T(1024)} %copy-done.39) | copy-start | bytes 30724
  296.7 50.1 %copy-start.4 = (bf16[2,1408,256]{2,1,0:T(8,128)(2,1)S(1)}, bf16[2,1408,256]{2,1,0:T(8,128)(2,1)}, u32[]{:S(2)}) copy-start(bf16[2,1408,256]{2,1,0:T(8,128)(2,1)} %get-tuple-element.83) | copy-start | bytes 4325380
  331.0 20.0 %copy-start.61 = (f32[64,4]{0,1:T(4,128)S(1)}, f32[64,4]{0,1:T(4,128)}, u32[]{:S(2)}) copy-start(f32[64,4]{0,1:T(4,128)} %param.42) | copy-start | bytes 3076
  331.1 37.9 %copy-start.62 = (f32[2,64]{1,0:T(2,128)S(1)}, f32[2,64]{1,0:T(2,128)}, u32[]{:S(2)}) copy-start(f32[2,64]{1,0:T(2,128)} %param.45) | copy-start | bytes 1540
  331.1 39.9 %copy-start.63 = (f32[2,64]{1,0:T(2,128)S(1)}, f32[2,64]{1,0:T(2,128)}, u32[]{:S(2)}) copy-start(f32[2,64]{1,0:T(2,128)} %param.44) | copy-start | bytes 1540
  331.1 39.9 %copy-start.53 = (f32[64,4]{0,1:T(4,128)S(1)}, f32[64,4]{0,1:T(4,128)}, u32[]{:S(2)}) copy-start(f32[64,4]{0,1:T(4,128)} %broadcast_multiply_fusion.4) | copy-start | bytes 3076
  331.1 44.3 %copy-start.50 = (f32[8,32]{1,0:T(8,128)S(1)}, f32[8,32]{1,0:T(8,128)}, u32[]{:S(2)}) copy-start(f32[8,32]{1,0:T(8,128)} %param.35) | copy-start | bytes 3076
  331.1 44.3 %copy-start.54 = (f32[8,32]{1,0:T(8,128)S(1)}, f32[8,32]{1,0:T(8,128)}, u32[]{:S(2)}) copy-start(f32[8,32]{1,0:T(8,128)} %param.47) | copy-start | bytes 3076
  331.1 44.3 %copy-start.55 = (f32[8,32]{1,0:T(8,128)S(1)}, f32[8,32]{1,0:T(8,128)}, u32[]{:S(2)}) copy-start(f32[8,32]{1,0:T(8,128)} %param.46) | copy-start | bytes 3076
  332.5 16.5 %collective-permute-start.17 = (f32[8,32]{1,0:T(8,128)S(1)}, f32[8,32]{1,0:T(8,128)S(1)}, u32[]{:S(2)}, u32[]{:S(2)}) collective-permute-start(f32[8,32]{1,0:T(8,128)S(1)} %fusion.21), channel_id=1, source_target_pairs={{0,2},{2,0},{4,6},{6,4},{1,3},{3,1},{5,7},{7,5},{8,10},{10,8},{12,... | collective-permute-start | bytes 3080 | tf_op jit(solution)/shard_map/ppermute | solution.py:66
  349.0 27.1 %collective-permute-start.11 = (bf16[1408,256]{1,0:T(8,128)(2,1)}, bf16[1408,256]{1,0:T(8,128)(2,1)S(1)}, u32[]{:S(2)}, u32[]{:S(2)}) collective-permute-start(bf16[1408,256]{1,0:T(8,128)(2,1)} %fusion.17), channel_id=1, source_target_pairs={{0,4},{2,6},{4,0},{6,2},{1,5},{3,7},{5,1},{7,3},{8,12},{10,14},{12... | collective-permute-start | bytes 2162696 | tf_op jit(solution)/shard_map/ppermute | solution.py:66
  349.0 18.3 %collective-permute-start.18 = (f32[8,32]{1,0:T(8,128)S(1)}, f32[8,32]{1,0:T(8,128)S(1)}, u32[]{:S(2)}, u32[]{:S(2)}) collective-permute-start(f32[8,32]{1,0:T(8,128)S(1)} %add.201), channel_id=1, source_target_pairs={{0,4},{2,6},{4,0},{6,2},{1,5},{3,7},{5,1},{7,3},{8,12},{10,14},{12... | collective-permute-start | bytes 3080 | tf_op jit(solution)/shard_map/ppermute | solution.py:66
  367.3 3.6 collective-permute-start.19
  370.9 4.5 collective-permute-start.20
  376.1 83.1 %copy-start.10 = (bf16[1408,256]{1,0:T(8,128)(2,1)}, bf16[1408,256]{1,0:T(8,128)(2,1)S(1)}, u32[]{:S(2)}) copy-start(bf16[1408,256]{1,0:T(8,128)(2,1)S(1)} %collective-permute-done.11) | copy-start | bytes 2162692
  376.1 83.1 %copy-start.2 = (bf16[2,256,1408]{2,1,0:T(8,128)(2,1)}, bf16[2,256,1408]{2,1,0:T(8,128)(2,1)S(1)}, u32[]{:S(2)}) copy-start(bf16[2,256,1408]{2,1,0:T(8,128)(2,1)S(1)} %collective-permute-done.10) | copy-start | bytes 4325380
  463.7 7.7 %copy-start.56 = (bf16[64,4]{0,1:T(4,128)(2,1)S(1)}, bf16[64,4]{0,1:T(4,128)(2,1)}, u32[]{:S(2)}) copy-start(bf16[64,4]{0,1:T(4,128)(2,1)} %param.33) | copy-start | bytes 1540
  463.7 10.1 %copy-start.57 = (bf16[2,64]{1,0:T(2,128)(2,1)S(1)}, bf16[2,64]{1,0:T(2,128)(2,1)}, u32[]{:S(2)}) copy-start(bf16[2,64]{1,0:T(2,128)(2,1)} %param.34) | copy-start | bytes 772
  463.7 10.8 %copy-start = (bf16[2,2,256,1408]{3,2,1,0:T(8,128)(2,1)S(1)}, bf16[2,2,256,1408]{3,2,1,0:T(8,128)(2,1)}, u32[]{:S(2)}) copy-start(bf16[2,2,256,1408]{3,2,1,0:T(8,128)(2,1)} %get-tuple-element.81) | copy-start | bytes 8650756
  464.8 32.2 %collective-permute-start.15 = (bf16[320,512]{1,0:T(8,128)(2,1)}, bf16[320,512]{1,0:T(8,128)(2,1)}, u32[]{:S(2)}, u32[]{:S(2)}) collective-permute-start(bf16[320,512]{1,0:T(8,128)(2,1)} %get-tuple-element.255), channel_id=1, source_target_pairs={{0,24},{8,16},{16,8},{24,0},{1,25},{9,17},{17,9},{25,1},{2,26},{10... | collective-permute-start | bytes 983048 | tf_op jit(solution)/shard_map/ppermute | solution.py:66
  464.8 32.2 %collective-permute-start.14 = (bf16[320,512]{1,0:T(8,128)(2,1)}, bf16[320,512]{1,0:T(8,128)(2,1)}, u32[]{:S(2)}, u32[]{:S(2)}) collective-permute-start(bf16[320,512]{1,0:T(8,128)(2,1)} %get-tuple-element.256), channel_id=1, source_target_pairs={{0,16},{8,24},{16,0},{24,8},{1,17},{9,25},{17,1},{25,9},{2,18},{10... | collective-permute-start | bytes 983048 | tf_op jit(solution)/shard_map/ppermute | solution.py:66
  464.8 32.2 %collective-permute-start.13 = (bf16[320,512]{1,0:T(8,128)(2,1)}, bf16[320,512]{1,0:T(8,128)(2,1)}, u32[]{:S(2)}, u32[]{:S(2)}) collective-permute-start(bf16[320,512]{1,0:T(8,128)(2,1)} %get-tuple-element.257), channel_id=1, source_target_pairs={{0,8},{8,0},{16,24},{24,16},{1,9},{9,1},{17,25},{25,17},{2,10},{10... | collective-permute-start | bytes 983048 | tf_op jit(solution)/shard_map/ppermute | solution.py:66
  487.6 8.2 %copy-start.22 = (bf16[64,3,512]{2,0,1:T(8,128)(2,1)S(1)}, bf16[64,3,512]{2,0,1:T(8,128)(2,1)}, u32[]{:S(2)}) copy-start(bf16[64,3,512]{2,0,1:T(8,128)(2,1)} %param.31) | copy-start | bytes 589828
  487.6 8.2 %copy-start.25 = (f32[64,3,512]{2,0,1:T(8,128)S(1)}, f32[64,3,512]{2,0,1:T(8,128)}, u32[]{:S(2)}) copy-start(f32[64,3,512]{2,0,1:T(8,128)} %param.39) | copy-start | bytes 1179652
  487.6 8.2 %copy-start.26 = (f32[64,3,512]{2,0,1:T(8,128)S(1)}, f32[64,3,512]{2,0,1:T(8,128)}, u32[]{:S(2)}) copy-start(f32[64,3,512]{2,0,1:T(8,128)} %param.38) | copy-start | bytes 1179652
  499.3 13.0 %copy-start.16 = (f32[512,1024]{1,0:T(8,128)S(1)}, f32[512,1024]{1,0:T(8,128)}, u32[]{:S(2)}) copy-start(f32[512,1024]{1,0:T(8,128)} %get-tuple-element.76) | copy-start | bytes 6291460
  499.3 12.9 %collective-permute-start.16 = (bf16[512,512]{1,0:T(8,128)(2,1)S(1)}, bf16[512,512]{1,0:T(8,128)(2,1)S(1)}, u32[]{:S(2)}, u32[]{:S(2)}) collective-permute-start(bf16[512,512]{1,0:T(8,128)(2,1)S(1)} %fusion.14), channel_id=1, source_target_pairs={{0,1},{1,0},{2,3},{3,2},{4,5},{5,4},{6,7},{7,6},{8,9},{9,8},{10,11... | collective-permute-start | bytes 1572872 | tf_op jit(solution)/shard_map/ppermute | solution.py:66
  (41 other events, 171.8 us)
